TPU v7x, 32 devices: a whole 2x2x4 slice. The times are simulated.
32 devices in a mesh: ctx: 8 (over z, core), fsdp: 4 (over y, x).
Axes of the slice: x: 2, y: 2, z: 4, core: 2. Of those that a mesh axis runs over, the one named last changes fastest.
Arguments:
- tokens: bfloat16 [4, 8, 2, 64, 2560], P('fsdp', 'ctx'), may hold values from -6 to 6
- doc_starts: int32 [4, 8, 2, 64], P('fsdp', 'ctx'), may hold values from 0 to 1023, as said below
- gain_one: bfloat16 [2560], P('fsdp'), may hold values from 0.25 to 1.75
- w_query: bfloat16 [2560, 2560], P('fsdp'), may hold values from -0.15625 to 0.15625
- key_weight_matrix: bfloat16 [2560, 640], P('fsdp'), may hold values from -0.15625 to 0.15625
- value_weight_matrix: bfloat16 [2560, 640], P('fsdp'), may hold values from -0.125 to 0.125
- w_out: bfloat16 [2560, 2560], P('fsdp'), may hold values from -0.5 to 0.5
- gain_two: bfloat16 [2560], P('fsdp'), may hold values from 0.25 to 1.75
- w_gate: bfloat16 [2560, 7168], P('fsdp'), may hold values from -0.125 to 0.125
- w_up: bfloat16 [2560, 7168], P('fsdp'), may hold values from -0.125 to 0.125
- w_down: bfloat16 [7168, 2560], P('fsdp'), may hold values from -0.09375 to 0.09375
- cotangent: bfloat16 [4, 8, 2, 64, 2560], P('fsdp', 'ctx'), may hold values from -6 to 6
Outputs:
- mixed: float32 [4, 8, 2, 64, 2560], P('fsdp', 'ctx')
- grad_tokens: float32 [4, 8, 2, 64, 2560], P('fsdp', 'ctx')
- grad_gain_one: float32 [2560], P('fsdp')
- grad_w_query: float32 [2560, 2560], P('fsdp')
- grad_w_key: float32 [2560, 640], P('fsdp')
- grad_w_value: float32 [2560, 640], P('fsdp')
- grad_w_out: float32 [2560, 2560], P('fsdp')
- grad_gain_two: float32 [2560], P('fsdp')
- grad_w_gate: float32 [2560, 7168], P('fsdp')
- grad_w_up: float32 [2560, 7168], P('fsdp')
- grad_w_down: float32 [7168, 2560], P('fsdp')
Inputs may be any that keep to these rules, and one draw needn't show every extreme that they name: `doc_starts`: documents are contiguous runs of a stream; each is at most 512 tokens and each stream has one of exactly 512 tokens.
All inputs are finite; a program needn't handle non-finite values.
Results may differ from a plain program's by a relative error of at most 0.025.
Values may be sent and summed in bfloat16 or wider, within the bound.
No kernel may reach another device: no remote copies, remote signals or barrier semaphores. Data moves between devices by JAX's collectives and lax.ppermute only.
A program may use at most 640 MiB of HBM per device.

v0:
```python
import jax
import jax.numpy as jnp
from jax import lax
from jax.sharding import PartitionSpec as P

QUERY_HEADS = 32
KEY_VALUE_HEADS = 8
HEAD_SIZE = 80


EPS = 1e-05
THETA = 1000000.0
NEGATIVE_LARGE = -1e30


def stream_pos(index_rows, block_len, ctx_count):
    device = index_rows // (2 * block_len)
    within = index_rows % (2 * block_len)
    return jnp.where(
        within < block_len,
        device * block_len + within,
        (2 * ctx_count - 1 - device) * block_len + within - block_len,
    )


def rms_forward(values, norm_gain):
    inverse = lax.rsqrt(jnp.mean(values * values, axis=-1, keepdims=True) + EPS)
    unit_rows = values * inverse
    return (unit_rows, inverse, (unit_rows * norm_gain.astype(jnp.float32)).astype(jnp.bfloat16))


def rms_backward(grad_normed, unit_rows, inverse, norm_gain):
    scaled = grad_normed * norm_gain.astype(jnp.float32)
    grad_rows = inverse * (
        scaled - unit_rows * jnp.mean(scaled * unit_rows, axis=-1, keepdims=True)
    )
    return (jnp.sum(grad_normed * unit_rows, axis=0), grad_rows)


def apply_rotation(values, cosine_table, sine_table):
    half_dim = values.shape[-1] // 2
    lead_half = values[..., :half_dim]
    tail_half = values[..., half_dim:]
    return jnp.concatenate(
        [
            lead_half * cosine_table - tail_half * sine_table,
            tail_half * cosine_table + lead_half * sine_table,
        ],
        axis=-1,
    )


def reverse_rotation(grads, cosine_table, sine_table):
    half_dim = grads.shape[-1] // 2
    lead_half = grads[..., :half_dim]
    tail_half = grads[..., half_dim:]
    return jnp.concatenate(
        [
            lead_half * cosine_table + tail_half * sine_table,
            tail_half * cosine_table - lead_half * sine_table,
        ],
        axis=-1,
    )


def per_device(
    tokens,
    doc_starts,
    gain_one,
    w_query,
    key_weight_matrix,
    value_weight_matrix,
    w_out,
    gain_two,
    w_gate,
    w_up,
    w_down,
    cotangent,
):
    single_float = jnp.float32
    bf16 = jnp.bfloat16
    ctx_count = lax.axis_size("ctx")
    ctx_index = lax.axis_index("ctx")
    block_len = tokens.shape[3]
    model_width = tokens.shape[4]
    total_row_count = 2 * block_len
    query_group_width = QUERY_HEADS // KEY_VALUE_HEADS
    residual = tokens.reshape(total_row_count, model_width).astype(single_float)
    own_starts = doc_starts.reshape(total_row_count)
    own_pos = stream_pos(
        jnp.arange(total_row_count, dtype=jnp.int32) + ctx_index * total_row_count,
        block_len,
        ctx_count,
    )
    rel_pos = (own_pos - own_starts).astype(single_float)
    inv_freq = THETA ** (-(jnp.arange(HEAD_SIZE // 2, dtype=single_float) * 2.0) / HEAD_SIZE)
    angles = rel_pos[:, None] * inv_freq[None, :]
    cosine_table = jnp.cos(angles)[:, None, :]
    sine_table = jnp.sin(angles)[:, None, :]
    attn_set = (
        lax.all_gather(gain_one, "fsdp", axis=0, tiled=True),
        lax.all_gather(w_query, "fsdp", axis=0, tiled=True),
        lax.all_gather(key_weight_matrix, "fsdp", axis=0, tiled=True),
        lax.all_gather(value_weight_matrix, "fsdp", axis=0, tiled=True),
        lax.all_gather(w_out, "fsdp", axis=0, tiled=True),
    )
    full_gain_one, full_query, full_key, full_value, full_out = attn_set
    unit_one, inv_one, first_normalized = rms_forward(residual, full_gain_one)
    query_projected = jnp.dot(first_normalized, full_query, preferred_element_type=single_float)
    key_projected = jnp.dot(first_normalized, full_key, preferred_element_type=single_float)
    value_proj = jnp.dot(first_normalized, full_value, preferred_element_type=single_float)
    query_matrix = (
        apply_rotation(
            query_projected.reshape(total_row_count, QUERY_HEADS, HEAD_SIZE),
            cosine_table,
            sine_table,
        )
        * HEAD_SIZE ** (-0.5)
    ).astype(bf16)
    query_matrix = query_matrix.reshape(
        total_row_count, KEY_VALUE_HEADS, query_group_width, HEAD_SIZE
    )
    keys_low = (
        apply_rotation(
            key_projected.reshape(total_row_count, KEY_VALUE_HEADS, HEAD_SIZE),
            cosine_table,
            sine_table,
        )
        .astype(bf16)
        .reshape(total_row_count, KEY_VALUE_HEADS * HEAD_SIZE)
    )
    values_low = value_proj.astype(bf16)

    def key_mask(key_total_count):
        key_pos = stream_pos(jnp.arange(key_total_count, dtype=jnp.int32), block_len, ctx_count)
        return (key_pos[None, :] >= own_starts[:, None]) & (key_pos[None, :] <= own_pos[:, None])

    key_block_tile = (
        lax.all_gather(keys_low, "ctx", axis=0, tiled=True),
        lax.all_gather(values_low, "ctx", axis=0, tiled=True),
    )
    running_maximum = jnp.full(
        (KEY_VALUE_HEADS, query_group_width, total_row_count), NEGATIVE_LARGE, single_float
    )
    key_total_count = key_block_tile[0].shape[0]
    visible = key_mask(key_total_count)
    scores = jnp.einsum(
        "qhgd,khd->hgqk",
        query_matrix,
        key_block_tile[0].reshape(key_total_count, KEY_VALUE_HEADS, HEAD_SIZE),
        preferred_element_type=single_float,
    )
    masked = jnp.where(visible, scores, NEGATIVE_LARGE)
    new_max = jnp.maximum(running_maximum, jnp.max(masked, axis=-1))
    exp_terms = jnp.where(visible, jnp.exp(masked - new_max[..., None]), 0.0)
    run_sum = jnp.sum(exp_terms, axis=-1)
    run_acc = jnp.einsum(
        "hgqk,khd->hgqd",
        exp_terms.astype(bf16),
        key_block_tile[1].reshape(key_total_count, KEY_VALUE_HEADS, HEAD_SIZE),
        preferred_element_type=single_float,
    )
    running_maximum, run_sum, run_acc = (new_max, run_sum, run_acc)
    log_norm = running_maximum + jnp.log(run_sum)
    attn_four = jnp.transpose(run_acc / run_sum[..., None], (2, 0, 1, 3))
    attn_low = attn_four.reshape(total_row_count, QUERY_HEADS * HEAD_SIZE).astype(bf16)
    middle = residual + jnp.dot(attn_low, full_out, preferred_element_type=single_float)
    mlp_set = (
        lax.all_gather(gain_two, "fsdp", axis=0, tiled=True),
        lax.all_gather(w_gate, "fsdp", axis=0, tiled=True),
        lax.all_gather(w_up, "fsdp", axis=0, tiled=True),
        lax.all_gather(w_down, "fsdp", axis=0, tiled=True),
    )
    full_gain_two, full_gate, full_up, full_down = mlp_set
    unit_two, inv_two, normed_two = rms_forward(middle, full_gain_two)
    gate_proj = jnp.dot(normed_two, full_gate, preferred_element_type=single_float)
    up_proj = jnp.dot(normed_two, full_up, preferred_element_type=single_float)
    hidden_low = (jax.nn.silu(gate_proj) * up_proj).astype(bf16)
    mixed = middle + jnp.dot(hidden_low, full_down, preferred_element_type=single_float)
    grad_out = cotangent.reshape(total_row_count, model_width).astype(single_float)
    grad_low = grad_out.astype(bf16)
    grad_hidden = jnp.einsum("td,fd->tf", grad_low, full_down, preferred_element_type=single_float)
    sigmoid_gate = jax.nn.sigmoid(gate_proj)
    grad_gate = (
        grad_hidden * up_proj * sigmoid_gate * (1.0 + gate_proj * (1.0 - sigmoid_gate))
    ).astype(bf16)
    grad_up = (grad_hidden * (gate_proj * sigmoid_gate)).astype(bf16)
    grad_normed_two = jnp.einsum(
        "tf,df->td", grad_gate, full_gate, preferred_element_type=single_float
    ) + jnp.einsum("tf,df->td", grad_up, full_up, preferred_element_type=single_float)
    grad_gain_two, grad_mid_norm = rms_backward(grad_normed_two, unit_two, inv_two, full_gain_two)
    grad_middle = grad_out + grad_mid_norm
    grad_w_down = jnp.einsum("tf,td->fd", hidden_low, grad_low, preferred_element_type=single_float)
    grad_w_gate = jnp.einsum(
        "td,tf->df", normed_two, grad_gate, preferred_element_type=single_float
    )
    grad_w_up = jnp.einsum("td,tf->df", normed_two, grad_up, preferred_element_type=single_float)
    mlp_shards = (
        lax.psum_scatter(
            grad_gain_two.astype(jnp.bfloat16), "fsdp", scatter_dimension=0, tiled=True
        ).astype(jnp.float32),
        lax.psum_scatter(
            grad_w_gate.astype(jnp.bfloat16), "fsdp", scatter_dimension=0, tiled=True
        ).astype(jnp.float32),
        lax.psum_scatter(
            grad_w_up.astype(jnp.bfloat16), "fsdp", scatter_dimension=0, tiled=True
        ).astype(jnp.float32),
        lax.psum_scatter(
            grad_w_down.astype(jnp.bfloat16), "fsdp", scatter_dimension=0, tiled=True
        ).astype(jnp.float32),
    )
    grad_branch = grad_middle.astype(bf16)
    attention_gradient = jnp.einsum(
        "td,qd->tq", grad_branch, full_out, preferred_element_type=single_float
    ).astype(bf16)
    attention_gradient_four = attention_gradient.reshape(
        total_row_count, KEY_VALUE_HEADS, query_group_width, HEAD_SIZE
    )
    row_dot = jnp.einsum("qhgd,qhgd->hgq", attention_gradient_four.astype(single_float), attn_four)
    key_block_tile = (
        lax.all_gather(keys_low, "ctx", axis=0, tiled=True),
        lax.all_gather(values_low, "ctx", axis=0, tiled=True),
    )
    key_total_count = key_block_tile[0].shape[0]
    key_three_axes = key_block_tile[0].reshape(key_total_count, KEY_VALUE_HEADS, HEAD_SIZE)
    value_three_axes = key_block_tile[1].reshape(key_total_count, KEY_VALUE_HEADS, HEAD_SIZE)
    visible = key_mask(key_total_count)
    scores = jnp.einsum(
        "qhgd,khd->hgqk", query_matrix, key_three_axes, preferred_element_type=single_float
    )
    probs_f32 = jnp.where(
        visible, jnp.exp(jnp.where(visible, scores, NEGATIVE_LARGE) - log_norm[..., None]), 0.0
    )
    value_gradient_partial = jnp.einsum(
        "hgqk,qhgd->khd",
        probs_f32.astype(bf16),
        attention_gradient_four,
        preferred_element_type=single_float,
    )
    grad_probs = jnp.einsum(
        "qhgd,khd->hgqk",
        attention_gradient_four,
        value_three_axes,
        preferred_element_type=single_float,
    )
    grad_scores = (probs_f32 * (grad_probs - row_dot[..., None])).astype(bf16)
    grad_query = jnp.einsum(
        "hgqk,khd->qhgd", grad_scores, key_three_axes, preferred_element_type=single_float
    )
    key_gradient_partial = jnp.einsum(
        "hgqk,qhgd->khd", grad_scores, query_matrix, preferred_element_type=single_float
    )
    key_gradient_total = key_gradient_partial.reshape(key_total_count, KEY_VALUE_HEADS * HEAD_SIZE)
    value_gradient_total = value_gradient_partial.reshape(
        key_total_count, KEY_VALUE_HEADS * HEAD_SIZE
    )
    grad_query, key_gradient_total, value_gradient_total = (
        grad_query,
        key_gradient_total,
        value_gradient_total,
    )
    key_gradient_local, grad_values_own = (
        lax.psum_scatter(
            key_gradient_total.astype(jnp.bfloat16), "ctx", scatter_dimension=0, tiled=True
        ).astype(jnp.float32),
        lax.psum_scatter(
            value_gradient_total.astype(jnp.bfloat16), "ctx", scatter_dimension=0, tiled=True
        ).astype(jnp.float32),
    )
    grad_query_proj = (
        reverse_rotation(
            grad_query.reshape(total_row_count, QUERY_HEADS, HEAD_SIZE) * HEAD_SIZE ** (-0.5),
            cosine_table,
            sine_table,
        )
        .reshape(total_row_count, QUERY_HEADS * HEAD_SIZE)
        .astype(bf16)
    )
    grad_key_proj = (
        reverse_rotation(
            key_gradient_local.reshape(total_row_count, KEY_VALUE_HEADS, HEAD_SIZE),
            cosine_table,
            sine_table,
        )
        .reshape(total_row_count, KEY_VALUE_HEADS * HEAD_SIZE)
        .astype(bf16)
    )
    grad_value_proj = grad_values_own.astype(bf16)
    grad_normed_one = jnp.einsum(
        "tq,dq->td", grad_query_proj, full_query, preferred_element_type=single_float
    )
    grad_normed_one = grad_normed_one + jnp.einsum(
        "tq,dq->td", grad_key_proj, full_key, preferred_element_type=single_float
    )
    grad_normed_one = grad_normed_one + jnp.einsum(
        "tq,dq->td", grad_value_proj, full_value, preferred_element_type=single_float
    )
    grad_gain_one, grad_res_norm = rms_backward(grad_normed_one, unit_one, inv_one, full_gain_one)
    grad_tokens = grad_middle + grad_res_norm
    grad_w_out = jnp.einsum("tq,td->qd", attn_low, grad_branch, preferred_element_type=single_float)
    grad_w_query = jnp.einsum(
        "td,tq->dq", first_normalized, grad_query_proj, preferred_element_type=single_float
    )
    grad_w_key = jnp.einsum(
        "td,tq->dq", first_normalized, grad_key_proj, preferred_element_type=single_float
    )
    grad_w_value = jnp.einsum(
        "td,tq->dq", first_normalized, grad_value_proj, preferred_element_type=single_float
    )
    attn_shards = (
        lax.psum_scatter(
            grad_gain_one.astype(jnp.bfloat16), "fsdp", scatter_dimension=0, tiled=True
        ).astype(jnp.float32),
        lax.psum_scatter(
            grad_w_query.astype(jnp.bfloat16), "fsdp", scatter_dimension=0, tiled=True
        ).astype(jnp.float32),
        lax.psum_scatter(
            grad_w_key.astype(jnp.bfloat16), "fsdp", scatter_dimension=0, tiled=True
        ).astype(jnp.float32),
        lax.psum_scatter(
            grad_w_value.astype(jnp.bfloat16), "fsdp", scatter_dimension=0, tiled=True
        ).astype(jnp.float32),
        lax.psum_scatter(
            grad_w_out.astype(jnp.bfloat16), "fsdp", scatter_dimension=0, tiled=True
        ).astype(jnp.float32),
    )
    shard_set = (
        attn_shards[0],
        attn_shards[1],
        attn_shards[2],
        attn_shards[3],
        attn_shards[4],
        mlp_shards[0],
        mlp_shards[1],
        mlp_shards[2],
        mlp_shards[3],
    )
    totals = (
        lax.psum(shard_set[0].astype(jnp.bfloat16), "ctx").astype(jnp.float32),
        lax.psum(shard_set[1].astype(jnp.bfloat16), "ctx").astype(jnp.float32),
        lax.psum(shard_set[2].astype(jnp.bfloat16), "ctx").astype(jnp.float32),
        lax.psum(shard_set[3].astype(jnp.bfloat16), "ctx").astype(jnp.float32),
        lax.psum(shard_set[4].astype(jnp.bfloat16), "ctx").astype(jnp.float32),
        lax.psum(shard_set[5].astype(jnp.bfloat16), "ctx").astype(jnp.float32),
        lax.psum(shard_set[6].astype(jnp.bfloat16), "ctx").astype(jnp.float32),
        lax.psum(shard_set[7].astype(jnp.bfloat16), "ctx").astype(jnp.float32),
        lax.psum(shard_set[8].astype(jnp.bfloat16), "ctx").astype(jnp.float32),
    )
    return (
        mixed.reshape(tokens.shape),
        grad_tokens.reshape(tokens.shape),
        totals[0],
        totals[1],
        totals[2],
        totals[3],
        totals[4],
        totals[5],
        totals[6],
        totals[7],
        totals[8],
    )


def solution(mesh):
    placed = (
        P("fsdp", "ctx", None, None, None),
        P("fsdp", "ctx", None, None),
        P("fsdp"),
        P("fsdp", None),
        P("fsdp", None),
        P("fsdp", None),
        P("fsdp", None),
        P("fsdp"),
        P("fsdp", None),
        P("fsdp", None),
        P("fsdp", None),
        P("fsdp", "ctx", None, None, None),
    )
    return jax.shard_map(
        per_device,
        mesh=mesh,
        in_specs=placed,
        out_specs=(
            P("fsdp", "ctx", None, None, None),
            P("fsdp", "ctx", None, None, None),
            P("fsdp"),
            P("fsdp", None),
            P("fsdp", None),
            P("fsdp", None),
            P("fsdp", None),
            P("fsdp"),
            P("fsdp", None),
            P("fsdp", None),
            P("fsdp", None),
        ),
        check_vma=False,
    )
```

profile of v0, /device:TPU:0, one launch (start us, length us, event | category | flops | bytes accessed | tf_op | source)
XLA Modules:
  0.0 3607.5 jit_solution(13189515931861710635)
XLA Ops:
  10.8 9.6 all-gather
  21.8 35.8 all-gather.18.cloned.1.call-done
  57.7 3.3 convolution_convert_fusion.8
  62.1 42.5 %all-gather.12.cloned.1.call-done = bf16[2560,640]{1,0:T(8,128)(2,1)} async-done(((bf16[640,640]{1,0:T(8,128)(2,1)}), bf16[2560,640]{1,0:T(8,128)(2,1)}) %all-gather.12.cloned.1.call-update) | async-done | bytes 3276816 | tf_op jit(solution)/shard_map/all_gather | solution.py:103
  104.6 5.7 copy.41
  110.3 2.9 fusion.52
  116.9 8.3 all-gather.1
  125.5 4.8 all-gather.20.cloned.1.call-done
  130.3 2.4 copy.43
  132.7 125.7 %all-gather.16.cloned.1.call-done = bf16[2560,2560]{1,0:T(8,128)(2,1)} async-done(((bf16[640,2560]{1,0:T(8,128)(2,1)}), bf16[2560,2560]{1,0:T(8,128)(2,1)}) %all-gather.16.cloned.1.call-update) | async-done | bytes 13107216 | tf_op jit(solution)/shard_map/all_gather | solution.py:102
  258.4 17.7 copy.42
  276.0 6.7 fusion.53
  282.9 3.4 all-gather.14.cloned.1.call-done
  286.3 9.6 fusion.2
  296.0 10.9 fusion.3
  306.9 8.7 fusion.51
  315.6 97.8 %all-gather.22.cloned.1.call-done = bf16[2560,2560]{1,0:T(8,128)(2,1)} async-done(((bf16[640,2560]{1,0:T(8,128)(2,1)}), bf16[2560,2560]{1,0:T(8,128)(2,1)}) %all-gather.22.cloned.1.call-update) | async-done | bytes 13107216 | tf_op jit(solution)/shard_map/all_gather | solution.py:105
  413.4 6.7 multiply_reduce_fusion.4
  420.4 319.3 %all-gather.26.cloned.1.call-done = bf16[2560,7168]{1,0:T(8,128)(2,1)} async-done(((bf16[640,7168]{1,0:T(8,128)(2,1)}), bf16[2560,7168]{1,0:T(8,128)(2,1)}) %all-gather.26.cloned.1.call-update) | async-done | bytes 36700176 | tf_op jit(solution)/shard_map/all_gather | solution.py:171
  739.7 20.3 fusion.55
  760.1 305.9 %all-gather.24.cloned.1.call-done = bf16[2560,7168]{1,0:T(8,128)(2,1)} async-done(((bf16[640,7168]{1,0:T(8,128)(2,1)}), bf16[2560,7168]{1,0:T(8,128)(2,1)}) %all-gather.24.cloned.1.call-update) | async-done | bytes 36700176 | tf_op jit(solution)/shard_map/all_gather | solution.py:170
  1066.0 19.9 fusion.54
  1085.9 306.4 %all-gather.28.cloned.1.call-done = bf16[7168,2560]{1,0:T(8,128)(2,1)} async-done(((bf16[1792,2560]{1,0:T(8,128)(2,1)}), bf16[7168,2560]{1,0:T(8,128)(2,1)}) %all-gather.28.cloned.1.call-update) | async-done | bytes 36700176 | tf_op jit(solution)/shard_map/all_gather | solution.py:172
  1392.3 21.0 multiply_convert_fusion
  1413.3 17.7 fusion.56
  1431.0 19.8 multiply_reduce_fusion
  1452.6 9.9 convolution_convert_fusion.7
  1462.5 2.2 copy.45
  1464.7 10.5 bitcast_convert_fusion
  1475.2 2.4 copy.67
  1479.4 9.5 fusion.1
  1488.9 3.8 bitcast_convert_fusion.1
  1492.7 2.4 copy.65
  1495.2 16.0 reduce-scatter.30.cloned.1.call-done
  1511.2 3.9 convolution_convert_fusion.5
  1515.1 30.2 reduce-scatter.28.cloned.1.call-done
  1546.6 2.8 convolution_convert_fusion.6
  1549.4 7.9 convolution_convert_fusion.3
  1557.4 5.5 convolution_multiply_fusion
  1564.0 6.8 convolution_convert_fusion.4
  1571.9 17.0 convolution_convert_fusion.1
  1589.0 16.9 convolution_convert_fusion.2
  1607.0 17.2 convolution_convert_fusion
  1624.5 16.4 reduce-scatter.22.cloned.1.call-done
  1640.9 128.6 %reduce-scatter.26.cloned.1.call-done = bf16[640,2560]{1,0:T(8,128)(2,1)} async-done(((bf16[2560,2560]{1,0:T(8,128)(2,1)}), bf16[640,2560]{1,0:T(8,128)(2,1)}) %reduce-scatter.26.cloned.1.call-update) | async-done | bytes 3276816 | tf_op jit(solution)/shard_map/reduce_scatter | solution.py:323
  1769.5 128.6 %reduce-scatter.20.cloned.1.call-done = bf16[640,2560]{1,0:T(8,128)(2,1)} async-done(((bf16[2560,2560]{1,0:T(8,128)(2,1)}), bf16[640,2560]{1,0:T(8,128)(2,1)}) %reduce-scatter.20.cloned.1.call-update) | async-done | bytes 3276816 | tf_op jit(solution)/shard_map/reduce_scatter | solution.py:314
  1898.1 317.1 %reduce-scatter.34.cloned.1.call-done = bf16[640,7168]{1,0:T(8,128)(2,1)} async-done(((bf16[2560,7168]{1,0:T(8,128)(2,1)}), bf16[640,7168]{1,0:T(8,128)(2,1)}) %reduce-scatter.34.cloned.1.call-update) | async-done | bytes 9175056
  2215.3 317.4 %reduce-scatter.32.cloned.1.call-done = bf16[640,7168]{1,0:T(8,128)(2,1)} async-done(((bf16[2560,7168]{1,0:T(8,128)(2,1)}), bf16[640,7168]{1,0:T(8,128)(2,1)}) %reduce-scatter.32.cloned.1.call-update) | async-done | bytes 9175056
  2532.7 317.1 %reduce-scatter.36.cloned.1.call-done = bf16[1792,2560]{1,0:T(8,128)(2,1)} async-done(((bf16[7168,2560]{1,0:T(8,128)(2,1)}), bf16[1792,2560]{1,0:T(8,128)(2,1)}) %reduce-scatter.36.cloned.1.call-update) | async-done | bytes 9175056
  2851.7 9.1 fusion.57
  2860.8 18.2 convolution_add_fusion.3
  2879.1 3.4 convolution_add_fusion.1
  2882.6 2.3 multiply_reduce_fusion.1
  2884.9 15.1 all-reduce.7
  2900.2 14.9 all-reduce.5
  2916.3 2.8 multiply_add_fusion
  2919.1 630.5 %all-reduce.10.cloned.1.call-done = (bf16[640,2560]{1,0:T(8,128)(2,1)}, bf16[640,640]{1,0:T(8,128)(2,1)}, bf16[640,640]{1,0:T(8,128)(2,1)}, bf16[640,2560]{1,0:T...) async-done(((bf16[640,2560]{1,0:T(8,128)(2,1)}, bf16[640,640]{1,0:T(8,128)(2,1)}, bf16[640,640]{1,0:T(8,128)(2,1)}, ...) | async-done | bytes 35717136 | tf_op jit(solution)/shard_map/psum | solution.py:340
  3549.6 2.6 convert_element_type.247
  3552.2 2.4 convert_element_type.249
  3554.6 3.7 convert_element_type.245
  3558.3 3.7 convert_element_type.251
  3562.0 12.8 convert_element_type.255
  3574.8 12.8 convert_element_type.257
  3587.6 12.9 convert_element_type.259
  (135 shorter events, 21.5 us)
Async XLA Ops:
  7.2 50.5 %all-gather.18.cloned.1.call-start = ((), (), s32[]{:S(2)}) async-start(), calls=%async_computation.12 | async-start | bytes 4096000 | tf_op jit(solution)/shard_map/all_gather | solution.py:104
  7.9 96.7 %all-gather.12.cloned.1.call-start = ((), (), s32[]{:S(2)}) async-start(), calls=%async_computation.9 | async-start | bytes 4096000 | tf_op jit(solution)/shard_map/all_gather | solution.py:103
  8.7 121.6 %all-gather.20.cloned.1.call-start = ((), (), s32[]{:S(2)}) async-start(), calls=%async_computation.13 | async-start | bytes 1474560 | tf_op jit(solution)/shard_map/all_gather | solution.py:140
  10.1 51.4 %copy-start.23 = (f32[128]{0:T(128)}, f32[128]{0:T(128)S(1)}, u32[]{:S(2)}) copy-start(f32[128]{0:T(128)S(1)} %rsqrt.21) | copy-start | bytes 1540
  20.4 41.5 %copy-start.20 = (f32[2560]{0:T(1024)}, f32[2560]{0:T(1024)S(1)}, u32[]{:S(2)}) copy-start(f32[2560]{0:T(1024)S(1)} %reshape.328) | copy-start | bytes 30724
  21.8 39.8 %copy-start.6 = (bf16[128,2560]{1,0:T(8,128)(2,1)}, bf16[128,2560]{1,0:T(8,128)(2,1)S(1)}, u32[]{:S(2)}) copy-start(bf16[128,2560]{1,0:T(8,128)(2,1)S(1)} %multiply_convert_fusion.4) | copy-start | bytes 1966084
  21.8 39.8 %copy-start.26 = (s32[1,1,2,64]{3,2,1,0:T(2,128)S(1)}, s32[1,1,2,64]{3,2,1,0:T(2,128)}, u32[]{:S(2)}) copy-start(s32[1,1,2,64]{3,2,1,0:T(2,128)} %param.13) | copy-start | bytes 1540
  21.8 40.1 %copy-start.1 = (bf16[1,1,2,64,2560]{4,3,2,1,0:T(8,128)(2,1)S(1)}, bf16[1,1,2,64,2560]{4,3,2,1,0:T(8,128)(2,1)}, u32[]{:S(2)}) copy-start(bf16[1,1,2,64,2560]{4,3,2,1,0:T(8,128)(2,1)} %param.12) | copy-start | bytes 1966084
  61.0 197.4 %all-gather.16.cloned.1.call-start = ((), (), s32[]{:S(2)}) async-start(), calls=%async_computation.11 | async-start | bytes 16384000 | tf_op jit(solution)/shard_map/all_gather | solution.py:102
  61.6 224.8 %all-gather.14.cloned.1.call-start = ((), (), s32[]{:S(2)}) async-start(), calls=%async_computation.10 | async-start | bytes 1474560 | tf_op jit(solution)/shard_map/all_gather | solution.py:139
  114.0 299.5 %all-gather.22.cloned.1.call-start = ((), (), s32[]{:S(2)}) async-start(), calls=%async_computation.14 | async-start | bytes 16384000 | tf_op jit(solution)/shard_map/all_gather | solution.py:105
  114.5 625.2 %all-gather.26.cloned.1.call-start = ((), (), s32[]{:S(2)}) async-start(), calls=%async_computation.16 | async-start | bytes 45875200 | tf_op jit(solution)/shard_map/all_gather | solution.py:171
  115.3 950.7 %all-gather.24.cloned.1.call-start = ((), (), s32[]{:S(2)}) async-start(), calls=%async_computation.15 | async-start | bytes 45875200 | tf_op jit(solution)/shard_map/all_gather | solution.py:170
  116.0 0.8 copy-start.25
  116.1 1276.2 %all-gather.28.cloned.1.call-start = ((), (), s32[]{:S(2)}) async-start(), calls=%async_computation.17 | async-start | bytes 45875200 | tf_op jit(solution)/shard_map/all_gather | solution.py:172
  116.8 1394.4 %reduce-scatter.30.cloned.1.call-start = ((), (), s32[]{:S(2)}) async-start(), calls=%async_computation.23 | async-start | bytes 1474560
  282.9 13.0 copy-start.9
  282.9 13.0 copy-start.11
  296.0 10.9 copy-start.18
  315.6 104.6 %copy-start.13 = (bf16[128,8,4,80]{0,3,2,1:T(8,128)(2,1)}, bf16[128,8,4,80]{0,3,2,1:T(8,128)(2,1)S(1)}, u32[]{:S(2)}) copy-start(bf16[128,8,4,80]{0,3,2,1:T(8,128)(2,1)S(1)} %get-tuple-element.41) | copy-start | bytes 1966084
  420.4 645.6 %copy-start.3 = (bf16[128,2560]{1,0:T(8,128)(2,1)}, bf16[128,2560]{1,0:T(8,128)(2,1)S(1)}, u32[]{:S(2)}) copy-start(bf16[128,2560]{1,0:T(8,128)(2,1)S(1)} %multiply_convert_fusion.3) | copy-start | bytes 1966084
  760.1 632.2 %copy-start.16 = (bf16[1,1,2,64,2560]{4,3,2,1,0:T(8,128)(2,1)S(1)}, bf16[1,1,2,64,2560]{4,3,2,1,0:T(8,128)(2,1)}, u32[]{:S(2)}) copy-start(bf16[1,1,2,64,2560]{4,3,2,1,0:T(8,128)(2,1)} %param.23) | copy-start | bytes 1966084
  1477.6 67.8 %reduce-scatter.28.cloned.1.call-start = ((), (), s32[]{:S(2)}) async-start(), calls=%async_computation.22 | async-start | bytes 1474560
  1479.4 9.5 copy-start.10
  1479.4 9.5 copy-start.12
  1488.9 3.8 copy-start
  1495.1 129.4 %reduce-scatter.24.cloned.1.call-start = ((), (), s32[]{:S(2)}) async-start(), calls=%async_computation.20 | async-start | bytes 4096000 | tf_op jit(solution)/shard_map/reduce_scatter | solution.py:320
  1515.1 125.8 %reduce-scatter.22.cloned.1.call-start = ((), (), s32[]{:S(2)}) async-start(), calls=%async_computation.19 | async-start | bytes 4096000 | tf_op jit(solution)/shard_map/reduce_scatter | solution.py:317
  1549.4 220.2 %reduce-scatter.26.cloned.1.call-start = ((), (), s32[]{:S(2)}) async-start(), calls=%async_computation.21 | async-start | bytes 16384000 | tf_op jit(solution)/shard_map/reduce_scatter | solution.py:323
  1557.3 340.8 %reduce-scatter.20.cloned.1.call-start = ((), (), s32[]{:S(2)}) async-start(), calls=%async_computation.18 | async-start | bytes 16384000 | tf_op jit(solution)/shard_map/reduce_scatter | solution.py:314
  1563.2 0.8 copy-start.7
  1570.9 1.1 copy-start.4
  1570.9 644.4 %reduce-scatter.34.cloned.1.call-start = ((), (), s32[]{:S(2)}) async-start(), calls=%async_computation.25 | async-start | bytes 45875200
  1589.0 943.7 %reduce-scatter.32.cloned.1.call-start = ((), (), s32[]{:S(2)}) async-start(), calls=%async_computation.24 | async-start | bytes 45875200
  1605.9 1.1 copy-start.17
  1605.9 1243.9 %reduce-scatter.36.cloned.1.call-start = ((), (), s32[]{:S(2)}) async-start(), calls=%async_computation.26 | async-start | bytes 45875200
  1624.2 1925.4 %all-reduce.10.cloned.1.call-start = ((), (), s32[]{:S(2)}) async-start(), calls=%async_computation.27 | async-start | bytes 71434240 | tf_op jit(solution)/shard_map/psum | solution.py:340
  2849.8 0.7 copy-start.27
  2849.8 1.9 copy-start.8
  2879.0 3.5 copy-start.2
  2879.0 3.5 copy-start.5
  2879.0 3.5 copy-start.19
  2879.0 3.5 copy-start.21
  2879.1 3.5 copy-start.24
  2882.5 2.3 copy-start.22
  3549.6 5.0 copy-start.15
  3554.6 3.7 copy-start.14
Sparse Core Ops, SparseCore 0:
  9.8 47.7 all-gather.17
  59.5 45.0 all-gather.11
  106.8 23.4 all-gather.19
  132.0 126.3 all-gather.15
  260.4 25.8 all-gather.13
  288.0 125.4 all-gather.21
  415.3 324.3 all-gather.25
  741.6 324.3 all-gather.23
  1067.9 324.3 all-gather.27
  1477.7 33.4 reduce-scatter.29
  1514.1 31.2 reduce-scatter.27
  1548.8 43.3 reduce-scatter.23
  1595.8 45.0 reduce-scatter.21
  1644.5 124.9 reduce-scatter.25
  1773.1 124.9 reduce-scatter.19
  1901.2 314.0 reduce-scatter.33
  2218.6 314.0 reduce-scatter.31
  2535.7 314.0 reduce-scatter.35
  2853.7 695.8 all-reduce.9
where the time goes:
time: 3610 us
  waiting for transfers between devices  3150 us (87%)
  matrix products  281 us (8%)
  other arithmetic  74.1 us (2%)
  blocking collectives  47.9 us (1%)
  local copies, waits for them, and re-layouts  39 us (1%)
    unnamed x24, waiting for transfers between devices  1000 us
    psum x1, waiting for transfers between devices, per_device(): lax.psum(shard_set[1].astype(jnp.bfloat16), 'ctx').astype(jnp.float32)  631 us
    all_gather x1, waiting for transfers between devices, per_device(): lax.all_gather(w_up, 'fsdp', axis=0, tiled=True)  319 us
    all_gather x1, waiting for transfers between devices, per_device(): lax.all_gather(w_down, 'fsdp', axis=0, tiled=True)  306 us
    all_gather x1, waiting for transfers between devices, per_device(): lax.all_gather(w_gate, 'fsdp', axis=0, tiled=True)  306 us
    reduce_scatter x1, waiting for transfers between devices, per_device(): lax.psum_scatter(grad_w_out.astype(jnp.bfloat16), 'fsdp', scatter_dimensi...  129 us
    reduce_scatter x1, waiting for transfers between devices, per_device(): lax.psum_scatter(grad_w_query.astype(jnp.bfloat16), 'fsdp', scatter_dimen...  129 us
    all_gather x1, waiting for transfers between devices, per_device(): lax.all_gather(w_query, 'fsdp', axis=0, tiled=True)  126 us
  transfers between devices with their start and end apart: 19, of which 18 were waited for; matrix products, arithmetic and copies ran while one was open for 7% of the time, Pallas kernels for 0%

commit v1 on v0

v1 whole, which is shorter than its diff:
```python
import jax
import jax.numpy as jnp
import numpy as np
from jax import lax
from jax.experimental import pallas as pl
from jax.experimental.pallas import tpu as pltpu
from jax.sharding import Mesh
from jax.sharding import PartitionSpec as P

QUERY_HEADS = 32
KEY_VALUE_HEADS = 8
HEAD_SIZE = 80
GROUP = QUERY_HEADS // KEY_VALUE_HEADS

EPS = 1e-05
THETA = 1000000.0
NEGATIVE_LARGE = -1e30

F32 = jnp.float32
BF16 = jnp.bfloat16


def after(value, *earlier):
    return lax.optimization_barrier((value,) + earlier)[0]


ANY = pl.BlockSpec(memory_space=pl.ANY)
VMEM_LIMIT = 56 * 1024 * 1024


def blank(shape, dtype):
    return pl.pallas_call(
        lambda out: None, out_shape=jax.ShapeDtypeStruct(shape, dtype), out_specs=ANY
    )()


def place(pieces, order):
    count = len(pieces)
    shape = pieces[0].shape

    def body(where, *refs):
        for i in range(count):

            @pl.when(pl.program_id(0) == i)
            def _(i=i):
                refs[count][0] = refs[i][...]

    zeros = (0,) * len(shape)
    return pl.pallas_call(
        body,
        out_shape=jax.ShapeDtypeStruct((count,) + shape, pieces[0].dtype),
        grid_spec=pltpu.PrefetchScalarGridSpec(
            num_scalar_prefetch=1,
            grid=(count,),
            in_specs=[pl.BlockSpec(shape, lambda g, where: zeros)] * count,
            out_specs=pl.BlockSpec((1,) + shape, lambda g, where: (where[g],) + zeros),
        ),
        compiler_params=pltpu.CompilerParams(vmem_limit_bytes=VMEM_LIMIT),
        cost_estimate=pl.CostEstimate(
            flops=0, transcendentals=0, bytes_accessed=2 * count * pieces[0].nbytes
        ),
    )(jnp.stack([jnp.asarray(i, jnp.int32) for i in order]), *pieces)


def join(pieces):
    return place(pieces, range(len(pieces))).reshape((-1,) + pieces[0].shape[1:])


def pack_qkv(w_query, w_key, w_value, t_of, n_t):
    rows = w_query.shape[0]
    q, kv = w_query.shape[1] // n_t, w_key.shape[1] // n_t
    n_f = len(t_of)

    def body(where, wq, wk, wv, *outs):
        for d in range(n_f):
            for t in range(n_t):

                @pl.when(where[d] == t)
                def _(d=d, t=t):
                    outs[d][:, :q] = wq[:, t * q : (t + 1) * q]
                    outs[d][:, q : q + kv] = wk[:, t * kv : (t + 1) * kv]
                    outs[d][:, q + kv :] = wv[:, t * kv : (t + 1) * kv]

    block = rows // 4
    return pl.pallas_call(
        body,
        out_shape=[jax.ShapeDtypeStruct((rows, q + 2 * kv), BF16)] * n_f,
        grid_spec=pltpu.PrefetchScalarGridSpec(
            num_scalar_prefetch=1,
            grid=(4,),
            in_specs=[
                pl.BlockSpec((block, w.shape[1]), lambda i, where: (i, 0))
                for w in (w_query, w_key, w_value)
            ],
            out_specs=[pl.BlockSpec((block, q + 2 * kv), lambda i, where: (i, 0))] * n_f,
        ),
        cost_estimate=pl.CostEstimate(
            flops=0, transcendentals=0, bytes_accessed=2 * w_query.nbytes
        ),
    )(jnp.stack(t_of).astype(jnp.int32), w_query, w_key, w_value)


def slice_columns(weight, t_of, size):
    rows, n_f = weight.shape[0], len(t_of)

    def body(where, *refs):
        for d in range(n_f):
            refs[n_f + d][...] = refs[d][...]

    block = rows // 4

    def in_map(d):
        return lambda i, where: (i, where[d])

    return pl.pallas_call(
        body,
        out_shape=[jax.ShapeDtypeStruct((rows, size), weight.dtype)] * n_f,
        grid_spec=pltpu.PrefetchScalarGridSpec(
            num_scalar_prefetch=1,
            grid=(4,),
            in_specs=[pl.BlockSpec((block, size), in_map(d)) for d in range(n_f)],
            out_specs=[pl.BlockSpec((block, size), lambda i, where: (i, 0))] * n_f,
        ),
        cost_estimate=pl.CostEstimate(
            flops=0, transcendentals=0, bytes_accessed=4 * n_f * rows * size
        ),
    )(jnp.stack(t_of).astype(jnp.int32), *[weight] * n_f)


def assemble_blocks(pieces, rows_of, core):
    n_z, n_c = len(pieces), len(pieces[0])
    n_f, rows, columns = pieces[0][0].shape
    flat = [piece for pair in pieces for piece in pair]
    count = len(flat)
    where = jnp.stack([jnp.asarray(i, jnp.int32) for i in rows_of] + [core.astype(jnp.int32)])

    def body(where, *refs):
        out = refs[count]
        for s in range(n_z):
            for own in range(n_c):

                @pl.when((pl.program_id(0) == s) & (where[n_z] == own))
                def _(s=s, own=own):
                    for e in range(n_c):
                        for i in range(n_f):
                            t = i * n_c + (own ^ e)
                            out[:, t * columns : (t + 1) * columns] = refs[s * n_c + e][i].astype(F32)

    return pl.pallas_call(
        body,
        out_shape=jax.ShapeDtypeStruct((n_z * rows, n_f * n_c * columns), F32),
        grid_spec=pltpu.PrefetchScalarGridSpec(
            num_scalar_prefetch=1,
            grid=(n_z,),
            in_specs=[pl.BlockSpec((n_f, rows, columns), lambda g, where: (0, 0, 0))] * count,
            out_specs=pl.BlockSpec((rows, n_f * n_c * columns), lambda g, where: (where[g], 0)),
        ),
        compiler_params=pltpu.CompilerParams(vmem_limit_bytes=VMEM_LIMIT),
        cost_estimate=pl.CostEstimate(
            flops=0, transcendentals=0, bytes_accessed=3 * count * flat[0].nbytes
        ),
    )(where, *flat)


def assemble_rows(pieces, rows_of):
    count = len(pieces)
    rows, columns = pieces[0].shape
    where = jnp.stack([jnp.asarray(i, jnp.int32) for i in rows_of])

    def body(where, *refs):
        for p in range(count):

            @pl.when(pl.program_id(0) == p)
            def _(p=p):
                refs[count][...] = refs[p][...].astype(F32)

    return pl.pallas_call(
        body,
        out_shape=jax.ShapeDtypeStruct((count * rows, columns), F32),
        grid_spec=pltpu.PrefetchScalarGridSpec(
            num_scalar_prefetch=1,
            grid=(count,),
            in_specs=[pl.BlockSpec((rows, columns), lambda g, where: (0, 0))] * count,
            out_specs=pl.BlockSpec((rows, columns), lambda g, where: (where[g], 0)),
        ),
        compiler_params=pltpu.CompilerParams(vmem_limit_bytes=VMEM_LIMIT),
        cost_estimate=pl.CostEstimate(
            flops=0, transcendentals=0, bytes_accessed=3 * count * pieces[0].nbytes
        ),
    )(where, *pieces)


def assemble_qkv(pieces, rows_of, core, n_c, q, kv):
    n_z = len(pieces)
    n_f, rows, columns = pieces[0][0].shape
    flat = [piece for pair in pieces for piece in pair]
    n_t = n_f * n_c
    where = jnp.stack([jnp.asarray(i, jnp.int32) for i in rows_of] + [core.astype(jnp.int32)])

    def body(where, *refs):
        ins, (out_q, out_k, out_v) = refs[: len(flat)], refs[len(flat) :]
        for s in range(n_z):
            for own in range(n_c):

                @pl.when((pl.program_id(0) == s) & (where[n_z] == own))
                def _(s=s, own=own):
                    for e in range(n_c):
                        block = ins[s * n_c + e]
                        for i in range(n_f):
                            t = i * n_c + (own ^ e)
                            part = block[i].astype(F32)
                            out_q[:, t * q : (t + 1) * q] = part[:, :q]
                            out_k[:, t * kv : (t + 1) * kv] = part[:, q : q + kv]
                            out_v[:, t * kv : (t + 1) * kv] = part[:, q + kv :]

    return pl.pallas_call(
        body,
        out_shape=[
            jax.ShapeDtypeStruct((n_z * rows, n_t * w), F32) for w in (q, kv, kv)
        ],
        grid_spec=pltpu.PrefetchScalarGridSpec(
            num_scalar_prefetch=1,
            grid=(n_z,),
            in_specs=[pl.BlockSpec((n_f, rows, columns), lambda g, where: (0, 0, 0))] * len(flat),
            out_specs=[
                pl.BlockSpec((rows, n_t * w), lambda g, where: (where[g], 0)) for w in (q, kv, kv)
            ],
        ),
        compiler_params=pltpu.CompilerParams(vmem_limit_bytes=VMEM_LIMIT),
        cost_estimate=pl.CostEstimate(
            flops=0, transcendentals=0, bytes_accessed=3 * len(flat) * flat[0].nbytes
        ),
    )(where, *flat)


def swap(value, axis, offset):
    size = lax.axis_size(axis)
    return lax.ppermute(value, axis, [(i, i ^ offset) for i in range(size)])


def gather_plane(own):
    n_f, n_c = lax.axis_size("f"), lax.axis_size("core")
    rows = own.shape[0]
    if n_f == 4 and rows % 32 == 0:
        half = rows // 2
        from_x = swap(own, "f", 1)
        from_y = swap(own, "f", 2)
        far_low = swap(from_x[:half], "f", 2)
        far_high = swap(from_y[half:], "f", 1)
        mine = [own, from_x, from_y, jnp.concatenate([far_low, far_high], axis=0)]
    else:
        mine = [own] + [swap(own, "f", d) for d in range(1, n_f)]
    blocks = []
    for part in mine:
        blocks.append(part)
        if n_c == 2:
            blocks.append(swap(part, "core", 1))
    return blocks


def scatter_plane(parts):
    n_f, n_c = lax.axis_size("f"), lax.axis_size("core")
    if n_c == 2:
        sums = []
        for d in range(n_f):
            sums.append(parts[d, 0] + swap(parts[d, 1].astype(BF16), "core", 1).astype(F32))
    else:
        sums = [parts[d, 0] for d in range(n_f)]
    rows = sums[0].shape[0]
    if n_f == 4 and rows % 32 == 0:
        half = rows // 2
        far = sums[3].astype(BF16)
        via_x = swap(far[:half], "f", 1).astype(F32)
        via_y = swap(far[half:], "f", 2).astype(F32)
        x_low = swap(sums[1][:half].astype(BF16), "f", 1)
        y_high = swap(sums[2][half:].astype(BF16), "f", 2)
        x_high = swap((sums[1][half:] + via_y).astype(BF16), "f", 1)
        y_low = swap((sums[2][:half] + via_x).astype(BF16), "f", 2)
        low = sums[0][:half] + x_low.astype(F32) + y_low.astype(F32)
        high = sums[0][half:] + x_high.astype(F32) + y_high.astype(F32)
        return jnp.concatenate([low, high], axis=0)
    total = sums[0]
    for d in range(1, n_f):
        total = total + swap(sums[d].astype(BF16), "f", d).astype(F32)
    return total


def pick(parts, index):
    return lax.dynamic_index_in_dim(parts, index, 0, keepdims=False)


def sum_along_z(parts, z_axis=0):
    n_z, z = lax.axis_size("z"), lax.axis_index("z")

    def chunk(k):
        return lax.dynamic_index_in_dim(
            parts, jnp.clip(k, 0, n_z - 1), z_axis, keepdims=False
        )

    up = down = None
    for step in range(1, n_z):
        send_up = chunk(z + n_z - step)
        send_down = chunk(z - n_z + step)
        if up is not None:
            send_up = (send_up.astype(F32) + up.astype(F32)).astype(BF16)
            send_down = (send_down.astype(F32) + down.astype(F32)).astype(BF16)
        up = lax.ppermute(send_up, "z", [(i, i + 1) for i in range(step)])
        down = lax.ppermute(send_down, "z", [(i, i - 1) for i in range(n_z - step, n_z)])
    total = chunk(z).astype(F32)
    if up is not None:
        total = total + up.astype(F32) + down.astype(F32)
    return total.astype(BF16)


def spread_along_z(own):
    n_z, z = lax.axis_size("z"), lax.axis_index("z")
    ups, downs = [own], [own]
    for step in range(1, n_z):
        ups.append(lax.ppermute(ups[-1], "z", [(i, i + 1) for i in range(step - 1, n_z - 1)]))
        downs.append(lax.ppermute(downs[-1], "z", [(i, i - 1) for i in range(1, n_z - step + 1)]))
    return [own] + [jnp.where(z >= s, ups[s], downs[n_z - s]) for s in range(1, n_z)]


def turn_along_z(own):
    n_z = lax.axis_size("z")
    return [own] + [
        lax.ppermute(own, "z", [(i, (i + s) % n_z) for i in range(n_z)]) for s in range(1, n_z)
    ]


def rms_parts(values):
    inverse = lax.rsqrt(jnp.mean(values * values, axis=-1, keepdims=True) + EPS)
    return values * inverse, inverse


def rms_backward(grad_normed, unit_rows, inverse, norm_gain):
    scaled = grad_normed * norm_gain
    grad_rows = inverse * (
        scaled - unit_rows * jnp.mean(scaled * unit_rows, axis=-1, keepdims=True)
    )
    return jnp.sum(grad_normed * unit_rows, axis=0), grad_rows


def rotate(values, cosine, sine):
    half = values.shape[1] // 2
    a, b = values[:, :half], values[:, half:]
    return jnp.concatenate([a * cosine - b * sine, b * cosine + a * sine], axis=1)


def rotate_back(grads, cosine, sine):
    half = grads.shape[1] // 2
    a, b = grads[:, :half], grads[:, half:]
    return jnp.concatenate([a * cosine + b * sine, b * cosine - a * sine], axis=1)


def dot(a, b, contract):
    return lax.dot_general(a, b, (contract, ((), ())), preferred_element_type=F32)


def stack_at(pieces, order):
    result = jnp.stack(pieces)
    for piece, index in zip(pieces, order, strict=True):
        result = lax.dynamic_update_index_in_dim(result, piece, index, 0)
    return result


def per_device(
    tokens, doc_starts, gain_one, w_query, w_key, w_value, w_out, gain_two, w_gate, w_up, w_down,
    cotangent,
):
    n_z, n_c, n_f = lax.axis_size("z"), lax.axis_size("core"), lax.axis_size("f")
    z, c, f = lax.axis_index("z"), lax.axis_index("core"), lax.axis_index("f")
    n_t = n_f * n_c
    block_len, width = tokens.shape[3], tokens.shape[4]
    rows = 2 * block_len
    plane = n_t * rows
    shard = width // n_f
    q_width = w_query.shape[1] // n_t
    kv_width = w_key.shape[1] // n_t
    hidden = w_gate.shape[1] // n_t
    qkv_width = q_width + 2 * kv_width
    heads = q_width // HEAD_SIZE

    own_x = tokens.reshape(rows, width)
    own_dy = cotangent.reshape(rows, width)
    t_of = [(f ^ d) * n_c + c for d in range(n_f)]

    qkv_parts = pack_qkv(w_query, w_key, w_value, t_of, n_t)
    qkv_parts = [qkv_parts[0]] + [swap(qkv_parts[d], "f", d) for d in range(1, n_f)]
    f_order = [f ^ d for d in range(n_f)]
    w_qkv = place(qkv_parts, f_order).reshape(width, qkv_width)

    gains = jnp.stack([gain_one, gain_two])
    gains = stack_at([gains] + [swap(gains, "f", d) for d in range(1, n_f)], f_order)
    gains = jnp.transpose(gains, (1, 0, 2)).reshape(2, width).astype(F32)
    gain_one_full, gain_two_full = gains[0], gains[1]

    x_all = join(gather_plane(own_x))
    starts_all = jnp.concatenate(gather_plane(doc_starts.reshape(1, rows)), axis=0)
    starts_all = starts_all.reshape(n_f, n_c * rows)

    def ctx_positions(z_index, core_offset):
        device = z_index * n_c + (c ^ core_offset)
        within = jnp.arange(rows, dtype=jnp.int32)
        return jnp.where(
            within < block_len,
            device * block_len + within,
            (2 * n_z * n_c - 1 - device) * block_len + within - block_len,
        )

    q_pos = jnp.concatenate([ctx_positions(z, e) for e in range(n_c)])
    k_pos = jnp.concatenate(
        [ctx_positions((z - s) % n_z, e) for s in range(n_z) for e in range(n_c)]
    )
    rel_pos = (q_pos[None, :] - starts_all).astype(F32).reshape(plane)
    inv_freq = THETA ** (-(jnp.arange(HEAD_SIZE // 2, dtype=F32) * 2.0) / HEAD_SIZE)
    angles = inv_freq[:, None] * rel_pos[None, :]
    cosine, sine = jnp.cos(angles), jnp.sin(angles)

    def ffn_slices(weight, *earlier):
        parts = slice_columns(weight, t_of, hidden)
        parts = [parts[0]] + [swap(after(parts[d], *earlier), "f", d) for d in range(1, n_f)]
        return place(parts, f_order).reshape(width, hidden)

    h_one = (rms_parts(x_all.astype(F32))[0] * gain_one_full).astype(BF16)
    qkv = dot(w_qkv, h_one, ((0,), (1,)))
    query = rotate(qkv[:q_width].reshape(heads, HEAD_SIZE, plane), cosine, sine)
    query = (query * HEAD_SIZE ** (-0.5)).astype(BF16)
    key = rotate(qkv[q_width : q_width + kv_width].reshape(1, HEAD_SIZE, plane), cosine, sine)
    key_value = jnp.concatenate([key[0].astype(BF16), qkv[q_width + kv_width :].astype(BF16)], axis=0)

    gate_full = ffn_slices(w_gate, key_value)
    up_full = ffn_slices(w_up, key_value)
    dy_all = join(gather_plane(after(own_dy, key_value)))

    kv_all = jnp.stack(turn_along_z(key_value))
    span = n_c * rows
    kv_all = kv_all.reshape(n_z, 2, HEAD_SIZE, n_f, span)
    kv_all = jnp.transpose(kv_all, (1, 3, 2, 0, 4)).reshape(2, n_f, HEAD_SIZE, n_z * span)
    keys, values = kv_all[0], kv_all[1]
    queries = jnp.transpose(query.reshape(heads, HEAD_SIZE, n_f, span), (2, 0, 1, 3))
    visible = (k_pos[None, None, :] >= starts_all[:, :, None]) & (
        k_pos[None, None, :] <= q_pos[None, :, None]
    )
    visible = visible[:, None]
    scores = jnp.einsum("shcq,sck->shqk", queries, keys, preferred_element_type=F32)
    masked = jnp.where(visible, scores, NEGATIVE_LARGE)
    row_max = jnp.max(masked, axis=-1, keepdims=True)
    terms = jnp.where(visible, jnp.exp(masked - row_max), 0.0)
    probs = terms / jnp.sum(terms, axis=-1, keepdims=True)
    probs_low = probs.astype(BF16)
    attn = jnp.einsum("shqk,sck->shcq", probs_low, values, preferred_element_type=F32)
    attn_low = jnp.transpose(attn.astype(BF16), (1, 2, 0, 3)).reshape(q_width, plane)

    out_rows = lax.dynamic_slice_in_dim(w_out, c * q_width, q_width, 0)
    projected = dot(attn_low, out_rows, ((0,), (0,)))
    residual = own_x.astype(F32)
    middle = residual + scatter_plane(projected.reshape(n_f, n_c, rows, width))
    unit_two, inv_two = rms_parts(middle)
    h_two_own = (unit_two * gain_two_full).astype(BF16)
    h_two = join(gather_plane(h_two_own))

    down_rows = lax.dynamic_slice_in_dim(w_down, c * hidden, hidden, 0)
    gate = dot(h_two, gate_full, ((1,), (0,)))
    up = dot(h_two, up_full, ((1,), (0,)))
    sigmoid = jax.nn.sigmoid(gate)
    silu = gate * sigmoid
    mid = (silu * up).astype(BF16)
    grad_down = dot(mid, dy_all, ((0,), (0,))).astype(BF16)
    grad_mid = dot(dy_all, down_rows, ((1,), (1,)))
    grad_g = (grad_mid * up * sigmoid * (1.0 + gate * (1.0 - sigmoid))).astype(BF16)
    grad_u = (grad_mid * silu).astype(BF16)
    grad_h_two = dot(grad_g, gate_full, ((1,), (1,))) + dot(grad_u, up_full, ((1,), (1,)))
    grad_gate = dot(h_two, grad_g, ((0,), (0,))).astype(BF16)
    grad_up = dot(h_two, grad_u, ((0,), (0,))).astype(BF16)
    grad_h_two = scatter_plane(grad_h_two.reshape(n_f, n_c, rows, width))
    mixed = middle + scatter_plane(
        dot(mid, down_rows, ((1,), (0,))).reshape(n_f, n_c, rows, width)
    )
    grad_gain_two, grad_norm = rms_backward(grad_h_two, unit_two, inv_two, gain_two_full)
    grad_middle = own_dy.astype(F32) + grad_norm

    grad_branch = join(gather_plane(grad_middle.astype(BF16)))
    grad_attn = dot(out_rows, grad_branch, ((1,), (1,))).astype(BF16)
    grad_out = dot(attn_low, grad_branch, ((1,), (0,))).astype(BF16)
    grad_attn = jnp.transpose(grad_attn.reshape(heads, HEAD_SIZE, n_f, span), (2, 0, 1, 3))
    delta = jnp.sum(grad_attn.astype(F32) * attn, axis=2)
    grad_values = jnp.einsum("shqk,shcq->sck", probs_low, grad_attn, preferred_element_type=F32)
    grad_probs = jnp.einsum("shcq,sck->shqk", grad_attn, values, preferred_element_type=F32)
    grad_scores = (probs * (grad_probs - delta[..., None])).astype(BF16)
    grad_query = jnp.einsum("shqk,sck->shcq", grad_scores, keys, preferred_element_type=F32)
    grad_keys = jnp.einsum("shqk,shcq->sck", grad_scores, queries, preferred_element_type=F32)
    grad_kv = jnp.concatenate([grad_keys, grad_values], axis=1)
    grad_kv = grad_kv.reshape(n_f, 2 * HEAD_SIZE, n_z, span)
    grad_kv = jnp.transpose(grad_kv, (2, 1, 0, 3)).reshape(n_z, 2 * HEAD_SIZE, plane)
    kv_total = grad_kv[0]
    for s in range(1, n_z):
        kv_total = kv_total + lax.ppermute(
            grad_kv[s].astype(BF16), "z", [(i, (i - s) % n_z) for i in range(n_z)]
        ).astype(F32)
    grad_query = jnp.transpose(grad_query, (1, 2, 0, 3)).reshape(heads, HEAD_SIZE, plane)
    grad_qkv = jnp.concatenate(
        [
            rotate_back(grad_query * HEAD_SIZE ** (-0.5), cosine, sine).reshape(q_width, plane),
            rotate_back(kv_total[None, :HEAD_SIZE], cosine, sine)[0],
            kv_total[HEAD_SIZE:],
        ],
        axis=0,
    ).astype(BF16)
    grad_h_one = dot(grad_qkv, w_qkv, ((0,), (1,)))
    grad_w_qkv = dot(h_one, grad_qkv, ((0,), (1,))).astype(BF16)
    grad_h_one = scatter_plane(grad_h_one.reshape(n_f, n_c, rows, width))
    unit_one, inv_one = rms_parts(residual)
    grad_gain_one, grad_norm = rms_backward(grad_h_one, unit_one, inv_one, gain_one_full)
    grad_tokens = grad_middle + grad_norm

    z_order = [(z - s) % n_z for s in range(n_z)]

    def both_cores(own):
        pieces = []
        for piece in spread_along_z(own):
            pieces.append([piece] + [swap(piece, "core", e) for e in range(1, n_c)])
        return pieces

    def finish_rows(grad):
        n_rows = grad.shape[0]
        piece_rows = n_rows // n_z
        pieces = both_cores(sum_along_z(grad.reshape(n_z, piece_rows, width)))
        if piece_rows % 16 == 0:
            return assemble_rows(
                [piece for pair in pieces for piece in pair],
                [(c ^ e) * n_z + zi for zi in z_order for e in range(n_c)],
            )
        result = blank((n_c, n_z, piece_rows, width), F32)
        for pair, zi in zip(pieces, z_order, strict=True):
            for e, piece in enumerate(pair):
                result = lax.dynamic_update_slice(
                    result, piece.astype(F32)[None, None], (c ^ e, zi, 0, 0)
                )
        return result.reshape(n_c * n_rows, width)

    def column_pieces(grad):
        columns = grad.shape[1]
        own = sum_along_z(grad.reshape(n_f, n_z, shard // n_z, columns), 1)
        parts = [pick(own, f)]
        for d in range(1, n_f):
            parts.append(swap(pick(own, f ^ d), "f", d))
        return both_cores(place(parts, f_order))

    def finish_columns(pieces, low, high):
        piece_rows = pieces[0][0].shape[1]
        if piece_rows % 16 == 0:
            return assemble_blocks(pieces, z_order, c)
        out = blank((n_z, piece_rows, n_f, n_c, high - low), F32)
        for pair, zi in zip(pieces, z_order, strict=True):
            for e, piece in enumerate(pair):
                update = jnp.transpose(piece[:, :, low:high].astype(F32), (1, 0, 2))
                out = lax.dynamic_update_slice(out, update[None, :, :, None], (zi, 0, 0, c ^ e, 0))
        return out.reshape(shard, n_t * (high - low))

    total_down = finish_rows(grad_down)
    total_gate = finish_columns(column_pieces(grad_gate), 0, hidden)
    total_up = finish_columns(column_pieces(grad_up), 0, hidden)
    total_out = finish_rows(grad_out)
    qkv_pieces = column_pieces(grad_w_qkv)
    if qkv_pieces[0][0].shape[1] % 16 == 0:
        total_query, total_key, total_value = assemble_qkv(
            qkv_pieces, z_order, c, n_c, q_width, kv_width
        )
    else:
        total_query = finish_columns(qkv_pieces, 0, q_width)
        total_key = finish_columns(qkv_pieces, q_width, q_width + kv_width)
        total_value = finish_columns(qkv_pieces, q_width + kv_width, qkv_width)
    gain_grads = lax.psum(jnp.stack([grad_gain_one, grad_gain_two]), ("z", "core", "f"))
    gain_grads = lax.dynamic_slice_in_dim(gain_grads, f * shard, shard, 1)
    return (
        mixed.reshape(tokens.shape),
        grad_tokens.reshape(tokens.shape),
        gain_grads[0],
        total_query,
        total_key,
        total_value,
        total_out,
        gain_grads[1],
        total_gate,
        total_up,
        total_down,
    )


def solution(mesh):
    n_ctx, n_fsdp = mesh.shape["ctx"], mesh.shape["fsdp"]
    n_core = KEY_VALUE_HEADS // n_fsdp
    inner = Mesh(
        np.asarray(mesh.devices).reshape(n_ctx // n_core, n_core, n_fsdp), ("z", "core", "f")
    )
    ctx = ("z", "core")
    return jax.shard_map(
        per_device,
        mesh=inner,
        in_specs=(
            P("f", ctx, None, None, None),
            P("f", ctx, None, None),
            P("f"),
            P("f", None),
            P("f", None),
            P("f", None),
            P("f", None),
            P("f"),
            P("f", None),
            P("f", None),
            P("f", None),
            P("f", ctx, None, None, None),
        ),
        out_specs=(
            P("f", ctx, None, None, None),
            P("f", ctx, None, None, None),
            P("f"),
            P("f", None),
            P("f", None),
            P("f", None),
            P("f", None),
            P("f"),
            P("f", None),
            P("f", None),
            P("f", None),
        ),
        check_vma=False,
    )
```

time: 3610 us -> 1400 us (0.39)
  waiting for transfers between devices: 3150 us -> 553 us
  starting transfers between devices: 1.02 us -> 265 us
  matrix products: 281 us -> 142 us
  Pallas kernels: 0 us -> 120 us
  local copies, waits for them, and re-layouts: 39 us -> 135 us
  other arithmetic: 74.1 us -> 127 us
    all_gather x9 -> x0, waiting for transfers between devices: 1240 us -> none  [the longest x1 319 us: per_device(): lax.all_gather(w_up, 'fsdp', axis=0, tiled=True)]
    unnamed x24 -> x0, waiting for transfers between devices: 1000 us -> none
    psum x1 -> x0, waiting for transfers between devices: 631 us -> none  [per_device(): lax.psum(shard_set[1].astype(jnp.bfloat16), 'ctx').astype(jnp.float32)]
    ppermute x0 -> x186, waiting for transfers between devices: none -> 553 us  [the longest x120 240 us: swap(): return lax.ppermute(value, axis, [(i, i ^ offset) for i in range(size)])]
    reduce_scatter x4 -> x0, waiting for transfers between devices: 274 us -> none  [the longest x1 129 us: per_device(): lax.psum_scatter(grad_w_out.astype(jnp.bfloat16), 'fsdp', scatter_dimensi...]
    ppermute x0 -> x186, starting transfers between devices: none -> 265 us  [the longest x15 90.2 us: sum_along_z(): up = lax.ppermute(send_up, 'z', [(i, i + 1) for i in range(step)])]
    dot_general x27 -> x20, matrix products: 281 us -> 130 us  [the longest x15 107 us: dot(): lax.dot_general(a, b, (contract, ((), ())), preferred_element_type=F32)]
    pallas_call x0 -> x18, Pallas kernels: none -> 120 us  [the longest x10 54.4 us: place(): pl.pallas_call(body, out_shape=jax.ShapeDtypeStruct((count,) + shape, pie...]
  transfers between devices with their start and end apart: 19 -> 186, of which waited for: 18 -> 63; matrix products, arithmetic and copies ran while one was open for 7% -> 17% of each run, Pallas kernels for 0% -> 7%
where the time goes in v1:
time: 1400 us; the launch traced here: 1390 us
  waiting for transfers between devices  553 us (40%)
  starting transfers between devices  265 us (19%)
  matrix products  142 us (10%)
  local copies, waits for them, and re-layouts  135 us (10%)
  other arithmetic  127 us (9%)
  Pallas kernels  120 us (9%)
  blocking collectives  39.3 us (3%)
    ppermute x120, waiting for transfers between devices, swap(): return lax.ppermute(value, axis, [(i, i ^ offset) for i in range(size)])  240 us
    ppermute x15, waiting for transfers between devices, spread_along_z(): lax.ppermute(downs[-1], 'z', [(i, i - 1) for i in range(1, n_z - step + 1)])  210 us
    dot_general x15, matrix products, dot(): lax.dot_general(a, b, (contract, ((), ())), preferred_element_type=F32)  107 us
    ppermute x15, starting transfers between devices, sum_along_z(): up = lax.ppermute(send_up, 'z', [(i, i + 1) for i in range(step)])  90.2 us
    ppermute x120, starting transfers between devices, swap(): return lax.ppermute(value, axis, [(i, i ^ offset) for i in range(size)])  86.5 us
    pallas_call x10, Pallas kernels, place(): pl.pallas_call(body, out_shape=jax.ShapeDtypeStruct((count,) + shape, pie...  54.4 us
    ppermute x15, waiting for transfers between devices, sum_along_z(): up = lax.ppermute(send_up, 'z', [(i, i + 1) for i in range(step)])  52.8 us
    psum x1, blocking collectives, per_device(): lax.psum(jnp.stack([grad_gain_one, grad_gain_two]), ('z', 'core', 'f'))  39.3 us
  transfers between devices with their start and end apart: 186, of which 63 were waited for; matrix products, arithmetic and copies ran while one was open for 17% of the time, Pallas kernels for 7%

profile of v1, /device:TPU:0, one launch (start us, length us, event | category | flops | bytes accessed | tf_op | source)
XLA Modules:
  0.0 1385.5 jit_solution(5371664729341936769)
XLA Ops:
  14.2 6.3 shard_map.203
  38.3 9.0 collective-permute-done.4.refs_2_
  53.2 27.6 %collective-permute-done.8 = bf16[64,2560]{1,0:T(8,128)(2,1)S(1)} collective-permute-done((bf16[64,2560]{1,0:T(8,128)(2,1)S(1)}, bf16[64,2560]{1,0:T(8,128)(2,1)S(1)}, u32[]{:S(2)}, u32[]{:S(2)}) %collective-permute-start.8) | collective-permute-done | bytes 327712 | tf_op jit(solution)/shard_map/ppermute | solution.py:238
  82.3 6.9 collective-permute-done.9
  104.6 7.1 shard_map.205
  137.3 18.6 %collective-permute-done.22 = bf16[160,1024]{1,0:T(8,128)(2,1)} collective-permute-done((bf16[160,1024]{1,0:T(8,128)(2,1)}, bf16[160,1024]{1,0:T(8,128)(2,1)}, u32[]{:S(2)}, u32[]{:S(2)}) %collective-permute-start.22) | collective-permute-done | bytes 327712 | tf_op jit(solution)/shard_map/ppermute | solution.py:327
  172.5 12.7 fusion.166
  185.2 7.0 fusion.10
  224.2 8.9 collective-permute-done.31
  274.8 31.3 %collective-permute-done.64 = bf16[64,2560]{1,0:T(8,128)(2,1)} collective-permute-done((bf16[64,2560]{1,0:T(8,128)(2,1)}, bf16[64,2560]{1,0:T(8,128)(2,1)}, u32[]{:S(2)}, u32[]{:S(2)}) %collective-permute-start.64) | collective-permute-done | bytes 327712 | tf_op jit(solution)/shard_map/ppermute | solution.py:238
  314.2 17.5 %collective-permute-done.47.refs_3_ = bf16[640,896]{1,0:T(8,128)(2,1)} collective-permute-done((bf16[640,896]{1,0:T(8,128)(2,1)}, bf16[640,896]{1,0:T(8,128)(2,1)}, u32[]{:S(2)}, u32[]{:S(2)}) %collective-permute-start.47) | collective-permute-done | bytes 1146912 | tf_op jit(solution)/shard_map/ppermute | solution.py:238
  331.7 23.7 %collective-permute-done.42.refs_1_ = bf16[640,896]{1,0:T(8,128)(2,1)} collective-permute-done((bf16[640,896]{1,0:T(8,128)(2,1)}, bf16[640,896]{1,0:T(8,128)(2,1)}, u32[]{:S(2)}, u32[]{:S(2)}) %collective-permute-start.42) | collective-permute-done | bytes 1146912 | tf_op jit(solution)/shard_map/ppermute | solution.py:238
  356.8 23.6 %collective-permute-done.44.refs_3_ = bf16[640,896]{1,0:T(8,128)(2,1)} collective-permute-done((bf16[640,896]{1,0:T(8,128)(2,1)}, bf16[640,896]{1,0:T(8,128)(2,1)}, u32[]{:S(2)}, u32[]{:S(2)}) %collective-permute-start.44) | collective-permute-done | bytes 1146912 | tf_op jit(solution)/shard_map/ppermute | solution.py:238
  381.0 6.0 fusion.5
  399.5 7.0 shard_map.211
  408.4 9.0 collective-permute-done.40
  417.5 10.3 fusion.11
  430.2 7.1 shard_map.206
  437.4 8.0 fusion.178
  445.4 8.7 multiply_convert_fusion.3
  454.2 8.2 fusion.179
  462.4 7.5 convolution_convert_fusion.1
  470.0 7.5 fusion.13
  477.5 6.8 convolution_convert_fusion
  484.3 7.3 convolution_convert_fusion.2
  491.7 11.7 convolution_add_fusion
  503.4 7.0 convert.118
  560.4 6.5 collective-permute-done.53
  615.7 13.1 collective-permute-done.79.refs_4_
  644.8 11.4 collective-permute-done.152
  658.9 6.0 collective-permute-done.82
  665.5 14.8 %collective-permute-done.171 = bf16[224,2560]{1,0:T(8,128)(2,1)S(1)} collective-permute-done((bf16[224,2560]{1,0:T(8,128)(2,1)S(1)}, bf16[224,2560]{1,0:T(8,128)(2,1)S(1)}, u32[]{:S(2)}, u32[]{:S(2)}) %collective-permute-start.171) | collective-permute-done | bytes 1146912 | tf_op jit(solution)/shard_map/ppermute | solution.py:307
  683.5 6.0 collective-permute-start.134
  691.0 7.0 shard_map.212
  712.0 7.4 multiply_convert_fusion
  734.3 6.2 fusion.47
  754.7 11.1 collective-permute-done.85
  765.9 6.5 collective-permute-start.153
  783.2 9.1 fusion.176
  793.9 7.2 convolution_convert_fusion.3
  827.6 6.4 collective-permute-done.139.refs_2_
  839.0 19.1 %collective-permute-start.97 = (bf16[4,160,480]{2,1,0:T(8,128)(2,1)}, bf16[4,160,480]{2,1,0:T(8,128)(2,1)S(1)}, u32[]{:S(2)}, u32[]{:S(2)}) collective-permute-start(bf16[4,160,480]{2,1,0:T(8,128)(2,1)} %get-tuple-element.117), channel_id=1, source_target_pairs={{0,8},{1,9},{2,10},{3,11},{4,12},{5,13},{6,14},{7,15}} | collective-permute-start | bytes 1843208 | tf_op jit(solution)/shard_map/ppermute | solution.py:307
  859.5 13.2 collective-permute-done.97
  932.5 14.1 %collective-permute-done.121 = bf16[80,2560]{1,0:T(8,128)(2,1)S(1)} collective-permute-done((bf16[80,2560]{1,0:T(8,128)(2,1)S(1)}, bf16[80,2560]{1,0:T(8,128)(2,1)S(1)}, u32[]{:S(2)}, u32[]{:S(2)}) %collective-permute-start.121) | collective-permute-done | bytes 409632 | tf_op jit(solution)/shard_map/ppermute | solution.py:308
  957.8 8.7 collective-permute-start.161
  972.0 7.3 collective-permute-done.143
  979.3 20.7 %collective-permute-start.99 = (bf16[4,160,480]{2,1,0:T(8,128)(2,1)S(1)}, bf16[4,160,480]{2,1,0:T(8,128)(2,1)S(1)}, u32[]{:S(2)}, u32[]{:S(2)}) collective-permute-start(bf16[4,160,480]{2,1,0:T(8,128)(2,1)S(1)} %get-tuple-element.115), channel_id=1, source_target_pairs={{0,8},{8,16},{16,24},{1,9},{9,17},{17,25},{2,10},{10,18},{18,26},{... | collective-permute-start | bytes 1843208 | tf_op jit(solution)/shard_map/ppermute | solution.py:307
  1013.7 8.2 collective-permute-start.177
  1022.1 8.0 collective-permute-start.178
  1034.5 22.3 %collective-permute-done.162 = bf16[4,160,896]{2,1,0:T(8,128)(2,1)} collective-permute-done((bf16[4,160,896]{2,1,0:T(8,128)(2,1)S(1)}, bf16[4,160,896]{2,1,0:T(8,128)(2,1)}, u32[]{:S(2)}, u32[]{:S(2)}) %collective-permute-start.162) | collective-permute-done | bytes 1146912 | tf_op jit(solution)/shard_map/ppermute | solution.py:320
  1058.9 31.1 %collective-permute-done.126 = bf16[80,2560]{1,0:T(8,128)(2,1)S(1)} collective-permute-done((bf16[80,2560]{1,0:T(8,128)(2,1)S(1)}, bf16[80,2560]{1,0:T(8,128)(2,1)S(1)}, u32[]{:S(2)}, u32[]{:S(2)}) %collective-permute-start.126) | collective-permute-done | bytes 409632 | tf_op jit(solution)/shard_map/ppermute | solution.py:320
  1101.6 13.0 collective-permute-done.144
  1121.4 13.1 collective-permute-done.163
  1142.1 12.2 collective-permute-done.108
  1158.3 20.5 %collective-permute-done.179 = bf16[224,2560]{1,0:T(8,128)(2,1)S(1)} collective-permute-done((bf16[224,2560]{1,0:T(8,128)(2,1)S(1)}, bf16[224,2560]{1,0:T(8,128)(2,1)S(1)}, u32[]{:S(2)}, u32[]{:S(2)}) %collective-permute-start.179) | collective-permute-done | bytes 1146912 | tf_op jit(solution)/shard_map/ppermute | solution.py:320
  1179.3 32.5 %collective-permute-done.109 = bf16[4,160,480]{2,1,0:T(8,128)(2,1)S(1)} collective-permute-done((bf16[4,160,480]{2,1,0:T(8,128)(2,1)S(1)}, bf16[4,160,480]{2,1,0:T(8,128)(2,1)S(1)}, u32[]{:S(2)}, u32[]{:S(2)}) %collective-permute-start.109) | collective-permute-done | bytes 614432 | tf_op jit(solution)/shard_map/ppermute | solution.py:320
  1219.8 23.1 %collective-permute-done.164 = bf16[4,160,896]{2,1,0:T(8,128)(2,1)S(1)} collective-permute-done((bf16[4,160,896]{2,1,0:T(8,128)(2,1)}, bf16[4,160,896]{2,1,0:T(8,128)(2,1)S(1)}, u32[]{:S(2)}, u32[]{:S(2)}) %collective-permute-start.164) | collective-permute-done | bytes 1146912 | tf_op jit(solution)/shard_map/ppermute | solution.py:320
  1243.8 31.2 %collective-permute-done.110 = bf16[4,160,480]{2,1,0:T(8,128)(2,1)S(1)} collective-permute-done((bf16[4,160,480]{2,1,0:T(8,128)(2,1)S(1)}, bf16[4,160,480]{2,1,0:T(8,128)(2,1)S(1)}, u32[]{:S(2)}, u32[]{:S(2)}) %collective-permute-start.110) | collective-permute-done | bytes 614432 | tf_op jit(solution)/shard_map/ppermute | solution.py:320
  1290.2 39.3 %psum.7 = f32[2,2560]{1,0:T(2,128)S(1)} all-reduce(f32[2,2560]{1,0:T(2,128)S(1)} %pad_maximum_fusion.9), channel_id=1, replica_groups=mesh['z'=4,'core'=2,'f'=4] {'z','core','f'}, use_global_device_ids=true, to_apply=%region_10.11 | all-reduce | flops 5120 | bytes 40960 | tf_op jit(solution)/shard_map/psum | solution.py:574
  1336.4 6.7 shard_map.215
  1343.1 11.1 shard_map.217
  1354.2 11.1 shard_map.219
  1366.2 7.8 shard_map.214
  1374.0 11.3 shard_map.220
  (897 shorter events, 565.0 us)
Async XLA Ops:
  36.2 67.8 %collective-permute-start.3 = (bf16[128,2560]{1,0:T(8,128)(2,1)}, bf16[128,2560]{1,0:T(8,128)(2,1)}, u32[]{:S(2)}, u32[]{:S(2)}) collective-permute-start(bf16[128,2560]{1,0:T(8,128)(2,1)} %bitcast.9.refs_0_), channel_id=1, source_target_pairs={{0,4},{4,0},{1,5},{5,1},{2,6},{6,2},{3,7},{7,3},{8,12},{12,8},{9,1... | collective-permute-start | bytes 1966088 | tf_op jit(solution)/shard_map/ppermute | solution.py:238
  36.3 53.7 %collective-permute-start = (bf16[640,480]{0,1:T(8,128)(2,1)S(1)}, bf16[640,480]{0,1:T(8,128)(2,1)S(1)}, u32[]{:S(2)}, u32[]{:S(2)}) collective-permute-start(bf16[640,480]{0,1:T(8,128)(2,1)S(1)} %copy-done.104), channel_id=1, source_target_pairs={{0,1},{1,0},{2,3},{3,2},{4,5},{5,4},{6,7},{7,6},{8,9},{9,8},{10,11... | collective-permute-start | bytes 1843208 | tf_op jit(solution)/shard_map/ppermute | solution.py:238
  36.9 53.6 %collective-permute-start.1 = (bf16[640,480]{0,1:T(8,128)(2,1)S(1)}, bf16[640,480]{0,1:T(8,128)(2,1)S(1)}, u32[]{:S(2)}, u32[]{:S(2)}) collective-permute-start(bf16[640,480]{0,1:T(8,128)(2,1)S(1)} %copy-done.103), channel_id=1, source_target_pairs={{0,2},{1,3},{2,0},{3,1},{4,6},{5,7},{6,4},{7,5},{8,10},{9,11},{10,... | collective-permute-start | bytes 1843208 | tf_op jit(solution)/shard_map/ppermute | solution.py:238
  50.5 46.9 %collective-permute-start.2 = (bf16[640,480]{0,1:T(8,128)(2,1)}, bf16[640,480]{0,1:T(8,128)(2,1)}, u32[]{:S(2)}, u32[]{:S(2)}) collective-permute-start(bf16[640,480]{0,1:T(8,128)(2,1)} %copy.74), channel_id=1, source_target_pairs={{0,3},{1,2},{2,1},{3,0},{4,7},{5,6},{6,5},{7,4},{8,11},{9,10},{10,... | collective-permute-start | bytes 1843208 | tf_op jit(solution)/shard_map/ppermute | solution.py:238
  244.7 61.7 %collective-permute-start.45 = (bf16[640,896]{1,0:T(8,128)(2,1)}, bf16[640,896]{1,0:T(8,128)(2,1)}, u32[]{:S(2)}, u32[]{:S(2)}) collective-permute-start(bf16[640,896]{1,0:T(8,128)(2,1)} %get-tuple-element.46), channel_id=1, source_target_pairs={{0,1},{1,0},{2,3},{3,2},{4,5},{5,4},{6,7},{7,6},{8,9},{9,8},{10,11... | collective-permute-start | bytes 3440648 | tf_op jit(solution)/shard_map/ppermute | solution.py:238
  254.2 54.0 %collective-permute-start.35 = (bf16[128,2560]{1,0:T(8,128)(2,1)}, bf16[128,2560]{1,0:T(8,128)(2,1)}, u32[]{:S(2)}, u32[]{:S(2)}) collective-permute-start(bf16[128,2560]{1,0:T(8,128)(2,1)} %multiply_convert_fusion.5.refs_0_), channel_id=1, source_target_pairs={{0,1},{1,0},{2,3},{3,2},{4,5},{5,4},{6,7},{7,6},{8,9},{9,8},{10,11... | collective-permute-start | bytes 1966088 | tf_op jit(solution)/shard_map/ppermute | solution.py:238
  265.4 40.7 %collective-permute-start.64 = (bf16[64,2560]{1,0:T(8,128)(2,1)}, bf16[64,2560]{1,0:T(8,128)(2,1)}, u32[]{:S(2)}, u32[]{:S(2)}) collective-permute-start(bf16[64,2560]{1,0:T(8,128)(2,1)} %slice.465), channel_id=1, source_target_pairs={{0,1},{1,0},{2,3},{3,2},{4,5},{5,4},{6,7},{7,6},{8,9},{9,8},{10,11... | collective-permute-start | bytes 983048 | tf_op jit(solution)/shard_map/ppermute | solution.py:238
  271.9 42.3 %collective-permute-start.46 = (bf16[640,896]{1,0:T(8,128)(2,1)}, bf16[640,896]{1,0:T(8,128)(2,1)}, u32[]{:S(2)}, u32[]{:S(2)}) collective-permute-start(bf16[640,896]{1,0:T(8,128)(2,1)} %get-tuple-element.48), channel_id=1, source_target_pairs={{0,2},{1,3},{2,0},{3,1},{4,6},{5,7},{6,4},{7,5},{8,10},{9,11},{10,... | collective-permute-start | bytes 3440648 | tf_op jit(solution)/shard_map/ppermute | solution.py:238
  272.1 59.6 %collective-permute-start.47 = (bf16[640,896]{1,0:T(8,128)(2,1)}, bf16[640,896]{1,0:T(8,128)(2,1)}, u32[]{:S(2)}, u32[]{:S(2)}) collective-permute-start(bf16[640,896]{1,0:T(8,128)(2,1)} %get-tuple-element.50), channel_id=1, source_target_pairs={{0,3},{1,2},{2,1},{3,0},{4,7},{5,6},{6,5},{7,4},{8,11},{9,10},{10,... | collective-permute-start | bytes 3440648 | tf_op jit(solution)/shard_map/ppermute | solution.py:238
  306.2 49.2 %collective-permute-start.42 = (bf16[640,896]{1,0:T(8,128)(2,1)}, bf16[640,896]{1,0:T(8,128)(2,1)}, u32[]{:S(2)}, u32[]{:S(2)}) collective-permute-start(bf16[640,896]{1,0:T(8,128)(2,1)} %get-tuple-element.39), channel_id=1, source_target_pairs={{0,1},{1,0},{2,3},{3,2},{4,5},{5,4},{6,7},{7,6},{8,9},{9,8},{10,11... | collective-permute-start | bytes 3440648 | tf_op jit(solution)/shard_map/ppermute | solution.py:238
  306.4 49.8 %collective-permute-start.43 = (bf16[640,896]{1,0:T(8,128)(2,1)}, bf16[640,896]{1,0:T(8,128)(2,1)}, u32[]{:S(2)}, u32[]{:S(2)}) collective-permute-start(bf16[640,896]{1,0:T(8,128)(2,1)} %get-tuple-element.41), channel_id=1, source_target_pairs={{0,2},{1,3},{2,0},{3,1},{4,6},{5,7},{6,4},{7,5},{8,10},{9,11},{10,... | collective-permute-start | bytes 3440648 | tf_op jit(solution)/shard_map/ppermute | solution.py:238
  308.2 72.3 %collective-permute-start.44 = (bf16[640,896]{1,0:T(8,128)(2,1)}, bf16[640,896]{1,0:T(8,128)(2,1)}, u32[]{:S(2)}, u32[]{:S(2)}) collective-permute-start(bf16[640,896]{1,0:T(8,128)(2,1)} %get-tuple-element.43), channel_id=1, source_target_pairs={{0,3},{1,2},{2,1},{3,0},{4,7},{5,6},{6,5},{7,4},{8,11},{9,10},{10,... | collective-permute-start | bytes 3440648 | tf_op jit(solution)/shard_map/ppermute | solution.py:238
  314.1 84.0 %collective-permute-start.60 = (bf16[128,2560]{1,0:T(8,128)(2,1)}, bf16[128,2560]{1,0:T(8,128)(2,1)S(1)}, u32[]{:S(2)}, u32[]{:S(2)}) collective-permute-start(bf16[128,2560]{1,0:T(8,128)(2,1)} %collective-permute-done.59.refs_2_), channel_id=1, source_target_pairs={{0,4},{4,0},{1,5},{5,1},{2,6},{6,2},{3,7},{7,3},{8,12},{12,8},{9,1... | collective-permute-start | bytes 1966088 | tf_op jit(solution)/shard_map/ppermute | solution.py:238
  331.7 66.5 %collective-permute-start.62 = (bf16[128,2560]{1,0:T(8,128)(2,1)}, bf16[128,2560]{1,0:T(8,128)(2,1)S(1)}, u32[]{:S(2)}, u32[]{:S(2)}) collective-permute-start(bf16[128,2560]{1,0:T(8,128)(2,1)} %collective-permute-done.61.refs_4_), channel_id=1, source_target_pairs={{0,4},{4,0},{1,5},{5,1},{2,6},{6,2},{3,7},{7,3},{8,12},{12,8},{9,1... | collective-permute-start | bytes 1966088 | tf_op jit(solution)/shard_map/ppermute | solution.py:238
  355.4 42.9 %collective-permute-start.65 = (bf16[128,2560]{1,0:T(8,128)(2,1)S(1)}, bf16[128,2560]{1,0:T(8,128)(2,1)S(1)}, u32[]{:S(2)}, u32[]{:S(2)}) collective-permute-start(bf16[128,2560]{1,0:T(8,128)(2,1)S(1)} %constant_dynamic-update-slice_fusion.5.refs_6_), channel_id=1, source_target_pairs={{0,4},{4,0},{1,5},{5,1},{2,6},{6,2},{3,7},{7,3},{8,12},{12,8},{9,1... | collective-permute-start | bytes 1966088 | tf_op jit(solution)/shard_map/ppermute | solution.py:238
  356.2 50.3 %collective-permute-start.37 = (bf16[128,2560]{1,0:T(8,128)(2,1)}, bf16[128,2560]{1,0:T(8,128)(2,1)}, u32[]{:S(2)}, u32[]{:S(2)}) collective-permute-start(bf16[128,2560]{1,0:T(8,128)(2,1)} %multiply_convert_fusion.5.refs_0_), channel_id=1, source_target_pairs={{0,2},{1,3},{2,0},{3,1},{4,6},{5,7},{6,4},{7,5},{8,10},{9,11},{10,... | collective-permute-start | bytes 1966088 | tf_op jit(solution)/shard_map/ppermute | solution.py:238
  529.0 40.2 %collective-permute-start.132 = (bf16[4,160,896]{2,1,0:T(8,128)(2,1)S(1)}, bf16[4,160,896]{2,1,0:T(8,128)(2,1)S(1)}, u32[]{:S(2)}, u32[]{:S(2)}) collective-permute-start(bf16[4,160,896]{2,1,0:T(8,128)(2,1)S(1)} %get-tuple-element.113), channel_id=1, source_target_pairs={{0,8},{1,9},{2,10},{3,11},{4,12},{5,13},{6,14},{7,15}} | collective-permute-start | bytes 3440648 | tf_op jit(solution)/shard_map/ppermute | solution.py:307
  538.6 55.5 %collective-permute-start.151 = (bf16[4,160,896]{2,1,0:T(8,128)(2,1)}, bf16[4,160,896]{2,1,0:T(8,128)(2,1)}, u32[]{:S(2)}, u32[]{:S(2)}) collective-permute-start(bf16[4,160,896]{2,1,0:T(8,128)(2,1)} %get-tuple-element.107), channel_id=1, source_target_pairs={{0,8},{1,9},{2,10},{3,11},{4,12},{5,13},{6,14},{7,15}} | collective-permute-start | bytes 3440648 | tf_op jit(solution)/shard_map/ppermute | solution.py:307
  583.1 48.7 %collective-permute-start.133 = (bf16[4,160,896]{2,1,0:T(8,128)(2,1)}, bf16[4,160,896]{2,1,0:T(8,128)(2,1)}, u32[]{:S(2)}, u32[]{:S(2)}) collective-permute-start(bf16[4,160,896]{2,1,0:T(8,128)(2,1)} %get-tuple-element.111), channel_id=1, source_target_pairs={{0,8},{8,16},{1,9},{9,17},{2,10},{10,18},{3,11},{11,19},{4,12},{12... | collective-permute-start | bytes 3440648 | tf_op jit(solution)/shard_map/ppermute | solution.py:307
  593.4 43.0 %collective-permute-start.136 = (bf16[4,160,896]{2,1,0:T(8,128)(2,1)}, bf16[4,160,896]{2,1,0:T(8,128)(2,1)S(1)}, u32[]{:S(2)}, u32[]{:S(2)}) collective-permute-start(bf16[4,160,896]{2,1,0:T(8,128)(2,1)} %get-tuple-element.112), channel_id=1, source_target_pairs={{16,8},{24,16},{17,9},{25,17},{18,10},{26,18},{19,11},{27,19},{20,... | collective-permute-start | bytes 3440648 | tf_op jit(solution)/shard_map/ppermute | solution.py:308
  599.7 56.5 %collective-permute-start.152 = (bf16[4,160,896]{2,1,0:T(8,128)(2,1)S(1)}, bf16[4,160,896]{2,1,0:T(8,128)(2,1)S(1)}, u32[]{:S(2)}, u32[]{:S(2)}) collective-permute-start(bf16[4,160,896]{2,1,0:T(8,128)(2,1)S(1)} %get-tuple-element.105), channel_id=1, source_target_pairs={{0,8},{8,16},{1,9},{9,17},{2,10},{10,18},{3,11},{11,19},{4,12},{12... | collective-permute-start | bytes 3440648 | tf_op jit(solution)/shard_map/ppermute | solution.py:307
  607.2 49.7 %collective-permute-start.155 = (bf16[4,160,896]{2,1,0:T(8,128)(2,1)S(1)}, bf16[4,160,896]{2,1,0:T(8,128)(2,1)S(1)}, u32[]{:S(2)}, u32[]{:S(2)}) collective-permute-start(bf16[4,160,896]{2,1,0:T(8,128)(2,1)S(1)} %get-tuple-element.106), channel_id=1, source_target_pairs={{16,8},{24,16},{17,9},{25,17},{18,10},{26,18},{19,11},{27,19},{20,... | collective-permute-start | bytes 3440648 | tf_op jit(solution)/shard_map/ppermute | solution.py:308
  628.8 36.1 %collective-permute-start.173 = (bf16[224,2560]{1,0:T(8,128)(2,1)S(1)}, bf16[224,2560]{1,0:T(8,128)(2,1)S(1)}, u32[]{:S(2)}, u32[]{:S(2)}) collective-permute-start(bf16[224,2560]{1,0:T(8,128)(2,1)S(1)} %copy-done.69), channel_id=1, source_target_pairs={{24,16},{25,17},{26,18},{27,19},{28,20},{29,21},{30,22},{31,23}} | collective-permute-start | bytes 3440648 | tf_op jit(solution)/shard_map/ppermute | solution.py:308
  631.8 48.5 %collective-permute-start.171 = (bf16[224,2560]{1,0:T(8,128)(2,1)S(1)}, bf16[224,2560]{1,0:T(8,128)(2,1)S(1)}, u32[]{:S(2)}, u32[]{:S(2)}) collective-permute-start(bf16[224,2560]{1,0:T(8,128)(2,1)S(1)} %fusion.18), channel_id=1, source_target_pairs={{0,8},{8,16},{1,9},{9,17},{2,10},{10,18},{3,11},{11,19},{4,12},{12... | collective-permute-start | bytes 3440648 | tf_op jit(solution)/shard_map/ppermute | solution.py:307
  644.8 38.7 %collective-permute-start.76 = (bf16[128,2560]{1,0:T(8,128)(2,1)S(1)}, bf16[128,2560]{1,0:T(8,128)(2,1)S(1)}, u32[]{:S(2)}, u32[]{:S(2)}) collective-permute-start(bf16[128,2560]{1,0:T(8,128)(2,1)S(1)} %add_convert_fusion.refs_0_), channel_id=1, source_target_pairs={{0,4},{4,0},{1,5},{5,1},{2,6},{6,2},{3,7},{7,3},{8,12},{12,8},{9,1... | collective-permute-start | bytes 1966088 | tf_op jit(solution)/shard_map/ppermute | solution.py:238
  680.3 130.3 %collective-permute-start.137 = (bf16[4,160,896]{2,1,0:T(8,128)(2,1)}, bf16[4,160,896]{2,1,0:T(8,128)(2,1)}, u32[]{:S(2)}, u32[]{:S(2)}) collective-permute-start(bf16[4,160,896]{2,1,0:T(8,128)(2,1)} %get-tuple-element.110), channel_id=1, source_target_pairs={{8,0},{16,8},{24,16},{9,1},{17,9},{25,17},{10,2},{18,10},{26,18},{... | collective-permute-start | bytes 3440648 | tf_op jit(solution)/shard_map/ppermute | solution.py:308
  683.5 128.5 %collective-permute-start.134 = (bf16[4,160,896]{2,1,0:T(8,128)(2,1)}, bf16[4,160,896]{2,1,0:T(8,128)(2,1)}, u32[]{:S(2)}, u32[]{:S(2)}) collective-permute-start(bf16[4,160,896]{2,1,0:T(8,128)(2,1)} %get-tuple-element.109), channel_id=1, source_target_pairs={{0,8},{8,16},{16,24},{1,9},{9,17},{17,25},{2,10},{10,18},{18,26},{... | collective-permute-start | bytes 3440648 | tf_op jit(solution)/shard_map/ppermute | solution.py:307
  753.4 67.1 %collective-permute-start.156 = (bf16[4,160,896]{2,1,0:T(8,128)(2,1)}, bf16[4,160,896]{2,1,0:T(8,128)(2,1)}, u32[]{:S(2)}, u32[]{:S(2)}) collective-permute-start(bf16[4,160,896]{2,1,0:T(8,128)(2,1)} %get-tuple-element.104), channel_id=1, source_target_pairs={{8,0},{16,8},{24,16},{9,1},{17,9},{25,17},{10,2},{18,10},{26,18},{... | collective-permute-start | bytes 3440648 | tf_op jit(solution)/shard_map/ppermute | solution.py:308
  765.9 56.1 %collective-permute-start.153 = (bf16[4,160,896]{2,1,0:T(8,128)(2,1)}, bf16[4,160,896]{2,1,0:T(8,128)(2,1)}, u32[]{:S(2)}, u32[]{:S(2)}) collective-permute-start(bf16[4,160,896]{2,1,0:T(8,128)(2,1)} %get-tuple-element.103), channel_id=1, source_target_pairs={{0,8},{8,16},{16,24},{1,9},{9,17},{17,25},{2,10},{10,18},{18,26},{... | collective-permute-start | bytes 3440648 | tf_op jit(solution)/shard_map/ppermute | solution.py:307
  827.6 46.6 %collective-permute-start.91 = (bf16[128,2560]{1,0:T(8,128)(2,1)}, bf16[128,2560]{1,0:T(8,128)(2,1)S(1)}, u32[]{:S(2)}, u32[]{:S(2)}) collective-permute-start(bf16[128,2560]{1,0:T(8,128)(2,1)} %get-tuple-element.83), channel_id=1, source_target_pairs={{0,4},{4,0},{1,5},{5,1},{2,6},{6,2},{3,7},{7,3},{8,12},{12,8},{9,1... | collective-permute-start | bytes 1966088 | tf_op jit(solution)/shard_map/ppermute | solution.py:238
  834.1 41.7 %collective-permute-start.90 = (bf16[128,2560]{1,0:T(8,128)(2,1)}, bf16[128,2560]{1,0:T(8,128)(2,1)}, u32[]{:S(2)}, u32[]{:S(2)}) collective-permute-start(bf16[128,2560]{1,0:T(8,128)(2,1)} %get-tuple-element.84), channel_id=1, source_target_pairs={{0,4},{4,0},{1,5},{5,1},{2,6},{6,2},{3,7},{7,3},{8,12},{12,8},{9,1... | collective-permute-start | bytes 1966088 | tf_op jit(solution)/shard_map/ppermute | solution.py:238
  834.1 42.3 %collective-permute-start.88 = (bf16[128,2560]{1,0:T(8,128)(2,1)}, bf16[128,2560]{1,0:T(8,128)(2,1)}, u32[]{:S(2)}, u32[]{:S(2)}) collective-permute-start(bf16[128,2560]{1,0:T(8,128)(2,1)} %get-tuple-element.85), channel_id=1, source_target_pairs={{0,4},{4,0},{1,5},{5,1},{2,6},{6,2},{3,7},{7,3},{8,12},{12,8},{9,1... | collective-permute-start | bytes 1966088 | tf_op jit(solution)/shard_map/ppermute | solution.py:238
  838.5 42.2 %collective-permute-start.87 = (bf16[128,2560]{1,0:T(8,128)(2,1)}, bf16[128,2560]{1,0:T(8,128)(2,1)S(1)}, u32[]{:S(2)}, u32[]{:S(2)}) collective-permute-start(bf16[128,2560]{1,0:T(8,128)(2,1)} %get-tuple-element.86), channel_id=1, source_target_pairs={{0,4},{4,0},{1,5},{5,1},{2,6},{6,2},{3,7},{7,3},{8,12},{12,8},{9,1... | collective-permute-start | bytes 1966088 | tf_op jit(solution)/shard_map/ppermute | solution.py:238
  912.0 42.4 %collective-permute-start.175 = (bf16[224,2560]{1,0:T(8,128)(2,1)}, bf16[224,2560]{1,0:T(8,128)(2,1)}, u32[]{:S(2)}, u32[]{:S(2)}) collective-permute-start(bf16[224,2560]{1,0:T(8,128)(2,1)} %fusion.17), channel_id=1, source_target_pairs={{8,0},{16,8},{24,16},{9,1},{17,9},{25,17},{10,2},{18,10},{26,18},{... | collective-permute-start | bytes 3440648 | tf_op jit(solution)/shard_map/ppermute | solution.py:308
  927.6 38.9 %collective-permute-start.142 = (bf16[4,160,896]{2,1,0:T(8,128)(2,1)}, bf16[4,160,896]{2,1,0:T(8,128)(2,1)}, u32[]{:S(2)}, u32[]{:S(2)}) collective-permute-start(bf16[4,160,896]{2,1,0:T(8,128)(2,1)} %shard_map.216.refs_0_), channel_id=1, source_target_pairs={{0,8},{8,16},{16,24},{1,9},{9,17},{17,25},{2,10},{10,18},{18,26},{... | collective-permute-start | bytes 3440648 | tf_op jit(solution)/shard_map/ppermute | solution.py:319
  955.8 49.8 %collective-permute-start.160 = (bf16[4,160,896]{2,1,0:T(8,128)(2,1)S(1)}, bf16[4,160,896]{2,1,0:T(8,128)(2,1)S(1)}, u32[]{:S(2)}, u32[]{:S(2)}) collective-permute-start(bf16[4,160,896]{2,1,0:T(8,128)(2,1)S(1)} %copy-done.28), channel_id=1, source_target_pairs={{0,4},{4,0},{1,5},{5,1},{2,6},{6,2},{3,7},{7,3},{8,12},{12,8},{9,1... | collective-permute-start | bytes 3440648 | tf_op jit(solution)/shard_map/ppermute | solution.py:238
  957.8 53.3 %collective-permute-start.161 = (bf16[4,160,896]{2,1,0:T(8,128)(2,1)S(1)}, bf16[4,160,896]{2,1,0:T(8,128)(2,1)}, u32[]{:S(2)}, u32[]{:S(2)}) collective-permute-start(bf16[4,160,896]{2,1,0:T(8,128)(2,1)S(1)} %copy-done.28), channel_id=1, source_target_pairs={{0,8},{8,16},{16,24},{1,9},{9,17},{17,25},{2,10},{10,18},{18,26},{... | collective-permute-start | bytes 3440648 | tf_op jit(solution)/shard_map/ppermute | solution.py:319
  966.6 38.4 %collective-permute-start.123 = (bf16[80,2560]{1,0:T(8,128)(2,1)S(1)}, bf16[80,2560]{1,0:T(8,128)(2,1)S(1)}, u32[]{:S(2)}, u32[]{:S(2)}) collective-permute-start(bf16[80,2560]{1,0:T(8,128)(2,1)S(1)} %fusion.94.refs_0_), channel_id=1, source_target_pairs={{0,8},{8,16},{16,24},{1,9},{9,17},{17,25},{2,10},{10,18},{18,26},{... | collective-permute-start | bytes 1228808 | tf_op jit(solution)/shard_map/ppermute | solution.py:319
  1011.2 45.6 %collective-permute-start.162 = (bf16[4,160,896]{2,1,0:T(8,128)(2,1)S(1)}, bf16[4,160,896]{2,1,0:T(8,128)(2,1)}, u32[]{:S(2)}, u32[]{:S(2)}) collective-permute-start(bf16[4,160,896]{2,1,0:T(8,128)(2,1)S(1)} %copy-done.28), channel_id=1, source_target_pairs={{8,0},{16,8},{24,16},{9,1},{17,9},{25,17},{10,2},{18,10},{26,18},{... | collective-permute-start | bytes 3440648 | tf_op jit(solution)/shard_map/ppermute | solution.py:320
  1013.7 44.5 %collective-permute-start.177 = (bf16[224,2560]{1,0:T(8,128)(2,1)}, bf16[224,2560]{1,0:T(8,128)(2,1)S(1)}, u32[]{:S(2)}, u32[]{:S(2)}) collective-permute-start(bf16[224,2560]{1,0:T(8,128)(2,1)} %fusion.21.refs_0_), channel_id=1, source_target_pairs={{0,8},{8,16},{16,24},{1,9},{9,17},{17,25},{2,10},{10,18},{18,26},{... | collective-permute-start | bytes 3440648 | tf_op jit(solution)/shard_map/ppermute | solution.py:319
  1022.0 36.1 %collective-permute-start.122 = (bf16[80,2560]{1,0:T(8,128)(2,1)S(1)}, bf16[80,2560]{1,0:T(8,128)(2,1)S(1)}, u32[]{:S(2)}, u32[]{:S(2)}) collective-permute-start(bf16[80,2560]{1,0:T(8,128)(2,1)S(1)} %fusion.94.refs_0_), channel_id=1, source_target_pairs={{0,4},{4,0},{1,5},{5,1},{2,6},{6,2},{3,7},{7,3},{8,12},{12,8},{9,1... | collective-permute-start | bytes 1228808 | tf_op jit(solution)/shard_map/ppermute | solution.py:238
  1022.1 69.2 %collective-permute-start.178 = (bf16[224,2560]{1,0:T(8,128)(2,1)}, bf16[224,2560]{1,0:T(8,128)(2,1)S(1)}, u32[]{:S(2)}, u32[]{:S(2)}) collective-permute-start(bf16[224,2560]{1,0:T(8,128)(2,1)} %fusion.21.refs_0_), channel_id=1, source_target_pairs={{8,0},{16,8},{24,16},{9,1},{17,9},{25,17},{10,2},{18,10},{26,18},{... | collective-permute-start | bytes 3440648 | tf_op jit(solution)/shard_map/ppermute | solution.py:320
  1032.1 57.9 %collective-permute-start.126 = (bf16[80,2560]{1,0:T(8,128)(2,1)S(1)}, bf16[80,2560]{1,0:T(8,128)(2,1)S(1)}, u32[]{:S(2)}, u32[]{:S(2)}) collective-permute-start(bf16[80,2560]{1,0:T(8,128)(2,1)S(1)} %collective-permute-done.125), channel_id=1, source_target_pairs={{8,0},{9,1},{10,2},{11,3},{12,4},{13,5},{14,6},{15,7}} | collective-permute-start | bytes 1228808 | tf_op jit(solution)/shard_map/ppermute | solution.py:320
  1056.8 57.8 %collective-permute-start.144 = (bf16[4,160,896]{2,1,0:T(8,128)(2,1)S(1)}, bf16[4,160,896]{2,1,0:T(8,128)(2,1)S(1)}, u32[]{:S(2)}, u32[]{:S(2)}) collective-permute-start(bf16[4,160,896]{2,1,0:T(8,128)(2,1)S(1)} %collective-permute-done.143), channel_id=1, source_target_pairs={{8,0},{16,8},{9,1},{17,9},{10,2},{18,10},{11,3},{19,11},{12,4},{20... | collective-permute-start | bytes 3440648 | tf_op jit(solution)/shard_map/ppermute | solution.py:320
  1058.2 36.1 %collective-permute-start.130 = (bf16[80,2560]{1,0:T(8,128)(2,1)S(1)}, bf16[80,2560]{1,0:T(8,128)(2,1)S(1)}, u32[]{:S(2)}, u32[]{:S(2)}) collective-permute-start(bf16[80,2560]{1,0:T(8,128)(2,1)S(1)} %collective-permute-done.128), channel_id=1, source_target_pairs={{16,24},{17,25},{18,26},{19,27},{20,28},{21,29},{22,30},{23,31}} | collective-permute-start | bytes 1228808 | tf_op jit(solution)/shard_map/ppermute | solution.py:319
  1093.0 41.5 %collective-permute-start.163 = (bf16[4,160,896]{2,1,0:T(8,128)(2,1)}, bf16[4,160,896]{2,1,0:T(8,128)(2,1)}, u32[]{:S(2)}, u32[]{:S(2)}) collective-permute-start(bf16[4,160,896]{2,1,0:T(8,128)(2,1)} %collective-permute-done.162), channel_id=1, source_target_pairs={{8,0},{16,8},{9,1},{17,9},{10,2},{18,10},{11,3},{19,11},{12,4},{20... | collective-permute-start | bytes 3440648 | tf_op jit(solution)/shard_map/ppermute | solution.py:320
  1099.7 36.2 %collective-permute-start.166 = (bf16[4,160,896]{2,1,0:T(8,128)(2,1)}, bf16[4,160,896]{2,1,0:T(8,128)(2,1)}, u32[]{:S(2)}, u32[]{:S(2)}) collective-permute-start(bf16[4,160,896]{2,1,0:T(8,128)(2,1)} %collective-permute-done.161), channel_id=1, source_target_pairs={{8,16},{16,24},{9,17},{17,25},{10,18},{18,26},{11,19},{19,27},{12,... | collective-permute-start | bytes 3440648 | tf_op jit(solution)/shard_map/ppermute | solution.py:319
  1101.6 36.7 %collective-permute-start.127 = (bf16[80,2560]{1,0:T(8,128)(2,1)S(1)}, bf16[80,2560]{1,0:T(8,128)(2,1)S(1)}, u32[]{:S(2)}, u32[]{:S(2)}) collective-permute-start(bf16[80,2560]{1,0:T(8,128)(2,1)S(1)} %broadcast_select_fusion.14.refs_2_), channel_id=1, source_target_pairs={{0,4},{4,0},{1,5},{5,1},{2,6},{6,2},{3,7},{7,3},{8,12},{12,8},{9,1... | collective-permute-start | bytes 1228808 | tf_op jit(solution)/shard_map/ppermute | solution.py:238
  1137.0 41.8 %collective-permute-start.179 = (bf16[224,2560]{1,0:T(8,128)(2,1)S(1)}, bf16[224,2560]{1,0:T(8,128)(2,1)S(1)}, u32[]{:S(2)}, u32[]{:S(2)}) collective-permute-start(bf16[224,2560]{1,0:T(8,128)(2,1)S(1)} %copy-done.77), channel_id=1, source_target_pairs={{8,0},{16,8},{9,1},{17,9},{10,2},{18,10},{11,3},{19,11},{12,4},{20... | collective-permute-start | bytes 3440648 | tf_op jit(solution)/shard_map/ppermute | solution.py:320
  1138.4 40.5 %collective-permute-start.182 = (bf16[224,2560]{1,0:T(8,128)(2,1)S(1)}, bf16[224,2560]{1,0:T(8,128)(2,1)S(1)}, u32[]{:S(2)}, u32[]{:S(2)}) collective-permute-start(bf16[224,2560]{1,0:T(8,128)(2,1)S(1)} %copy-done.75), channel_id=1, source_target_pairs={{8,16},{16,24},{9,17},{17,25},{10,18},{18,26},{11,19},{19,27},{12,... | collective-permute-start | bytes 3440648 | tf_op jit(solution)/shard_map/ppermute | solution.py:319
  1139.1 74.7 %collective-permute-start.145 = (bf16[4,160,896]{2,1,0:T(8,128)(2,1)S(1)}, bf16[4,160,896]{2,1,0:T(8,128)(2,1)S(1)}, u32[]{:S(2)}, u32[]{:S(2)}) collective-permute-start(bf16[4,160,896]{2,1,0:T(8,128)(2,1)S(1)} %copy-done.79), channel_id=1, source_target_pairs={{8,0},{9,1},{10,2},{11,3},{12,4},{13,5},{14,6},{15,7}} | collective-permute-start | bytes 3440648 | tf_op jit(solution)/shard_map/ppermute | solution.py:320
  1154.3 57.6 %collective-permute-start.109 = (bf16[4,160,480]{2,1,0:T(8,128)(2,1)S(1)}, bf16[4,160,480]{2,1,0:T(8,128)(2,1)S(1)}, u32[]{:S(2)}, u32[]{:S(2)}) collective-permute-start(bf16[4,160,480]{2,1,0:T(8,128)(2,1)S(1)} %collective-permute-done.108), channel_id=1, source_target_pairs={{8,0},{16,8},{9,1},{17,9},{10,2},{18,10},{11,3},{19,11},{12,4},{20... | collective-permute-start | bytes 1843208 | tf_op jit(solution)/shard_map/ppermute | solution.py:320
  1155.6 57.0 %collective-permute-start.112 = (bf16[4,160,480]{2,1,0:T(8,128)(2,1)S(1)}, bf16[4,160,480]{2,1,0:T(8,128)(2,1)S(1)}, u32[]{:S(2)}, u32[]{:S(2)}) collective-permute-start(bf16[4,160,480]{2,1,0:T(8,128)(2,1)S(1)} %collective-permute-done.107), channel_id=1, source_target_pairs={{8,16},{16,24},{9,17},{17,25},{10,18},{18,26},{11,19},{19,27},{12,... | collective-permute-start | bytes 1843208 | tf_op jit(solution)/shard_map/ppermute | solution.py:319
  1178.8 37.2 %collective-permute-start.106 = (bf16[4,160,480]{2,1,0:T(8,128)(2,1)S(1)}, bf16[4,160,480]{2,1,0:T(8,128)(2,1)S(1)}, u32[]{:S(2)}, u32[]{:S(2)}) collective-permute-start(bf16[4,160,480]{2,1,0:T(8,128)(2,1)S(1)} %copy-done.44), channel_id=1, source_target_pairs={{0,4},{4,0},{1,5},{5,1},{2,6},{6,2},{3,7},{7,3},{8,12},{12,8},{9,1... | collective-permute-start | bytes 1843208 | tf_op jit(solution)/shard_map/ppermute | solution.py:238
  1178.8 38.0 %collective-permute-start.148 = (bf16[4,160,896]{2,1,0:T(8,128)(2,1)S(1)}, bf16[4,160,896]{2,1,0:T(8,128)(2,1)S(1)}, u32[]{:S(2)}, u32[]{:S(2)}) collective-permute-start(bf16[4,160,896]{2,1,0:T(8,128)(2,1)S(1)} %broadcast_select_fusion.6.refs_4_), channel_id=1, source_target_pairs={{0,4},{4,0},{1,5},{5,1},{2,6},{6,2},{3,7},{7,3},{8,12},{12,8},{9,1... | collective-permute-start | bytes 3440648 | tf_op jit(solution)/shard_map/ppermute | solution.py:238
  1216.0 62.1 %collective-permute-start.167 = (bf16[4,160,896]{2,1,0:T(8,128)(2,1)S(1)}, bf16[4,160,896]{2,1,0:T(8,128)(2,1)S(1)}, u32[]{:S(2)}, u32[]{:S(2)}) collective-permute-start(bf16[4,160,896]{2,1,0:T(8,128)(2,1)S(1)} %broadcast_select_fusion.5.refs_4_), channel_id=1, source_target_pairs={{0,4},{4,0},{1,5},{5,1},{2,6},{6,2},{3,7},{7,3},{8,12},{12,8},{9,1... | collective-permute-start | bytes 3440648 | tf_op jit(solution)/shard_map/ppermute | solution.py:238
  1216.9 62.0 %collective-permute-start.180 = (bf16[224,2560]{1,0:T(8,128)(2,1)S(1)}, bf16[224,2560]{1,0:T(8,128)(2,1)S(1)}, u32[]{:S(2)}, u32[]{:S(2)}) collective-permute-start(bf16[224,2560]{1,0:T(8,128)(2,1)S(1)} %collective-permute-done.179), channel_id=1, source_target_pairs={{8,0},{9,1},{10,2},{11,3},{12,4},{13,5},{14,6},{15,7}} | collective-permute-start | bytes 3440648 | tf_op jit(solution)/shard_map/ppermute | solution.py:320
  1218.3 56.6 %collective-permute-start.110 = (bf16[4,160,480]{2,1,0:T(8,128)(2,1)S(1)}, bf16[4,160,480]{2,1,0:T(8,128)(2,1)S(1)}, u32[]{:S(2)}, u32[]{:S(2)}) collective-permute-start(bf16[4,160,480]{2,1,0:T(8,128)(2,1)S(1)} %collective-permute-done.109), channel_id=1, source_target_pairs={{8,0},{9,1},{10,2},{11,3},{12,4},{13,5},{14,6},{15,7}} | collective-permute-start | bytes 1843208 | tf_op jit(solution)/shard_map/ppermute | solution.py:320
  1242.9 35.8 %collective-permute-start.114 = (bf16[4,160,480]{2,1,0:T(8,128)(2,1)S(1)}, bf16[4,160,480]{2,1,0:T(8,128)(2,1)S(1)}, u32[]{:S(2)}, u32[]{:S(2)}) collective-permute-start(bf16[4,160,480]{2,1,0:T(8,128)(2,1)S(1)} %collective-permute-done.112), channel_id=1, source_target_pairs={{16,24},{17,25},{18,26},{19,27},{20,28},{21,29},{22,30},{23,31}} | collective-permute-start | bytes 1843208 | tf_op jit(solution)/shard_map/ppermute | solution.py:319
  1280.5 51.0 %collective-permute-start.111 = (bf16[4,160,480]{2,1,0:T(8,128)(2,1)}, bf16[4,160,480]{2,1,0:T(8,128)(2,1)}, u32[]{:S(2)}, u32[]{:S(2)}) collective-permute-start(bf16[4,160,480]{2,1,0:T(8,128)(2,1)} %broadcast_select_fusion.11.refs_2_), channel_id=1, source_target_pairs={{0,4},{4,0},{1,5},{5,1},{2,6},{6,2},{3,7},{7,3},{8,12},{12,8},{9,1... | collective-permute-start | bytes 1843208 | tf_op jit(solution)/shard_map/ppermute | solution.py:238
  1281.7 92.2 %collective-permute-start.176 = (bf16[224,2560]{1,0:T(8,128)(2,1)}, bf16[224,2560]{1,0:T(8,128)(2,1)}, u32[]{:S(2)}, u32[]{:S(2)}) collective-permute-start(bf16[224,2560]{1,0:T(8,128)(2,1)} %fusion.21.refs_0_), channel_id=1, source_target_pairs={{0,4},{4,0},{1,5},{5,1},{2,6},{6,2},{3,7},{7,3},{8,12},{12,8},{9,1... | collective-permute-start | bytes 3440648 | tf_op jit(solution)/shard_map/ppermute | solution.py:238
  1282.7 91.3 %collective-permute-start.183 = (bf16[224,2560]{1,0:T(8,128)(2,1)}, bf16[224,2560]{1,0:T(8,128)(2,1)}, u32[]{:S(2)}, u32[]{:S(2)}) collective-permute-start(bf16[224,2560]{1,0:T(8,128)(2,1)} %broadcast_select_fusion.1.refs_4_), channel_id=1, source_target_pairs={{0,4},{4,0},{1,5},{5,1},{2,6},{6,2},{3,7},{7,3},{8,12},{12,8},{9,1... | collective-permute-start | bytes 3440648 | tf_op jit(solution)/shard_map/ppermute | solution.py:238
  1286.4 87.6 %collective-permute-start.181 = (bf16[224,2560]{1,0:T(8,128)(2,1)}, bf16[224,2560]{1,0:T(8,128)(2,1)}, u32[]{:S(2)}, u32[]{:S(2)}) collective-permute-start(bf16[224,2560]{1,0:T(8,128)(2,1)} %broadcast_select_fusion.2.refs_2_), channel_id=1, source_target_pairs={{0,4},{4,0},{1,5},{5,1},{2,6},{6,2},{3,7},{7,3},{8,12},{12,8},{9,1... | collective-permute-start | bytes 3440648 | tf_op jit(solution)/shard_map/ppermute | solution.py:238
  1289.2 84.7 %collective-permute-start.185 = (bf16[224,2560]{1,0:T(8,128)(2,1)}, bf16[224,2560]{1,0:T(8,128)(2,1)}, u32[]{:S(2)}, u32[]{:S(2)}) collective-permute-start(bf16[224,2560]{1,0:T(8,128)(2,1)} %broadcast_select_fusion.refs_6_), channel_id=1, source_target_pairs={{0,4},{4,0},{1,5},{5,1},{2,6},{6,2},{3,7},{7,3},{8,12},{12,8},{9,1... | collective-permute-start | bytes 3440648 | tf_op jit(solution)/shard_map/ppermute | solution.py:238
  (287 other events, 5172.4 us)

commit v2 on v1

v2 whole, which is shorter than its diff:
```python
import jax
import jax.numpy as jnp
import numpy as np
from jax import lax
from jax.experimental import pallas as pl
from jax.experimental.pallas import tpu as pltpu
from jax.sharding import Mesh
from jax.sharding import PartitionSpec as P

QUERY_HEADS = 32
KEY_VALUE_HEADS = 8
HEAD_SIZE = 80

EPS = 1e-05
THETA = 1000000.0
NEGATIVE_LARGE = -1e30

F32 = jnp.float32
BF16 = jnp.bfloat16

ANY = pl.BlockSpec(memory_space=pl.ANY)
PARAMS = pltpu.CompilerParams(vmem_limit_bytes=56 * 1024 * 1024)


class Order:
    def __init__(self):
        self.last = ()

    def pin(self, *arrays):
        return lax.optimization_barrier(arrays + self.last)[: len(arrays)]

    def region(self, function, *arrays):
        results = function(*self.pin(*arrays))
        single = not isinstance(results, (tuple, list))
        self.last = (results,) if single else tuple(results)
        return results


def scalars(*values):
    return jnp.stack([jnp.asarray(v, jnp.int32) for v in values])


def moved(*arrays):
    return pl.CostEstimate(
        flops=0, transcendentals=0, bytes_accessed=2 * sum(a.size * a.dtype.itemsize for a in arrays)
    )


def whole(shape):
    return pl.BlockSpec(shape, lambda *_: (0,) * len(shape))


def blank(shape, dtype):
    return pl.pallas_call(
        lambda out: None, out_shape=jax.ShapeDtypeStruct(shape, dtype), out_specs=ANY
    )()


def swap(value, axis, offset):
    size = lax.axis_size(axis)
    return lax.ppermute(value, axis, [(i, i ^ offset) for i in range(size)])


def pack_qkv(w_query, w_key, w_value, core, n_f, n_c):
    rows = w_query.shape[0]
    n_t = n_f * n_c
    q, kv = w_query.shape[1] // n_t, w_key.shape[1] // n_t

    def body(where, wq, wk, wv, out):
        for c in range(n_c):

            @pl.when(where[0] == c)
            def _(c=c):
                for f in range(n_f):
                    t = f * n_c + c
                    out[f, :, :q] = wq[:, t * q : (t + 1) * q]
                    out[f, :, q : q + kv] = wk[:, t * kv : (t + 1) * kv]
                    out[f, :, q + kv :] = wv[:, t * kv : (t + 1) * kv]

    block = rows // 4
    return pl.pallas_call(
        body,
        out_shape=jax.ShapeDtypeStruct((n_f, rows, q + 2 * kv), BF16),
        grid_spec=pltpu.PrefetchScalarGridSpec(
            num_scalar_prefetch=1,
            grid=(4,),
            in_specs=[
                pl.BlockSpec((block, w.shape[1]), lambda i, where: (i, 0))
                for w in (w_query, w_key, w_value)
            ],
            out_specs=pl.BlockSpec((n_f, block, q + 2 * kv), lambda i, where: (0, i, 0)),
        ),
        compiler_params=PARAMS,
        cost_estimate=moved(w_query),
    )(scalars(core), w_query, w_key, w_value)


def slice_columns(weight, core, n_f, n_c):
    rows, size = weight.shape[0], weight.shape[1] // (n_f * n_c)

    def body(where, source, out):
        out[0] = source[...]

    return pl.pallas_call(
        body,
        out_shape=jax.ShapeDtypeStruct((n_f, rows, size), weight.dtype),
        grid_spec=pltpu.PrefetchScalarGridSpec(
            num_scalar_prefetch=1,
            grid=(n_f,),
            in_specs=[pl.BlockSpec((rows, size), lambda i, where: (0, i * n_c + where[0]))],
            out_specs=pl.BlockSpec((1, rows, size), lambda i, where: (i, 0, 0)),
        ),
        compiler_params=PARAMS,
        cost_estimate=moved(weight),
    )(scalars(core), weight)


EXTRA = 32
DIGIT = 64


def payload(x, starts, gain_one, gain_two):
    rows, width = x.shape

    def body(x, starts, one, two, out):
        out[:rows] = x[...]
        out[rows : rows + EXTRA] = jnp.zeros((EXTRA, width), BF16)
        low = (starts[...] & (DIGIT - 1)).astype(F32)
        high = (starts[...] // DIGIT).astype(F32)
        for row, value in enumerate((low, high, one[...].astype(F32), two[...].astype(F32))):
            out[rows + row : rows + row + 1, : value.shape[1]] = value.astype(BF16)

    return pl.pallas_call(
        body,
        out_shape=jax.ShapeDtypeStruct((rows + EXTRA, width), BF16),
        compiler_params=PARAMS,
        cost_estimate=moved(x),
    )(x, starts, gain_one, gain_two)


def project_first(payloads, gains, w_qkv, z, n_z, n_c, block_len):
    width, columns = w_qkv.shape
    rows = 2 * block_len
    count = payloads.shape[0] // (rows + EXTRA)
    half = HEAD_SIZE // 2
    q_width = columns - 2 * HEAD_SIZE
    inv_freq = THETA ** (-(jnp.arange(half, dtype=F32) * 2.0) / HEAD_SIZE)

    def body(where, block, gain, w, freq, h_out, q_out, kv_out, cos_out, sin_out, st_out):
        x = block[:rows].astype(F32)
        inverse = lax.rsqrt(jnp.mean(x * x, axis=-1, keepdims=True) + EPS)
        h_out[...] = (x * inverse * gain[0:1]).astype(BF16)
        low, high = block[rows : rows + 1, :rows], block[rows + 1 : rows + 2, :rows]
        start = (low.astype(F32) + high.astype(F32) * DIGIT).astype(jnp.int32)
        st_out[0] = start
        device = where[0] * n_c + lax.rem(pl.program_id(0), n_c)
        within = lax.broadcasted_iota(jnp.int32, (1, rows), 1)
        position = jnp.where(
            within < block_len,
            device * block_len + within,
            (2 * n_z * n_c - 1 - device) * block_len + within - block_len,
        )
        angles = freq[...] * (position - start).astype(F32)
        cosine, sine = jnp.cos(angles), jnp.sin(angles)
        cos_out[...] = cosine
        sin_out[...] = sine
        projected = nn(h_out[...], w[...]).T

        def turned(row):
            a, b = projected[row : row + half], projected[row + half : row + HEAD_SIZE]
            return jnp.concatenate([a * cosine - b * sine, b * cosine + a * sine], axis=0)

        for row in range(0, q_width, HEAD_SIZE):
            q_out[row : row + HEAD_SIZE] = (turned(row) * HEAD_SIZE ** (-0.5)).astype(BF16)
        kv_out[:HEAD_SIZE] = turned(q_width).astype(BF16)
        kv_out[HEAD_SIZE:] = projected[q_width + HEAD_SIZE :].astype(BF16)

    tokens = count * rows

    def lanes(size):
        return pl.BlockSpec((size, rows), lambda g, where: (0, g))

    return pl.pallas_call(
        body,
        out_shape=[
            jax.ShapeDtypeStruct((tokens, width), BF16),
            jax.ShapeDtypeStruct((q_width, tokens), BF16),
            jax.ShapeDtypeStruct((2 * HEAD_SIZE, tokens), BF16),
            jax.ShapeDtypeStruct((half, tokens), F32),
            jax.ShapeDtypeStruct((half, tokens), F32),
            jax.ShapeDtypeStruct((count, 1, rows), jnp.int32),
        ],
        grid_spec=pltpu.PrefetchScalarGridSpec(
            num_scalar_prefetch=1,
            grid=(count,),
            in_specs=[
                pl.BlockSpec((rows + EXTRA, width), lambda g, where: (g, 0)),
                whole(gains.shape),
                whole(w_qkv.shape),
                whole((half, 1)),
            ],
            out_specs=[
                pl.BlockSpec((rows, width), lambda g, where: (g, 0)),
                lanes(q_width),
                lanes(2 * HEAD_SIZE),
                lanes(half),
                lanes(half),
                pl.BlockSpec((1, 1, rows), lambda g, where: (g, 0, 0)),
            ],
        ),
        compiler_params=PARAMS,
        cost_estimate=pl.CostEstimate(
            flops=2 * tokens * width * columns,
            transcendentals=tokens * HEAD_SIZE,
            bytes_accessed=4 * tokens * width,
        ),
    )(scalars(z), payloads, gains, w_qkv, inv_freq[:, None])


def tn(a, b):
    return lax.dot_general(a, b, (((0,), (0,)), ((), ())), preferred_element_type=F32)


def nt(a, b):
    return lax.dot_general(a, b, (((1,), (1,)), ((), ())), preferred_element_type=F32)


def nn(a, b):
    return lax.dot_general(a, b, (((1,), (0,)), ((), ())), preferred_element_type=F32)


def visible_rows(k_pos, q_pos, starts):
    return (k_pos >= starts) & (k_pos <= q_pos)


def attention(query, key_values, k_pos, q_pos, starts, n_f):
    width, tokens = query.shape
    heads, span, n_z = width // HEAD_SIZE, tokens // n_f, len(key_values)

    def body(*refs):
        q, kvs = refs[0], refs[1 : 1 + n_z]
        kp, qp, st, out, low, lse = refs[1 + n_z :]
        keys = jnp.concatenate([kv[:HEAD_SIZE] for kv in kvs], axis=1)
        values = jnp.concatenate([kv[HEAD_SIZE:] for kv in kvs], axis=1)
        seen = visible_rows(kp[...], qp[...], st[0])
        for h in range(heads):
            part = slice(h * HEAD_SIZE, (h + 1) * HEAD_SIZE)
            scores = jnp.where(seen, tn(keys, q[part]), NEGATIVE_LARGE)
            top = jnp.max(scores, axis=0, keepdims=True)
            terms = jnp.exp(scores - top)
            total = jnp.sum(terms, axis=0, keepdims=True)
            result = nn(values, terms.astype(BF16)) / total
            out[part] = result
            low[part] = result.astype(BF16)
            lse[0, h : h + 1] = top + jnp.log(total)

    return pl.pallas_call(
        body,
        out_shape=[
            jax.ShapeDtypeStruct((width, tokens), F32),
            jax.ShapeDtypeStruct((width, tokens), BF16),
            jax.ShapeDtypeStruct((n_f, heads, span), F32),
        ],
        grid=(n_f,),
        in_specs=[pl.BlockSpec((width, span), lambda i: (0, i))]
        + [pl.BlockSpec((2 * HEAD_SIZE, span), lambda i: (0, i))] * n_z
        + [
            whole(k_pos.shape),
            whole(q_pos.shape),
            pl.BlockSpec((1, 1, span), lambda i: (i, 0, 0)),
        ],
        out_specs=[
            pl.BlockSpec((width, span), lambda i: (0, i)),
            pl.BlockSpec((width, span), lambda i: (0, i)),
            pl.BlockSpec((1, heads, span), lambda i: (i, 0, 0)),
        ],
        compiler_params=PARAMS,
        cost_estimate=pl.CostEstimate(
            flops=4 * width * tokens * span * n_z,
            transcendentals=heads * tokens * span * n_z,
            bytes_accessed=8 * width * tokens,
        ),
    )(query, *key_values, k_pos, q_pos, starts)


def attention_back(query, key_values, grad, out, lse, k_pos, q_pos, starts, n_f, z_order):
    width, tokens = query.shape
    heads, span, n_z = width // HEAD_SIZE, tokens // n_f, len(key_values)

    def body(where, *refs):
        q, kvs = refs[0], refs[1 : 1 + n_z]
        do, o, l, kp, qp, st, dq = refs[1 + n_z : 8 + n_z]
        dkv = refs[8 + n_z]
        keys = jnp.concatenate([kv[:HEAD_SIZE] for kv in kvs], axis=1)
        values = jnp.concatenate([kv[HEAD_SIZE:] for kv in kvs], axis=1)
        seen = visible_rows(kp[...], qp[...], st[0])
        grad_keys = jnp.zeros((HEAD_SIZE, n_z * span), F32)
        grad_values = jnp.zeros((HEAD_SIZE, n_z * span), F32)
        for h in range(heads):
            part = slice(h * HEAD_SIZE, (h + 1) * HEAD_SIZE)
            scores = jnp.where(seen, tn(keys, q[part]), NEGATIVE_LARGE)
            probs = jnp.exp(scores - l[0, h : h + 1])
            delta = jnp.sum(do[part].astype(F32) * o[part], axis=0, keepdims=True)
            grad_values += nt(do[part], probs.astype(BF16))
            grad_scores = (probs * (tn(values, do[part]) - delta)).astype(BF16)
            dq[part] = nn(keys, grad_scores)
            grad_keys += nt(q[part], grad_scores)
        for s in range(n_z):
            here = slice(s * span, (s + 1) * span)
            dkv[where[s], :HEAD_SIZE] = grad_keys[:, here].astype(BF16)
            dkv[where[s], HEAD_SIZE:] = grad_values[:, here].astype(BF16)

    wide = pl.BlockSpec((width, span), lambda i, where: (0, i))
    narrow = pl.BlockSpec((2 * HEAD_SIZE, span), lambda i, where: (0, i))
    return pl.pallas_call(
        body,
        out_shape=[
            jax.ShapeDtypeStruct((width, tokens), F32),
            jax.ShapeDtypeStruct((n_z, 2 * HEAD_SIZE, tokens), BF16),
        ],
        grid_spec=pltpu.PrefetchScalarGridSpec(
            num_scalar_prefetch=1,
            grid=(n_f,),
            in_specs=[wide]
            + [narrow] * n_z
            + [
                wide,
                wide,
                pl.BlockSpec((1, heads, span), lambda i, where: (i, 0, 0)),
                whole(k_pos.shape),
                whole(q_pos.shape),
                pl.BlockSpec((1, 1, span), lambda i, where: (i, 0, 0)),
            ],
            out_specs=[
                wide,
                pl.BlockSpec((n_z, 2 * HEAD_SIZE, span), lambda i, where: (0, 0, i)),
            ],
        ),
        compiler_params=PARAMS,
        cost_estimate=pl.CostEstimate(
            flops=10 * width * tokens * span * n_z,
            transcendentals=heads * tokens * span * n_z,
            bytes_accessed=12 * width * tokens,
        ),
    )(scalars(*z_order), query, *key_values, grad, out, lse, k_pos, q_pos, starts)


def collect(own, ups, downs, z):
    shape = own.shape
    n_z = len(ups) + 1
    zeros = (0,) * len(shape)

    def body(where, *refs):
        out = refs[2 * n_z - 1]
        k = pl.program_id(0)

        @pl.when(k == where[0])
        def _():
            out[0] = refs[0][...]

        for s in range(1, n_z):

            @pl.when(where[0] - k == s)
            def _(s=s):
                out[0] = refs[s][...]

            @pl.when(k - where[0] == s)
            def _(s=s):
                out[0] = refs[n_z - 1 + s][...]

    return pl.pallas_call(
        body,
        out_shape=jax.ShapeDtypeStruct((n_z,) + shape, own.dtype),
        grid_spec=pltpu.PrefetchScalarGridSpec(
            num_scalar_prefetch=1,
            grid=(n_z,),
            in_specs=[whole(shape)] * (2 * n_z - 1),
            out_specs=pl.BlockSpec((1,) + shape, lambda g, where: (g,) + zeros),
        ),
        compiler_params=PARAMS,
        cost_estimate=moved(*[own] * n_z),
    )(scalars(z), own, *ups, *downs)


def assemble(cores, core, splits):
    n_c = len(cores)
    n_z, n_f, rows, columns = cores[0].shape
    n_t = n_f * n_c

    def body(where, *refs):
        outs = refs[n_c:]
        for own in range(n_c):

            @pl.when(where[0] == own)
            def _(own=own):
                for e in range(n_c):
                    for i in range(n_f):
                        t = i * n_c + (own ^ e)
                        part = refs[e][0, i].astype(F32)
                        for out, (low, high) in zip(outs, splits, strict=True):
                            size = high - low
                            out[:, t * size : (t + 1) * size] = part[:, low:high]

    return pl.pallas_call(
        body,
        out_shape=[
            jax.ShapeDtypeStruct((n_z * rows, n_t * (high - low)), F32) for low, high in splits
        ],
        grid_spec=pltpu.PrefetchScalarGridSpec(
            num_scalar_prefetch=1,
            grid=(n_z,),
            in_specs=[
                pl.BlockSpec((1, n_f, rows, columns), lambda g, where: (g, 0, 0, 0))
                for _ in cores
            ],
            out_specs=[
                pl.BlockSpec((rows, n_t * (high - low)), lambda g, where: (g, 0))
                for low, high in splits
            ],
        ),
        compiler_params=PARAMS,
        cost_estimate=moved(*cores),
    )(scalars(core), *cores)


def assemble_rows(cores, core):
    n_c = len(cores)
    n_z, rows, columns = cores[0].shape

    def body(where, *refs):
        for e in range(n_c):

            @pl.when(pl.program_id(0) == e)
            def _(e=e):
                refs[n_c][...] = refs[e][0].astype(F32)

    def in_map(e):
        return lambda g, k, where: (jnp.clip(k + (g - e) * n_z, 0, n_z - 1), 0, 0)

    return pl.pallas_call(
        body,
        out_shape=jax.ShapeDtypeStruct((n_c * n_z * rows, columns), F32),
        grid_spec=pltpu.PrefetchScalarGridSpec(
            num_scalar_prefetch=1,
            grid=(n_c, n_z),
            in_specs=[pl.BlockSpec((1, rows, columns), in_map(e)) for e in range(n_c)],
            out_specs=pl.BlockSpec(
                (rows, columns), lambda g, k, where: ((where[0] ^ g) * n_z + k, 0)
            ),
        ),
        compiler_params=PARAMS,
        cost_estimate=moved(*cores),
    )(scalars(core), *cores)


def turn_along_z(own):
    n_z = lax.axis_size("z")
    return [own] + [
        lax.ppermute(own, "z", [(i, (i + s) % n_z) for i in range(n_z)]) for s in range(1, n_z)
    ]


def after(value, *earlier):
    return lax.optimization_barrier((value,) + earlier)[0]


class ZSum:
    def __init__(self, parts, z_axis, between=None):
        self.parts, self.z_axis, self.between = parts, z_axis, between
        self.n_z, self.z = lax.axis_size("z"), lax.axis_index("z")
        self.up = self.down = None

    def chunk(self, k):
        k = jnp.clip(k, 0, self.n_z - 1)
        return lax.dynamic_index_in_dim(self.parts, k, self.z_axis, keepdims=False)

    def add(self, step, *earlier):
        n_z = self.n_z
        up, down = self.chunk(self.z + n_z - step), self.chunk(self.z - n_z + step)
        if self.up is not None:
            up = (up.astype(F32) + self.up.astype(F32)).astype(BF16)
            down = (down.astype(F32) + self.down.astype(F32)).astype(BF16)
        if earlier:
            up, down = after(up, *earlier), after(down, *earlier)
        self.up = lax.ppermute(up, "z", [(i, i + 1) for i in range(step)])
        self.down = lax.ppermute(down, "z", [(i, i - 1) for i in range(n_z - step, n_z)])

    def close(self):
        total = self.chunk(self.z).astype(F32)
        total = (total + self.up.astype(F32) + self.down.astype(F32)).astype(BF16)
        self.own = total if self.between is None else self.between(total)
        self.ups, self.downs = [self.own], [self.own]

    def spread(self, step, *earlier):
        n_z = self.n_z
        up, down = self.ups[-1], self.downs[-1]
        if earlier:
            up, down = after(up, *earlier), after(down, *earlier)
        self.ups.append(lax.ppermute(up, "z", [(i, i + 1) for i in range(step - 1, n_z - 1)]))
        self.downs.append(lax.ppermute(down, "z", [(i, i - 1) for i in range(1, n_z - step + 1)]))

    def result(self):
        mine = collect(self.own, self.ups[1:], self.downs[1:], self.z)
        return [mine] + [swap(mine, "core", e) for e in range(1, lax.axis_size("core"))]


def run_sums(sums, waits):
    previous, slot = None, 0

    def due():
        return tuple(waits[slot]()) if slot in waits else ()

    for one in sums:
        n_z = one.n_z
        for step in range(1, n_z):
            earlier = due()
            if previous is not None:
                earlier += (previous.ups[step], previous.downs[step])
            one.add(step, *earlier)
            if previous is not None and step + 1 < n_z:
                previous.spread(step + 1)
            slot += 1
        one.close()
        one.spread(1, *due())
        slot += 1
        previous = one
    for step in range(2, previous.n_z):
        previous.spread(step, *due())
        slot += 1


def rms_parts(values):
    inverse = lax.rsqrt(jnp.mean(values * values, axis=-1, keepdims=True) + EPS)
    return values * inverse, inverse


def rms_backward(grad_normed, unit_rows, inverse, norm_gain):
    scaled = grad_normed * norm_gain
    grad_rows = inverse * (
        scaled - unit_rows * jnp.mean(scaled * unit_rows, axis=-1, keepdims=True)
    )
    return jnp.sum(grad_normed * unit_rows, axis=0), grad_rows


def rotate(values, cosine, sine):
    half = values.shape[1] // 2
    a, b = values[:, :half], values[:, half:]
    return jnp.concatenate([a * cosine - b * sine, b * cosine + a * sine], axis=1)


def rotate_back(grads, cosine, sine):
    half = grads.shape[1] // 2
    a, b = grads[:, :half], grads[:, half:]
    return jnp.concatenate([a * cosine + b * sine, b * cosine - a * sine], axis=1)


def per_device(
    tokens, doc_starts, gain_one, w_query, w_key, w_value, w_out, gain_two, w_gate, w_up, w_down,
    cotangent,
):
    n_z, n_c, n_f = lax.axis_size("z"), lax.axis_size("core"), lax.axis_size("f")
    z, c, f = lax.axis_index("z"), lax.axis_index("core"), lax.axis_index("f")
    n_t = n_f * n_c
    block_len, width = tokens.shape[3], tokens.shape[4]
    rows = 2 * block_len
    plane, span = n_t * rows, n_c * rows
    shard = width // n_f
    q_width = w_query.shape[1] // n_t
    kv_width = w_key.shape[1] // n_t
    hidden = w_gate.shape[1] // n_t
    qkv_width = q_width + 2 * kv_width
    heads = q_width // HEAD_SIZE
    in_plane = ("f", "core")

    own_x = tokens.reshape(rows, width)
    own_dy = cotangent.reshape(rows, width)

    z_order = [(z - s) % n_z for s in range(n_z)]

    order = Order()
    do = order.region

    first = do(
        payload,
        own_x, doc_starts.reshape(1, rows), gain_one.reshape(1, shard), gain_two.reshape(1, shard),
    )
    payloads = lax.all_gather(first, in_plane, axis=0, tiled=True)

    w_qkv = do(lambda *w: pack_qkv(*w, c, n_f, n_c), w_query, w_key, w_value)
    w_qkv = lax.all_to_all(w_qkv, "f", 0, 0)
    gate_parts, up_parts = do(
        lambda *w: [slice_columns(x, c, n_f, n_c) for x in w], w_gate, w_up
    )

    def project(payloads, w_qkv):
        gains = payloads.reshape(n_f, n_c, rows + EXTRA, width)[:, 0, rows + 2 : rows + 4, :shard]
        gains = jnp.transpose(gains, (1, 0, 2)).reshape(2, width).astype(F32)
        w_qkv = w_qkv.reshape(width, qkv_width)
        return (gains, w_qkv) + tuple(
            project_first(payloads, gains, w_qkv, z, n_z, n_c, block_len)
        )

    payloads, w_qkv = order.pin(payloads, w_qkv)
    gate_full = lax.all_to_all(
        lax.optimization_barrier((gate_parts, w_qkv))[0], "f", 0, 0
    )
    gains, w_qkv, h_one, query, key_value, cosine, sine, starts = do(project, payloads, w_qkv)
    gain_one_full, gain_two_full = gains[0], gains[1]
    starts = starts.reshape(n_f, 1, span)
    (early_dy,) = order.pin(own_dy)
    dy_all = lax.all_gather(early_dy, in_plane, axis=0, tiled=True)

    def positions(z_index):
        device = z_index * n_c + jnp.arange(n_c, dtype=jnp.int32)[:, None]
        within = jnp.arange(rows, dtype=jnp.int32)[None, :]
        return jnp.where(
            within < block_len,
            device * block_len + within,
            (2 * n_z * n_c - 1 - device) * block_len + within - block_len,
        ).reshape(span)

    q_pos = positions(z)[None, :]
    k_pos = jnp.concatenate([positions(zi) for zi in z_order])[:, None]

    key_values = turn_along_z(key_value)
    attn, attn_low, lse = do(
        lambda query, *kvs: attention(query, kvs, k_pos, q_pos, starts, n_f), query, *key_values
    )
    def reduce_plane(value):
        return lax.psum_scatter(value, in_plane, scatter_dimension=0, tiled=True)

    residual = own_x.astype(F32)
    def project_out(attn_low, w_out, gate_full):
        rows_of = lax.dynamic_slice_in_dim(w_out, c * q_width, q_width, 0)
        return rows_of, tn(attn_low, rows_of).astype(BF16), gate_full

    out_rows, projected, gate_full = do(project_out, attn_low, w_out, gate_full)
    (up_parts,) = order.pin(up_parts)
    up_full = lax.all_to_all(up_parts, "f", 0, 0).reshape(width, hidden)
    gate_full = gate_full.reshape(width, hidden)

    def after_attention(reduced, up_full):
        middle = residual + reduced.astype(F32)
        unit, inverse = rms_parts(middle)
        return middle, unit, inverse, (unit * gain_two_full).astype(BF16), up_full

    middle, unit_two, inv_two, h_two, up_full = do(
        after_attention, reduce_plane(projected), up_full
    )
    h_two = lax.all_gather(h_two, in_plane, axis=0, tiled=True)

    def forward(h_two, gate_full, up_full):
        gate, up = nn(h_two, gate_full), nn(h_two, up_full)
        return gate, up, (gate * jax.nn.sigmoid(gate) * up).astype(BF16)

    gate, up, mid = do(forward, h_two, gate_full, up_full)
    down_rows = do(lambda w: lax.dynamic_slice_in_dim(w, c * hidden, hidden, 0), w_down)

    def work(dy, down_rows, gate, up):
        sigmoid = jax.nn.sigmoid(gate)
        grad_mid = nt(dy, down_rows)
        grad_g = (grad_mid * up * sigmoid * (1.0 + gate * (1.0 - sigmoid))).astype(BF16)
        return grad_g, (grad_mid * (gate * sigmoid)).astype(BF16)

    grad_g, grad_u = do(work, dy_all, down_rows, gate, up)
    h_two_parts = do(lambda g, u: (nt(g, gate_full) + nt(u, up_full)).astype(BF16), grad_g, grad_u)
    h_two_back = reduce_plane(h_two_parts)

    grad_down = tn(mid, dy_all).astype(BF16)
    grad_gate = tn(h_two, grad_g).astype(BF16)
    grad_up = tn(h_two, grad_u).astype(BF16)
    grad_gain_two, grad_norm = rms_backward(
        h_two_back.astype(F32), unit_two, inv_two, gain_two_full
    )
    grad_middle = own_dy.astype(F32) + grad_norm

    branch_low = grad_middle.astype(BF16)
    grad_branch = lax.all_gather(branch_low, in_plane, axis=0, tiled=True)
    grad_attn = nt(out_rows, grad_branch).astype(BF16)
    grad_out = nn(attn_low, grad_branch).astype(BF16)
    grad_query, grad_kv = attention_back(
        query, key_values, grad_attn, attn, lse, k_pos, q_pos, starts, n_f, z_order
    )
    kv_total = jnp.sum(lax.all_to_all(grad_kv, "z", 0, 0).astype(F32), axis=0)
    grad_query = grad_query.reshape(heads, HEAD_SIZE, plane) * HEAD_SIZE ** (-0.5)
    grad_qkv = jnp.concatenate(
        [
            rotate_back(grad_query, cosine, sine).reshape(q_width, plane),
            rotate_back(kv_total[None, :HEAD_SIZE], cosine, sine)[0],
            kv_total[HEAD_SIZE:],
        ],
        axis=0,
    ).astype(BF16)
    grad_w_qkv = lax.dot_general(
        h_one, grad_qkv, (((0,), (1,)), ((), ())), preferred_element_type=F32
    ).astype(BF16)
    h_one_parts = lax.dot_general(
        grad_qkv, w_qkv, (((0,), (1,)), ((), ())), preferred_element_type=F32
    ).astype(BF16)
    mixed_parts = nn(mid, down_rows).astype(BF16)
    mixed = middle + reduce_plane(after(mixed_parts, grad_branch)).astype(F32)
    grad_h_one = reduce_plane(h_one_parts).astype(F32)
    unit_one, inv_one = rms_parts(residual)
    grad_gain_one, grad_norm = rms_backward(grad_h_one, unit_one, inv_one, gain_one_full)
    grad_tokens = grad_middle + grad_norm
    gains = jnp.stack([grad_gain_one, grad_gain_two])
    for axis, size in (("z", n_z), ("f", n_f), ("core", n_c)):
        for bit in range(size.bit_length() - 1):
            gains = gains + swap(gains, axis, 1 << bit)
    gain_grads = lax.dynamic_slice_in_dim(gains, f * shard, shard, 1)

    def to_shards(grad):
        return lax.all_to_all(grad, "f", 0, 0)

    def by_z(grad, axis):
        shape = grad.shape
        return grad.reshape(shape[:axis] + (n_z, shape[axis] // n_z) + shape[axis + 1 :])

    gate_shards = to_shards(grad_gate.reshape(n_f, shard, hidden))
    up_shards = to_shards(after(grad_up.reshape(n_f, shard, hidden), gate_shards))
    sum_down = ZSum(by_z(grad_down, 0), 0)
    sum_gate = ZSum(by_z(gate_shards, 1), 1)
    sum_up = ZSum(by_z(up_shards, 1), 1)
    sum_out = ZSum(by_z(grad_out, 0), 0)
    sum_qkv = ZSum(by_z(grad_w_qkv.reshape(n_f, shard, qkv_width), 1), 1, to_shards)
    def finish_rows(one):
        cores = one.result()
        piece_rows, columns = cores[0].shape[1:]
        if piece_rows % 8 == 0:
            return assemble_rows(cores, c)
        result = blank((n_c, n_z, piece_rows, columns), F32)
        for e, piece in enumerate(cores):
            result = lax.dynamic_update_index_in_dim(result, piece.astype(F32), c ^ e, 0)
        return result.reshape(-1, columns)

    def finish_columns(one, splits):
        cores = one.result()
        piece_rows = cores[0].shape[2]
        if piece_rows % 8 == 0:
            return assemble(cores, c, splits)
        results = []
        for low, high in splits:
            out = blank((n_z, piece_rows, n_f, n_c, high - low), F32)
            for e, piece in enumerate(cores):
                update = jnp.transpose(piece[..., low:high].astype(F32), (0, 2, 1, 3))
                out = lax.dynamic_update_index_in_dim(out, update, c ^ e, 3)
            results.append(out.reshape(shard, n_t * (high - low)))
        return results

    totals = {}

    def finish(name, function, *args):
        def get():
            if name not in totals:
                made = function(*args)
                totals[name] = made if isinstance(made, (list, tuple)) else [made]
            return totals[name]

        return get

    down_done = finish("down", finish_rows, sum_down)
    gate_done = finish("gate", finish_columns, sum_gate, [(0, hidden)])
    up_done = finish("up", finish_columns, sum_up, [(0, hidden)])
    out_done = finish("out", finish_rows, sum_out)
    splits = [(0, q_width), (q_width, q_width + kv_width), (q_width + kv_width, qkv_width)]
    qkv_done = finish("qkv", finish_columns, sum_qkv, splits)

    def slot(which, step):
        return which * n_z + min(step, n_z - 1)

    run_sums(
        [sum_down, sum_gate, sum_up, sum_out, sum_qkv],
        {
            slot(3, 0): down_done,
            slot(3, 2): gate_done,
            slot(4, 2): lambda: [*up_done(), gain_grads],
            slot(4, 3): out_done,
        },
    )
    total_down, total_gate, total_up, total_out = (
        done()[0] for done in (down_done, gate_done, up_done, out_done)
    )
    total_query, total_key, total_value = qkv_done()
    return (
        mixed.reshape(tokens.shape),
        grad_tokens.reshape(tokens.shape),
        gain_grads[0],
        total_query,
        total_key,
        total_value,
        total_out,
        gain_grads[1],
        total_gate,
        total_up,
        total_down,
    )


def solution(mesh):
    n_ctx, n_fsdp = mesh.shape["ctx"], mesh.shape["fsdp"]
    n_core = KEY_VALUE_HEADS // n_fsdp
    inner = Mesh(
        np.asarray(mesh.devices).reshape(n_ctx // n_core, n_core, n_fsdp), ("z", "core", "f")
    )
    ctx = ("z", "core")
    return jax.shard_map(
        per_device,
        mesh=inner,
        in_specs=(
            P("f", ctx, None, None, None),
            P("f", ctx, None, None),
            P("f"),
            P("f", None),
            P("f", None),
            P("f", None),
            P("f", None),
            P("f"),
            P("f", None),
            P("f", None),
            P("f", None),
            P("f", ctx, None, None, None),
        ),
        out_specs=(
            P("f", ctx, None, None, None),
            P("f", ctx, None, None, None),
            P("f"),
            P("f", None),
            P("f", None),
            P("f", None),
            P("f", None),
            P("f"),
            P("f", None),
            P("f", None),
            P("f", None),
        ),
        check_vma=False,
    )
```

time: 1400 us -> 1080 us (0.77)
  local copies, waits for them, and re-layouts: 135 us -> 34.8 us
  other arithmetic: 127 us -> 54.5 us
  starting transfers between devices: 265 us -> 194 us
  blocking collectives: 39.3 us -> 0 us
  matrix products: 142 us -> 112 us
  waiting for transfers between devices: 553 us -> 528 us
    ppermute x120 -> x10, waiting for transfers between devices: 240 us -> 1.38 us  [swap(): return lax.ppermute(value, axis, [(i, i ^ offset) for i in range(size)])]
    all_to_all x0 -> x7, waiting for transfers between devices: none -> 103 us  [the longest x1 65.5 us: per_device(): up_full = lax.all_to_all(up_parts, 'f', 0, 0).reshape(width, hidden)]
    all_gather x0 -> x4, waiting for transfers between devices: none -> 77.7 us  [the longest x1 40.4 us: per_device(): h_two = lax.all_gather(h_two, in_plane, axis=0, tiled=True)]
    ppermute x120 -> x10, starting transfers between devices: 86.5 us -> 12.3 us  [swap(): return lax.ppermute(value, axis, [(i, i ^ offset) for i in range(size)])]
    psum x1 -> x0, blocking collectives: 39.3 us -> none  [per_device(): lax.psum(jnp.stack([grad_gain_one, grad_gain_two]), ('z', 'core', 'f'))]
    all_to_all x0 -> x7, starting transfers between devices: none -> 33.3 us  [the longest x3 13.6 us: to_shards(): return lax.all_to_all(grad, 'f', 0, 0)]
    ppermute x63 -> x60, starting transfers between devices: 174 us -> 144 us  [the longest x15 67.5 us: add(): self.up = lax.ppermute(up, 'z', [(i, i + 1) for i in range(step)])]
    convert_element_type x39 -> x19, other arithmetic: 71.3 us -> 42.1 us  [the longest x10 25.1 us: add(): up = (up.astype(F32) + self.up.astype(F32)).astype(BF16)]
  transfers between devices with their start and end apart: 186 -> 88, of which waited for: 63 -> 42; matrix products, arithmetic and copies ran while one was open for 17% -> 14% of each run, Pallas kernels for 7% -> 11%
where the time goes in v2:
time: 1080 us; the launch traced here: 1070 us
  waiting for transfers between devices  528 us (49%)
  starting transfers between devices  194 us (18%)
  Pallas kernels  131 us (12%)
  matrix products  112 us (10%)
  other arithmetic  54.5 us (5%)
  local copies, waits for them, and re-layouts  34.8 us (3%)
  between operations  16 us (1%)
    ppermute x15, waiting for transfers between devices, add(): self.up = lax.ppermute(up, 'z', [(i, i + 1) for i in range(step)])  148 us
    ppermute x15, waiting for transfers between devices, spread(): lax.ppermute(down, 'z', [(i, i - 1) for i in range(1, n_z - step + 1)])  114 us
    ppermute x15, starting transfers between devices, add(): self.up = lax.ppermute(up, 'z', [(i, i + 1) for i in range(step)])  67.5 us
    all_to_all x1, waiting for transfers between devices, per_device(): up_full = lax.all_to_all(up_parts, 'f', 0, 0).reshape(width, hidden)  65.5 us
    all_gather x1, waiting for transfers between devices, per_device(): h_two = lax.all_gather(h_two, in_plane, axis=0, tiled=True)  40.4 us
    ppermute x15, starting transfers between devices, spread(): lax.ppermute(up, 'z', [(i, i + 1) for i in range(step - 1, n_z - 1)])  39.9 us
    ppermute x15, waiting for transfers between devices, add(): lax.ppermute(down, 'z', [(i, i - 1) for i in range(n_z - step, n_z)])  36.7 us
    dot_general x4, matrix products, nn(): lax.dot_general(a, b, (((1,), (0,)), ((), ())), preferred_element_type=F32)  34.3 us
  transfers between devices with their start and end apart: 88, of which 42 were waited for; matrix products, arithmetic and copies ran while one was open for 14% of the time, Pallas kernels for 11%

profile of v2, /device:TPU:0, one launch (start us, length us, event | category | flops | bytes accessed | tf_op | source)
XLA Modules:
  0.0 1071.1 jit_solution(10727848268024543991)
XLA Ops:
  22.4 5.2 all-to-all-start
  37.5 26.7 %all-to-all-done = bf16[4,640,480]{1,2,0:T(8,128)(2,1)} async-done(((bf16[4,640,480]{1,2,0:T(8,128)(2,1)}), bf16[4,640,480]{1,2,0:T(8,128)(2,1)}, u32[]{:S(2)}, u32[]{:S(2)}) %all-to-all-start) | async-done | bytes 2457632 | tf_op jit(solution)/shard_map/all_to_all | solution.py:590
  64.3 17.2 %all-gather.5.cloned.1.call-done.block = bf16[1280,2560]{1,0:T(8,128)(2,1)} async-done(((bf16[160,2560]{1,0:T(8,128)(2,1)}), bf16[1280,2560]{1,0:T(8,128)(2,1)}) %all-gather.5.cloned.1.call-update) | async-done | bytes 6553616 | tf_op jit(solution)/shard_map/all_gather | solution.py:587
  93.0 11.1 %shard_map.207 = (bf16[1024,2560]{1,0:T(8,128)(2,1)}, bf16[320,1024]{1,0:T(8,128)(2,1)}, bf16[160,1024]{1,0:T(8,128)(2,1)}, f32[40,1024]{1,0:T(8,128)}, f32[40,1024]{1,0:T(8,128)}, /*index=5*/s32[8,1,128]{2,1,0:T(1,128)}) custom-call(s32[1]{0:T(128)} %bitcast.1.where, bf16[1280,2560]{1,0:T(8,128)(2,1)} %all-gather.5.cloned.1.call-done.block, ...), custom_call_target="tpu_custom_call" | custom-call | flops 2516582400 | bytes 10485760 | tf_op jit(solution)/shard_map/pallas_call | solution.py:183
  110.3 5.7 collective-permute-done.2.refs_4_
  116.0 20.4 %collective-permute-done.1.refs_3_ = bf16[160,1024]{1,0:T(8,128)(2,1)} collective-permute-done((bf16[160,1024]{1,0:T(8,128)(2,1)}, bf16[160,1024]{1,0:T(8,128)(2,1)}, u32[]{:S(2)}, u32[]{:S(2)}) %collective-permute-start.1) | collective-permute-done | bytes 327712 | tf_op jit(solution)/shard_map/ppermute | solution.py:459
  136.4 14.1 %shard_map.208 = (f32[320,1024]{1,0:T(8,128)}, bf16[320,1024]{1,0:T(8,128)(2,1)}, f32[4,4,256]{2,1,0:T(4,128)}) custom-call(bf16[320,1024]{1,0:T(8,128)(2,1)} %get-tuple-element.107.refs_0_, bf16[160,1024]{1,0:T(8,128)(2,1)} %get-tuple-element.108.refs_1_, bf16[160,1024]{1,0:T(8,128)(2,1)} %collective-permute-done.refs_2_, ...), custom_call_target="tpu_custom_call" | custom-call | flops 1342177280 | bytes 2621440 | tf_op jit(solution)/shard_map/pallas_call | solution.py:257
  156.4 5.1 all-to-all-start.2
  161.6 65.5 %all-to-all-done.2 = bf16[4,640,896]{2,1,0:T(8,128)(2,1)} async-done(((bf16[4,640,896]{2,1,0:T(8,128)(2,1)}), bf16[4,640,896]{2,1,0:T(8,128)(2,1)}, u32[]{:S(2)}, u32[]{:S(2)}) %all-to-all-start.2) | async-done | bytes 4587552 | tf_op jit(solution)/shard_map/all_to_all | solution.py:639
  227.1 16.4 %reduce-scatter.5.cloned.1.call-done = bf16[128,2560]{1,0:T(8,128)(2,1)} async-done(((bf16[1024,2560]{1,0:T(8,128)(2,1)}), bf16[128,2560]{1,0:T(8,128)(2,1)}) %reduce-scatter.5.cloned.1.call-update) | async-done | bytes 655376 | tf_op jit(solution)/shard_map/reduce_scatter | solution.py:630
  247.9 40.4 %all-gather.7.cloned.1.call-done = bf16[1024,2560]{1,0:T(8,128)(2,1)} async-done(((bf16[128,2560]{1,0:T(8,128)(2,1)}), bf16[1024,2560]{1,0:T(8,128)(2,1)}) %all-gather.7.cloned.1.call-update) | async-done | bytes 5242896 | tf_op jit(solution)/shard_map/all_gather | solution.py:650
  288.3 9.0 fusion.58
  297.4 11.2 %multiply_convert_fusion.2 = (bf16[1024,896]{1,0:T(8,128)(2,1)S(1)}, f32[1024,896]{1,0:T(8,128)}) fusion(f32[1024,896]{1,0:T(8,128)S(1)} %fusion.58, bf16[1024,2560]{1,0:T(8,128)(2,1)S(1)} %copy-done.42, bf16[2560,896]{1,0:T(8,128)(2,1)} %bitcast.14), kind=kOutput, calls=%fused_computation.12 | convolution fusion | flops 4703125504 | bytes 19005440 | tf_op jit(solution)/shard_map/dot_general | solution.py:229
  311.3 20.1 %all-gather.9.cloned.1.call-done = bf16[1024,2560]{1,0:T(8,128)(2,1)} async-done(((bf16[128,2560]{1,0:T(8,128)(2,1)}), bf16[1024,2560]{1,0:T(8,128)(2,1)}) %all-gather.9.cloned.1.call-update) | async-done | bytes 5242896 | tf_op jit(solution)/shard_map/all_gather | solution.py:611
  331.4 11.4 %multiply_convert_fusion = (bf16[1024,896]{1,0:T(8,128)(2,1)S(1)}, bf16[1024,896]{1,0:T(8,128)(2,1)S(1)}) fusion(f32[1024,896]{1,0:T(8,128)} %copy-done.48, f32[1024,896]{1,0:T(8,128)} %get-tuple-element.129, bf16[1024,2560]{1,0:T(8,128)(2,1)} %all-gather.9.cloned.1.call-done, bf16[896,2560]{1,0:T(8,128)(2,1)} %constant_dynamic-slice_fusion.2), kind=kOutput, calls=%fused_computation.9 | convolution fusion | flops 4709548032 | bytes 20840448 | tf_op jit(solution)/shard_map/dot_general | solution.py:225
  344.1 7.5 fusion.59
  351.6 10.2 add_convert_fusion
  361.8 7.5 convolution_convert_fusion.5
  377.1 23.5 %collective-permute-done.8 = bf16[224,2560]{1,0:T(8,128)(2,1)} collective-permute-done((bf16[224,2560]{1,0:T(8,128)(2,1)}, bf16[224,2560]{1,0:T(8,128)(2,1)}, u32[]{:S(2)}, u32[]{:S(2)}) %collective-permute-start.8) | collective-permute-done | bytes 1146912 | tf_op jit(solution)/shard_map/ppermute | solution.py:485
  403.5 5.5 collective-permute-start.9
  409.0 23.4 %collective-permute-done.9 = bf16[224,2560]{1,0:T(8,128)(2,1)} collective-permute-done((bf16[224,2560]{1,0:T(8,128)(2,1)}, bf16[224,2560]{1,0:T(8,128)(2,1)}, u32[]{:S(2)}, u32[]{:S(2)}) %collective-permute-start.9) | collective-permute-done | bytes 1146912 | tf_op jit(solution)/shard_map/ppermute | solution.py:485
  436.9 9.5 convolution_convert_fusion.3
  451.5 6.2 collective-permute-start.10
  464.9 15.1 %collective-permute-done.10 = bf16[224,2560]{1,0:T(8,128)(2,1)} collective-permute-done((bf16[224,2560]{1,0:T(8,128)(2,1)}, bf16[224,2560]{1,0:T(8,128)(2,1)}, u32[]{:S(2)}, u32[]{:S(2)}) %collective-permute-start.10) | collective-permute-done | bytes 1146912 | tf_op jit(solution)/shard_map/ppermute | solution.py:485
  480.0 14.4 %collective-permute-done.13 = bf16[224,2560]{1,0:T(8,128)(2,1)} collective-permute-done((bf16[224,2560]{1,0:T(8,128)(2,1)}, bf16[224,2560]{1,0:T(8,128)(2,1)}, u32[]{:S(2)}, u32[]{:S(2)}) %collective-permute-start.13) | collective-permute-done | bytes 1146912 | tf_op jit(solution)/shard_map/ppermute | solution.py:486
  498.0 5.6 collective-permute-start.14
  503.6 5.3 all-to-all-done.4
  510.7 12.0 %collective-permute-done.17.refs_4_ = bf16[224,2560]{1,0:T(8,128)(2,1)S(1)} collective-permute-done((bf16[224,2560]{1,0:T(8,128)(2,1)S(1)}, bf16[224,2560]{1,0:T(8,128)(2,1)S(1)}, u32[]{:S(2)}, u32[]{:S(2)}) %collective-permute-start.17) | collective-permute-done | bytes 1146912 | tf_op jit(solution)/shard_map/ppermute | solution.py:500
  532.6 16.5 %collective-permute-done.21 = bf16[4,160,896]{2,1,0:T(8,128)(2,1)S(1)} collective-permute-done((bf16[4,160,896]{2,1,0:T(8,128)(2,1)S(1)}, bf16[4,160,896]{2,1,0:T(8,128)(2,1)S(1)}, u32[]{:S(2)}, u32[]{:S(2)}) %collective-permute-start.21) | collective-permute-done | bytes 1146912 | tf_op jit(solution)/shard_map/ppermute | solution.py:485
  563.5 9.6 convolution_convert_fusion.4
  589.6 16.2 %collective-permute-done.23 = bf16[4,160,896]{2,1,0:T(8,128)(2,1)S(1)} collective-permute-done((bf16[4,160,896]{2,1,0:T(8,128)(2,1)S(1)}, bf16[4,160,896]{2,1,0:T(8,128)(2,1)S(1)}, u32[]{:S(2)}, u32[]{:S(2)}) %collective-permute-start.23) | collective-permute-done | bytes 1146912 | tf_op jit(solution)/shard_map/ppermute | solution.py:485
  605.7 6.3 collective-permute-done.26
  615.1 5.6 collective-permute-start.27
  625.8 8.9 collective-permute-done.28.refs_4_
  646.5 12.8 %collective-permute-done.29 = bf16[4,160,896]{2,1,0:T(8,128)(2,1)S(1)} collective-permute-done((bf16[4,160,896]{2,1,0:T(8,128)(2,1)S(1)}, bf16[4,160,896]{2,1,0:T(8,128)(2,1)S(1)}, u32[]{:S(2)}, u32[]{:S(2)}) %collective-permute-start.29) | collective-permute-done | bytes 1146912 | tf_op jit(solution)/shard_map/ppermute | solution.py:485
  662.8 6.9 collective-permute-start.32
  671.4 5.2 convolution_convert_fusion.8.refs_5_
  676.7 17.2 %shard_map.209 = (f32[320,1024]{1,0:T(8,128)}, bf16[4,160,1024]{2,1,0:T(8,128)(2,1)}) custom-call(s32[4]{0:T(128)} %pad_add_fusion.1.where, bf16[320,1024]{1,0:T(8,128)(2,1)} %get-tuple-element.107.refs_0_, bf16[160,1024]{1,0:T(8,128)(2,1)} %get-tuple-element.108.refs_1_, bf16[160,1024]{1,0:T(8,128)(2,1)} %collective-permute-done.refs_2_, ...), custom_call_target="tpu_custom_call" | custom-call | flops 3355443200 | bytes 3932160 | tf_op jit(solution)/shard_map/pallas_call | solution.py:315
  700.6 5.9 shard_map.210.refs_0_
  710.9 23.4 %collective-permute-done.34.refs_6_ = bf16[4,160,896]{2,1,0:T(8,128)(2,1)S(1)} collective-permute-done((bf16[4,160,896]{2,1,0:T(8,128)(2,1)}, bf16[4,160,896]{2,1,0:T(8,128)(2,1)S(1)}, u32[]{:S(2)}, u32[]{:S(2)}) %collective-permute-start.34) | collective-permute-done | bytes 1146912 | tf_op jit(solution)/shard_map/ppermute | solution.py:500
  746.4 5.3 collective-permute-done.35
  751.6 8.6 collective-permute-done.38
  769.0 6.0 shard_map.212.refs_0_
  775.1 12.1 %shard_map.211 = f32[1792,2560]{1,0:T(8,128)} custom-call(s32[1]{0:T(128)} %bitcast.2.where, bf16[4,224,2560]{2,1,0:T(8,128)(2,1)} %shard_map.210.refs_0_, bf16[4,224,2560]{2,1,0:T(8,128)(2,1)} %collective-permute-done.20.refs_1_), custom_call_target="tpu_custom_call" | custom-call | bytes 18350080 | tf_op jit(solution)/shard_map/pallas_call | solution.py:440
  794.7 7.1 collective-permute-start.41
  802.5 8.0 collective-permute-done.41
  810.7 6.3 collective-permute-done.43.refs_5_
  824.2 5.2 collective-permute-done.44
  831.3 10.0 shard_map.213
  841.4 8.5 collective-permute-done.47.refs_6_
  849.8 6.0 shard_map.214.refs_0_
  860.4 9.6 convolution_convert_fusion.2
  876.1 5.3 collective-permute-start.52
  881.4 7.1 convolution_convert_fusion.6
  901.1 9.5 collective-permute-done.54
  918.7 10.0 collective-permute-start.5
  931.9 7.3 collective-permute-done.60.refs_6_
  946.5 10.0 shard_map.215
  959.4 12.9 %collective-permute-done.61 = bf16[4,160,480]{2,1,0:T(8,128)(2,1)S(1)} collective-permute-done((bf16[4,160,480]{2,1,0:T(8,128)(2,1)S(1)}, bf16[4,160,480]{2,1,0:T(8,128)(2,1)S(1)}, u32[]{:S(2)}, u32[]{:S(2)}) %collective-permute-start.61) | collective-permute-done | bytes 614432 | tf_op jit(solution)/shard_map/ppermute | solution.py:485
  981.9 7.0 shard_map.217
  997.7 12.8 %collective-permute-done.69.refs_4_ = bf16[4,160,480]{2,1,0:T(8,128)(2,1)S(1)} collective-permute-done((bf16[4,160,480]{2,1,0:T(8,128)(2,1)S(1)}, bf16[4,160,480]{2,1,0:T(8,128)(2,1)S(1)}, u32[]{:S(2)}, u32[]{:S(2)}) %collective-permute-start.69) | collective-permute-done | bytes 614432 | tf_op jit(solution)/shard_map/ppermute | solution.py:500
  1012.5 15.8 %collective-permute-done.70.refs_5_ = bf16[4,160,480]{2,1,0:T(8,128)(2,1)S(1)} collective-permute-done((bf16[4,160,480]{2,1,0:T(8,128)(2,1)S(1)}, bf16[4,160,480]{2,1,0:T(8,128)(2,1)S(1)}, u32[]{:S(2)}, u32[]{:S(2)}) %collective-permute-start.70) | collective-permute-done | bytes 614432 | tf_op jit(solution)/shard_map/ppermute | solution.py:500
  1030.7 14.6 %collective-permute-done.71.refs_6_ = bf16[4,160,480]{2,1,0:T(8,128)(2,1)S(1)} collective-permute-done((bf16[4,160,480]{2,1,0:T(8,128)(2,1)S(1)}, bf16[4,160,480]{2,1,0:T(8,128)(2,1)S(1)}, u32[]{:S(2)}, u32[]{:S(2)}) %collective-permute-start.71) | collective-permute-done | bytes 614432 | tf_op jit(solution)/shard_map/ppermute | solution.py:500
  1056.6 7.2 shard_map.219
  (336 shorter events, 283.2 us)
Async XLA Ops:
  7.2 74.3 %all-gather.5.cloned.1.call-start = ((), (), s32[]{:S(2)}) async-start(), calls=%async_computation.11 | async-start | bytes 7372800 | tf_op jit(solution)/shard_map/all_gather | solution.py:587
  22.4 41.9 %all-to-all-start = ((bf16[4,640,480]{1,2,0:T(8,128)(2,1)}), bf16[4,640,480]{1,2,0:T(8,128)(2,1)}, u32[]{:S(2)}, u32[]{:S(2)}) async-start(bf16[4,640,480]{1,2,0:T(8,128)(2,1)} %copy.64), calls=%async_computation | async-start | bytes 4915200 | tf_op jit(solution)/shard_map/all_to_all | solution.py:590
  81.4 69.0 %all-to-all-start.1 = ((bf16[4,640,896]{2,1,0:T(8,128)(2,1)}), bf16[4,640,896]{2,1,0:T(8,128)(2,1)}, u32[]{:S(2)}, u32[]{:S(2)}) async-start(bf16[4,640,896]{2,1,0:T(8,128)(2,1)} %shard_map.205), calls=%async_computation.1 | async-start | bytes 9175040 | tf_op jit(solution)/shard_map/all_to_all | solution.py:604
  86.4 157.1 %reduce-scatter.5.cloned.1.call-start = ((), (), s32[]{:S(2)}) async-start(), calls=%async_computation.12 | async-start | bytes 5898240 | tf_op jit(solution)/shard_map/reduce_scatter | solution.py:630
  107.5 28.8 %collective-permute-start.1 = (bf16[160,1024]{1,0:T(8,128)(2,1)}, bf16[160,1024]{1,0:T(8,128)(2,1)}, u32[]{:S(2)}, u32[]{:S(2)}) collective-permute-start(bf16[160,1024]{1,0:T(8,128)(2,1)} %get-tuple-element.108.refs_1_), channel_id=1, source_target_pairs={{0,16},{8,24},{16,0},{24,8},{1,17},{9,25},{17,1},{25,9},{2,18},{10... | collective-permute-start | bytes 983048 | tf_op jit(solution)/shard_map/ppermute | solution.py:459
  107.5 28.8 %collective-permute-start = (bf16[160,1024]{1,0:T(8,128)(2,1)}, bf16[160,1024]{1,0:T(8,128)(2,1)}, u32[]{:S(2)}, u32[]{:S(2)}) collective-permute-start(bf16[160,1024]{1,0:T(8,128)(2,1)} %get-tuple-element.108.refs_1_), channel_id=1, source_target_pairs={{0,8},{8,16},{16,24},{24,0},{1,9},{9,17},{17,25},{25,1},{2,10},{10... | collective-permute-start | bytes 983048 | tf_op jit(solution)/shard_map/ppermute | solution.py:459
  156.4 70.6 %all-to-all-start.2 = ((bf16[4,640,896]{2,1,0:T(8,128)(2,1)}), bf16[4,640,896]{2,1,0:T(8,128)(2,1)}, u32[]{:S(2)}, u32[]{:S(2)}) async-start(bf16[4,640,896]{2,1,0:T(8,128)(2,1)} %shard_map.206), calls=%async_computation.3 | async-start | bytes 9175040 | tf_op jit(solution)/shard_map/all_to_all | solution.py:639
  161.5 126.8 %all-gather.7.cloned.1.call-start = ((), (), s32[]{:S(2)}) async-start(), calls=%async_computation.13 | async-start | bytes 5898240 | tf_op jit(solution)/shard_map/all_gather | solution.py:650
  247.1 84.3 %all-gather.9.cloned.1.call-start = ((), (), s32[]{:S(2)}) async-start(), calls=%async_computation.14 | async-start | bytes 5898240 | tf_op jit(solution)/shard_map/all_gather | solution.py:611
  247.7 213.9 %reduce-scatter.7.cloned.1.call-start = ((), (), s32[]{:S(2)}) async-start(), calls=%async_computation.15 | async-start | bytes 5898240 | tf_op jit(solution)/shard_map/reduce_scatter | solution.py:630
  371.9 28.7 %collective-permute-start.8 = (bf16[224,2560]{1,0:T(8,128)(2,1)}, bf16[224,2560]{1,0:T(8,128)(2,1)}, u32[]{:S(2)}, u32[]{:S(2)}) collective-permute-start(bf16[224,2560]{1,0:T(8,128)(2,1)} %get-tuple-element.187), channel_id=1, source_target_pairs={{0,8},{1,9},{2,10},{3,11},{4,12},{5,13},{6,14},{7,15}} | collective-permute-start | bytes 3440648 | tf_op jit(solution)/shard_map/ppermute | solution.py:485
  376.4 32.6 %collective-permute-start.11 = (bf16[224,2560]{1,0:T(8,128)(2,1)S(1)}, bf16[224,2560]{1,0:T(8,128)(2,1)S(1)}, u32[]{:S(2)}, u32[]{:S(2)}) collective-permute-start(bf16[224,2560]{1,0:T(8,128)(2,1)S(1)} %get-tuple-element.188), channel_id=1, source_target_pairs={{24,16},{25,17},{26,18},{27,19},{28,20},{29,21},{30,22},{31,23}} | collective-permute-start | bytes 3440648 | tf_op jit(solution)/shard_map/ppermute | solution.py:486
  403.5 28.8 %collective-permute-start.9 = (bf16[224,2560]{1,0:T(8,128)(2,1)}, bf16[224,2560]{1,0:T(8,128)(2,1)}, u32[]{:S(2)}, u32[]{:S(2)}) collective-permute-start(bf16[224,2560]{1,0:T(8,128)(2,1)} %fusion.14), channel_id=1, source_target_pairs={{0,8},{8,16},{1,9},{9,17},{2,10},{10,18},{3,11},{11,19},{4,12},{12... | collective-permute-start | bytes 3440648 | tf_op jit(solution)/shard_map/ppermute | solution.py:485
  436.2 21.4 %collective-permute-start.12 = (bf16[224,2560]{1,0:T(8,128)(2,1)}, bf16[224,2560]{1,0:T(8,128)(2,1)S(1)}, u32[]{:S(2)}, u32[]{:S(2)}) collective-permute-start(bf16[224,2560]{1,0:T(8,128)(2,1)} %get-tuple-element.186), channel_id=1, source_target_pairs={{16,8},{24,16},{17,9},{25,17},{18,10},{26,18},{19,11},{27,19},{20,... | collective-permute-start | bytes 3440648 | tf_op jit(solution)/shard_map/ppermute | solution.py:486
  446.5 62.5 %all-to-all-start.4 = ((bf16[4,640,896]{2,1,0:T(8,128)(2,1)}), bf16[4,640,896]{2,1,0:T(8,128)(2,1)}, u32[]{:S(2)}, u32[]{:S(2)}) async-start(bf16[4,640,896]{2,1,0:T(8,128)(2,1)} %bitcast.261), calls=%async_computation.8 | async-start | bytes 9175040 | tf_op jit(solution)/shard_map/all_to_all | solution.py:713
  451.4 220.0 %all-gather.11.cloned.1.call-start = ((), (), s32[]{:S(2)}) async-start(), calls=%async_computation.16 | async-start | bytes 5898240 | tf_op jit(solution)/shard_map/all_gather | solution.py:678
  451.5 28.5 %collective-permute-start.10 = (bf16[224,2560]{1,0:T(8,128)(2,1)}, bf16[224,2560]{1,0:T(8,128)(2,1)}, u32[]{:S(2)}, u32[]{:S(2)}) collective-permute-start(bf16[224,2560]{1,0:T(8,128)(2,1)} %get-tuple-element.185), channel_id=1, source_target_pairs={{0,8},{8,16},{16,24},{1,9},{9,17},{17,25},{2,10},{10,18},{18,26},{... | collective-permute-start | bytes 3440648 | tf_op jit(solution)/shard_map/ppermute | solution.py:485
  460.1 34.2 %collective-permute-start.13 = (bf16[224,2560]{1,0:T(8,128)(2,1)}, bf16[224,2560]{1,0:T(8,128)(2,1)}, u32[]{:S(2)}, u32[]{:S(2)}) collective-permute-start(bf16[224,2560]{1,0:T(8,128)(2,1)} %fusion.13), channel_id=1, source_target_pairs={{8,0},{16,8},{24,16},{9,1},{17,9},{25,17},{10,2},{18,10},{26,18},{... | collective-permute-start | bytes 3440648 | tf_op jit(solution)/shard_map/ppermute | solution.py:486
  496.7 26.1 %collective-permute-start.17 = (bf16[224,2560]{1,0:T(8,128)(2,1)S(1)}, bf16[224,2560]{1,0:T(8,128)(2,1)S(1)}, u32[]{:S(2)}, u32[]{:S(2)}) collective-permute-start(bf16[224,2560]{1,0:T(8,128)(2,1)S(1)} %fusion.17.refs_0_), channel_id=1, source_target_pairs={{8,0},{16,8},{24,16},{9,1},{17,9},{25,17},{10,2},{18,10},{26,18},{... | collective-permute-start | bytes 3440648 | tf_op jit(solution)/shard_map/ppermute | solution.py:500
  498.0 26.0 %collective-permute-start.14 = (bf16[224,2560]{1,0:T(8,128)(2,1)S(1)}, bf16[224,2560]{1,0:T(8,128)(2,1)}, u32[]{:S(2)}, u32[]{:S(2)}) collective-permute-start(bf16[224,2560]{1,0:T(8,128)(2,1)S(1)} %fusion.17.refs_0_), channel_id=1, source_target_pairs={{0,8},{8,16},{16,24},{1,9},{9,17},{17,25},{2,10},{10,18},{18,26},{... | collective-permute-start | bytes 3440648 | tf_op jit(solution)/shard_map/ppermute | solution.py:499
  524.0 25.1 %collective-permute-start.21 = (bf16[4,160,896]{2,1,0:T(8,128)(2,1)S(1)}, bf16[4,160,896]{2,1,0:T(8,128)(2,1)S(1)}, u32[]{:S(2)}, u32[]{:S(2)}) collective-permute-start(bf16[4,160,896]{2,1,0:T(8,128)(2,1)S(1)} %get-tuple-element.137), channel_id=1, source_target_pairs={{0,8},{1,9},{2,10},{3,11},{4,12},{5,13},{6,14},{7,15}} | collective-permute-start | bytes 3440648 | tf_op jit(solution)/shard_map/ppermute | solution.py:485
  528.7 20.4 %collective-permute-start.24 = (bf16[4,160,896]{2,1,0:T(8,128)(2,1)S(1)}, bf16[4,160,896]{2,1,0:T(8,128)(2,1)S(1)}, u32[]{:S(2)}, u32[]{:S(2)}) collective-permute-start(bf16[4,160,896]{2,1,0:T(8,128)(2,1)S(1)} %get-tuple-element.140), channel_id=1, source_target_pairs={{24,16},{25,17},{26,18},{27,19},{28,20},{29,21},{30,22},{31,23}} | collective-permute-start | bytes 3440648 | tf_op jit(solution)/shard_map/ppermute | solution.py:486
  529.6 24.6 %collective-permute-start.18 = (bf16[224,2560]{1,0:T(8,128)(2,1)S(1)}, bf16[224,2560]{1,0:T(8,128)(2,1)S(1)}, u32[]{:S(2)}, u32[]{:S(2)}) collective-permute-start(bf16[224,2560]{1,0:T(8,128)(2,1)S(1)} %collective-permute-done.17.refs_4_), channel_id=1, source_target_pairs={{8,0},{16,8},{9,1},{17,9},{10,2},{18,10},{11,3},{19,11},{12,4},{20... | collective-permute-start | bytes 3440648 | tf_op jit(solution)/shard_map/ppermute | solution.py:500
  530.9 23.3 %collective-permute-start.15 = (bf16[224,2560]{1,0:T(8,128)(2,1)}, bf16[224,2560]{1,0:T(8,128)(2,1)}, u32[]{:S(2)}, u32[]{:S(2)}) collective-permute-start(bf16[224,2560]{1,0:T(8,128)(2,1)} %collective-permute-done.14.refs_1_), channel_id=1, source_target_pairs={{8,16},{16,24},{9,17},{17,25},{10,18},{18,26},{11,19},{19,27},{12,... | collective-permute-start | bytes 3440648 | tf_op jit(solution)/shard_map/ppermute | solution.py:499
  554.2 23.9 %collective-permute-start.22 = (bf16[4,160,896]{2,1,0:T(8,128)(2,1)}, bf16[4,160,896]{2,1,0:T(8,128)(2,1)}, u32[]{:S(2)}, u32[]{:S(2)}) collective-permute-start(bf16[4,160,896]{2,1,0:T(8,128)(2,1)} %get-tuple-element.138), channel_id=1, source_target_pairs={{0,8},{8,16},{1,9},{9,17},{2,10},{10,18},{3,11},{11,19},{4,12},{12... | collective-permute-start | bytes 3440648 | tf_op jit(solution)/shard_map/ppermute | solution.py:485
  558.8 19.3 %collective-permute-start.25 = (bf16[4,160,896]{2,1,0:T(8,128)(2,1)}, bf16[4,160,896]{2,1,0:T(8,128)(2,1)}, u32[]{:S(2)}, u32[]{:S(2)}) collective-permute-start(bf16[4,160,896]{2,1,0:T(8,128)(2,1)} %get-tuple-element.141), channel_id=1, source_target_pairs={{16,8},{24,16},{17,9},{25,17},{18,10},{26,18},{19,11},{27,19},{20,... | collective-permute-start | bytes 3440648 | tf_op jit(solution)/shard_map/ppermute | solution.py:486
  560.5 22.9 %collective-permute-start.19 = (bf16[224,2560]{1,0:T(8,128)(2,1)S(1)}, bf16[224,2560]{1,0:T(8,128)(2,1)S(1)}, u32[]{:S(2)}, u32[]{:S(2)}) collective-permute-start(bf16[224,2560]{1,0:T(8,128)(2,1)S(1)} %collective-permute-done.18.refs_5_), channel_id=1, source_target_pairs={{8,0},{9,1},{10,2},{11,3},{12,4},{13,5},{14,6},{15,7}} | collective-permute-start | bytes 3440648 | tf_op jit(solution)/shard_map/ppermute | solution.py:500
  561.8 21.6 %collective-permute-start.16 = (bf16[224,2560]{1,0:T(8,128)(2,1)}, bf16[224,2560]{1,0:T(8,128)(2,1)}, u32[]{:S(2)}, u32[]{:S(2)}) collective-permute-start(bf16[224,2560]{1,0:T(8,128)(2,1)} %collective-permute-done.15.refs_2_), channel_id=1, source_target_pairs={{16,24},{17,25},{18,26},{19,27},{20,28},{21,29},{22,30},{23,31}} | collective-permute-start | bytes 3440648 | tf_op jit(solution)/shard_map/ppermute | solution.py:499
  573.1 50.9 %all-to-all-start.5 = ((bf16[4,640,896]{2,1,0:T(8,128)(2,1)}), bf16[4,640,896]{2,1,0:T(8,128)(2,1)}, u32[]{:S(2)}, u32[]{:S(2)}) async-start(bf16[4,640,896]{2,1,0:T(8,128)(2,1)} %bitcast.262), calls=%async_computation.9 | async-start | bytes 9175040 | tf_op jit(solution)/shard_map/all_to_all | solution.py:713
  583.4 22.3 %collective-permute-start.23 = (bf16[4,160,896]{2,1,0:T(8,128)(2,1)S(1)}, bf16[4,160,896]{2,1,0:T(8,128)(2,1)S(1)}, u32[]{:S(2)}, u32[]{:S(2)}) collective-permute-start(bf16[4,160,896]{2,1,0:T(8,128)(2,1)S(1)} %get-tuple-element.139), channel_id=1, source_target_pairs={{0,8},{8,16},{16,24},{1,9},{9,17},{17,25},{2,10},{10,18},{18,26},{... | collective-permute-start | bytes 3440648 | tf_op jit(solution)/shard_map/ppermute | solution.py:485
  588.3 23.8 %collective-permute-start.26 = (bf16[4,160,896]{2,1,0:T(8,128)(2,1)S(1)}, bf16[4,160,896]{2,1,0:T(8,128)(2,1)S(1)}, u32[]{:S(2)}, u32[]{:S(2)}) collective-permute-start(bf16[4,160,896]{2,1,0:T(8,128)(2,1)S(1)} %get-tuple-element.142), channel_id=1, source_target_pairs={{8,0},{16,8},{24,16},{9,1},{17,9},{25,17},{10,2},{18,10},{26,18},{... | collective-permute-start | bytes 3440648 | tf_op jit(solution)/shard_map/ppermute | solution.py:486
  613.8 20.9 %collective-permute-start.28 = (bf16[4,160,896]{2,1,0:T(8,128)(2,1)S(1)}, bf16[4,160,896]{2,1,0:T(8,128)(2,1)}, u32[]{:S(2)}, u32[]{:S(2)}) collective-permute-start(bf16[4,160,896]{2,1,0:T(8,128)(2,1)S(1)} %fusion.7.refs_0_), channel_id=1, source_target_pairs={{8,0},{16,8},{24,16},{9,1},{17,9},{25,17},{10,2},{18,10},{26,18},{... | collective-permute-start | bytes 3440648 | tf_op jit(solution)/shard_map/ppermute | solution.py:500
  615.1 22.6 %collective-permute-start.27 = (bf16[4,160,896]{2,1,0:T(8,128)(2,1)S(1)}, bf16[4,160,896]{2,1,0:T(8,128)(2,1)}, u32[]{:S(2)}, u32[]{:S(2)}) collective-permute-start(bf16[4,160,896]{2,1,0:T(8,128)(2,1)S(1)} %fusion.7.refs_0_), channel_id=1, source_target_pairs={{0,8},{8,16},{16,24},{1,9},{9,17},{17,25},{2,10},{10,18},{18,26},{... | collective-permute-start | bytes 3440648 | tf_op jit(solution)/shard_map/ppermute | solution.py:499
  637.6 21.7 %collective-permute-start.29 = (bf16[4,160,896]{2,1,0:T(8,128)(2,1)S(1)}, bf16[4,160,896]{2,1,0:T(8,128)(2,1)S(1)}, u32[]{:S(2)}, u32[]{:S(2)}) collective-permute-start(bf16[4,160,896]{2,1,0:T(8,128)(2,1)S(1)} %get-tuple-element.143), channel_id=1, source_target_pairs={{0,8},{1,9},{2,10},{3,11},{4,12},{5,13},{6,14},{7,15}} | collective-permute-start | bytes 3440648 | tf_op jit(solution)/shard_map/ppermute | solution.py:485
  642.9 19.9 %collective-permute-start.31 = (bf16[4,160,896]{2,1,0:T(8,128)(2,1)}, bf16[4,160,896]{2,1,0:T(8,128)(2,1)}, u32[]{:S(2)}, u32[]{:S(2)}) collective-permute-start(bf16[4,160,896]{2,1,0:T(8,128)(2,1)} %collective-permute-done.28.refs_4_), channel_id=1, source_target_pairs={{8,0},{16,8},{9,1},{17,9},{10,2},{18,10},{11,3},{19,11},{12,4},{20... | collective-permute-start | bytes 3440648 | tf_op jit(solution)/shard_map/ppermute | solution.py:500
  644.2 18.6 %collective-permute-start.30 = (bf16[4,160,896]{2,1,0:T(8,128)(2,1)}, bf16[4,160,896]{2,1,0:T(8,128)(2,1)}, u32[]{:S(2)}, u32[]{:S(2)}) collective-permute-start(bf16[4,160,896]{2,1,0:T(8,128)(2,1)} %collective-permute-done.27.refs_1_), channel_id=1, source_target_pairs={{8,16},{16,24},{9,17},{17,25},{10,18},{18,26},{11,19},{19,27},{12,... | collective-permute-start | bytes 3440648 | tf_op jit(solution)/shard_map/ppermute | solution.py:499
  662.8 43.7 %collective-permute-start.32 = (bf16[4,160,896]{2,1,0:T(8,128)(2,1)}, bf16[4,160,896]{2,1,0:T(8,128)(2,1)}, u32[]{:S(2)}, u32[]{:S(2)}) collective-permute-start(bf16[4,160,896]{2,1,0:T(8,128)(2,1)} %get-tuple-element.144), channel_id=1, source_target_pairs={{0,8},{8,16},{1,9},{9,17},{2,10},{10,18},{3,11},{11,19},{4,12},{12... | collective-permute-start | bytes 3440648 | tf_op jit(solution)/shard_map/ppermute | solution.py:485
  669.8 36.8 %collective-permute-start.37 = (bf16[4,160,896]{2,1,0:T(8,128)(2,1)}, bf16[4,160,896]{2,1,0:T(8,128)(2,1)}, u32[]{:S(2)}, u32[]{:S(2)}) collective-permute-start(bf16[4,160,896]{2,1,0:T(8,128)(2,1)} %get-tuple-element.147), channel_id=1, source_target_pairs={{16,8},{24,16},{17,9},{25,17},{18,10},{26,18},{19,11},{27,19},{20,... | collective-permute-start | bytes 3440648 | tf_op jit(solution)/shard_map/ppermute | solution.py:486
  693.9 45.6 %all-to-all-start.3 = ((bf16[4,160,1024]{2,1,0:T(8,128)(2,1)}), bf16[4,160,1024]{2,1,0:T(8,128)(2,1)S(1)}, u32[]{:S(2)}, u32[]{:S(2)}) async-start(bf16[4,160,1024]{2,1,0:T(8,128)(2,1)} %get-tuple-element.135), calls=%async_computation.6 | async-start | bytes 2621440 | tf_op jit(solution)/shard_map/all_to_all | solution.py:684
  698.4 193.3 %reduce-scatter.11.cloned.1.call-start = ((), (), s32[]{:S(2)}) async-start(), calls=%async_computation.18 | async-start | bytes 5898240 | tf_op jit(solution)/shard_map/reduce_scatter | solution.py:630
  698.4 35.9 %collective-permute-start.34 = (bf16[4,160,896]{2,1,0:T(8,128)(2,1)}, bf16[4,160,896]{2,1,0:T(8,128)(2,1)S(1)}, u32[]{:S(2)}, u32[]{:S(2)}) collective-permute-start(bf16[4,160,896]{2,1,0:T(8,128)(2,1)} %collective-permute-done.31.refs_5_), channel_id=1, source_target_pairs={{8,0},{9,1},{10,2},{11,3},{12,4},{13,5},{14,6},{15,7}} | collective-permute-start | bytes 3440648 | tf_op jit(solution)/shard_map/ppermute | solution.py:500
  699.9 34.4 %collective-permute-start.33 = (bf16[4,160,896]{2,1,0:T(8,128)(2,1)}, bf16[4,160,896]{2,1,0:T(8,128)(2,1)S(1)}, u32[]{:S(2)}, u32[]{:S(2)}) collective-permute-start(bf16[4,160,896]{2,1,0:T(8,128)(2,1)} %collective-permute-done.30.refs_2_), channel_id=1, source_target_pairs={{16,24},{17,25},{18,26},{19,27},{20,28},{21,29},{22,30},{23,31}} | collective-permute-start | bytes 3440648 | tf_op jit(solution)/shard_map/ppermute | solution.py:499
  706.6 68.5 %collective-permute-start.20 = (bf16[4,224,2560]{2,1,0:T(8,128)(2,1)}, bf16[4,224,2560]{2,1,0:T(8,128)(2,1)}, u32[]{:S(2)}, u32[]{:S(2)}) collective-permute-start(bf16[4,224,2560]{2,1,0:T(8,128)(2,1)} %shard_map.210.refs_0_), channel_id=1, source_target_pairs={{0,4},{4,0},{1,5},{5,1},{2,6},{6,2},{3,7},{7,3},{8,12},{12,8},{9,1... | collective-permute-start | bytes 13762568 | tf_op jit(solution)/shard_map/ppermute | solution.py:61
  736.9 23.4 %collective-permute-start.38 = (bf16[4,160,896]{2,1,0:T(8,128)(2,1)}, bf16[4,160,896]{2,1,0:T(8,128)(2,1)}, u32[]{:S(2)}, u32[]{:S(2)}) collective-permute-start(bf16[4,160,896]{2,1,0:T(8,128)(2,1)} %get-tuple-element.148), channel_id=1, source_target_pairs={{8,0},{16,8},{24,16},{9,1},{17,9},{25,17},{10,2},{18,10},{26,18},{... | collective-permute-start | bytes 3440648 | tf_op jit(solution)/shard_map/ppermute | solution.py:486
  746.3 305.0 %reduce-scatter.9.cloned.1.call-start = ((), (), s32[]{:S(2)}) async-start(), calls=%async_computation.17 | async-start | bytes 5898240 | tf_op jit(solution)/shard_map/reduce_scatter | solution.py:630
  763.1 24.1 %collective-permute-start.40 = (bf16[4,160,896]{2,1,0:T(8,128)(2,1)S(1)}, bf16[4,160,896]{2,1,0:T(8,128)(2,1)S(1)}, u32[]{:S(2)}, u32[]{:S(2)}) collective-permute-start(bf16[4,160,896]{2,1,0:T(8,128)(2,1)S(1)} %fusion.11.refs_0_), channel_id=1, source_target_pairs={{8,0},{16,8},{24,16},{9,1},{17,9},{25,17},{10,2},{18,10},{26,18},{... | collective-permute-start | bytes 3440648 | tf_op jit(solution)/shard_map/ppermute | solution.py:500
  764.4 24.1 %collective-permute-start.39 = (bf16[4,160,896]{2,1,0:T(8,128)(2,1)S(1)}, bf16[4,160,896]{2,1,0:T(8,128)(2,1)S(1)}, u32[]{:S(2)}, u32[]{:S(2)}) collective-permute-start(bf16[4,160,896]{2,1,0:T(8,128)(2,1)S(1)} %fusion.11.refs_0_), channel_id=1, source_target_pairs={{0,8},{8,16},{16,24},{1,9},{9,17},{17,25},{2,10},{10,18},{18,26},{... | collective-permute-start | bytes 3440648 | tf_op jit(solution)/shard_map/ppermute | solution.py:499
  775.1 56.2 %collective-permute-start.45 = (bf16[4,4,160,896]{3,2,1,0:T(8,128)(2,1)}, bf16[4,4,160,896]{3,2,1,0:T(8,128)(2,1)}, u32[]{:S(2)}, u32[]{:S(2)}) collective-permute-start(bf16[4,4,160,896]{3,2,1,0:T(8,128)(2,1)} %shard_map.212.refs_0_), channel_id=1, source_target_pairs={{0,4},{4,0},{1,5},{5,1},{2,6},{6,2},{3,7},{7,3},{8,12},{12,8},{9,1... | collective-permute-start | bytes 13762568 | tf_op jit(solution)/shard_map/ppermute | solution.py:61
  787.2 29.7 %collective-permute-start.43 = (bf16[4,160,896]{2,1,0:T(8,128)(2,1)S(1)}, bf16[4,160,896]{2,1,0:T(8,128)(2,1)}, u32[]{:S(2)}, u32[]{:S(2)}) collective-permute-start(bf16[4,160,896]{2,1,0:T(8,128)(2,1)S(1)} %collective-permute-done.40.refs_4_), channel_id=1, source_target_pairs={{8,0},{16,8},{9,1},{17,9},{10,2},{18,10},{11,3},{19,11},{12,4},{20... | collective-permute-start | bytes 3440648 | tf_op jit(solution)/shard_map/ppermute | solution.py:500
  788.6 28.4 %collective-permute-start.42 = (bf16[4,160,896]{2,1,0:T(8,128)(2,1)S(1)}, bf16[4,160,896]{2,1,0:T(8,128)(2,1)}, u32[]{:S(2)}, u32[]{:S(2)}) collective-permute-start(bf16[4,160,896]{2,1,0:T(8,128)(2,1)S(1)} %collective-permute-done.39.refs_1_), channel_id=1, source_target_pairs={{8,16},{16,24},{9,17},{17,25},{10,18},{18,26},{11,19},{19,27},{12,... | collective-permute-start | bytes 3440648 | tf_op jit(solution)/shard_map/ppermute | solution.py:499
  801.9 22.3 %collective-permute-start.49 = (bf16[80,2560]{1,0:T(8,128)(2,1)S(1)}, bf16[80,2560]{1,0:T(8,128)(2,1)S(1)}, u32[]{:S(2)}, u32[]{:S(2)}) collective-permute-start(bf16[80,2560]{1,0:T(8,128)(2,1)S(1)} %get-tuple-element.152), channel_id=1, source_target_pairs={{24,16},{25,17},{26,18},{27,19},{28,20},{29,21},{30,22},{31,23}} | collective-permute-start | bytes 1228808 | tf_op jit(solution)/shard_map/ppermute | solution.py:486
  821.2 28.6 %collective-permute-start.47 = (bf16[4,160,896]{2,1,0:T(8,128)(2,1)}, bf16[4,160,896]{2,1,0:T(8,128)(2,1)}, u32[]{:S(2)}, u32[]{:S(2)}) collective-permute-start(bf16[4,160,896]{2,1,0:T(8,128)(2,1)} %collective-permute-done.43.refs_5_), channel_id=1, source_target_pairs={{8,0},{9,1},{10,2},{11,3},{12,4},{13,5},{14,6},{15,7}} | collective-permute-start | bytes 3440648 | tf_op jit(solution)/shard_map/ppermute | solution.py:500
  822.5 27.3 %collective-permute-start.46 = (bf16[4,160,896]{2,1,0:T(8,128)(2,1)}, bf16[4,160,896]{2,1,0:T(8,128)(2,1)}, u32[]{:S(2)}, u32[]{:S(2)}) collective-permute-start(bf16[4,160,896]{2,1,0:T(8,128)(2,1)} %collective-permute-done.42.refs_2_), channel_id=1, source_target_pairs={{16,24},{17,25},{18,26},{19,27},{20,28},{21,29},{22,30},{23,31}} | collective-permute-start | bytes 3440648 | tf_op jit(solution)/shard_map/ppermute | solution.py:499
  830.3 27.7 %collective-permute-start.50 = (bf16[80,2560]{1,0:T(8,128)(2,1)S(1)}, bf16[80,2560]{1,0:T(8,128)(2,1)S(1)}, u32[]{:S(2)}, u32[]{:S(2)}) collective-permute-start(bf16[80,2560]{1,0:T(8,128)(2,1)S(1)} %get-tuple-element.153), channel_id=1, source_target_pairs={{16,8},{24,16},{17,9},{25,17},{18,10},{26,18},{19,11},{27,19},{20,... | collective-permute-start | bytes 1228808 | tf_op jit(solution)/shard_map/ppermute | solution.py:486
  855.8 90.7 %collective-permute-start.58 = (bf16[4,4,160,896]{3,2,1,0:T(8,128)(2,1)}, bf16[4,4,160,896]{3,2,1,0:T(8,128)(2,1)}, u32[]{:S(2)}, u32[]{:S(2)}) collective-permute-start(bf16[4,4,160,896]{3,2,1,0:T(8,128)(2,1)} %shard_map.214.refs_0_), channel_id=1, source_target_pairs={{0,4},{4,0},{1,5},{5,1},{2,6},{6,2},{3,7},{7,3},{8,12},{12,8},{9,1... | collective-permute-start | bytes 13762568 | tf_op jit(solution)/shard_map/ppermute | solution.py:61
  874.8 19.6 %collective-permute-start.53 = (bf16[80,2560]{1,0:T(8,128)(2,1)}, bf16[80,2560]{1,0:T(8,128)(2,1)}, u32[]{:S(2)}, u32[]{:S(2)}) collective-permute-start(bf16[80,2560]{1,0:T(8,128)(2,1)} %fusion.42.refs_0_), channel_id=1, source_target_pairs={{8,0},{16,8},{24,16},{9,1},{17,9},{25,17},{10,2},{18,10},{26,18},{... | collective-permute-start | bytes 1228808 | tf_op jit(solution)/shard_map/ppermute | solution.py:500
  876.1 18.4 %collective-permute-start.52 = (bf16[80,2560]{1,0:T(8,128)(2,1)}, bf16[80,2560]{1,0:T(8,128)(2,1)}, u32[]{:S(2)}, u32[]{:S(2)}) collective-permute-start(bf16[80,2560]{1,0:T(8,128)(2,1)} %fusion.42.refs_0_), channel_id=1, source_target_pairs={{0,8},{8,16},{16,24},{1,9},{9,17},{17,25},{2,10},{10,18},{18,26},{... | collective-permute-start | bytes 1228808 | tf_op jit(solution)/shard_map/ppermute | solution.py:499
  912.1 32.8 %collective-permute-start.63 = (bf16[4,160,480]{2,1,0:T(8,128)(2,1)}, bf16[4,160,480]{2,1,0:T(8,128)(2,1)}, u32[]{:S(2)}, u32[]{:S(2)}) collective-permute-start(bf16[4,160,480]{2,1,0:T(8,128)(2,1)} %get-tuple-element.159), channel_id=1, source_target_pairs={{16,8},{24,16},{17,9},{25,17},{18,10},{26,18},{19,11},{27,19},{20,... | collective-permute-start | bytes 1843208 | tf_op jit(solution)/shard_map/ppermute | solution.py:486
  913.6 31.2 %collective-permute-start.57 = (bf16[4,160,480]{2,1,0:T(8,128)(2,1)}, bf16[4,160,480]{2,1,0:T(8,128)(2,1)}, u32[]{:S(2)}, u32[]{:S(2)}) collective-permute-start(bf16[4,160,480]{2,1,0:T(8,128)(2,1)} %get-tuple-element.156), channel_id=1, source_target_pairs={{0,8},{8,16},{1,9},{9,17},{2,10},{10,18},{3,11},{11,19},{4,12},{12... | collective-permute-start | bytes 1843208 | tf_op jit(solution)/shard_map/ppermute | solution.py:485
  944.2 37.7 %collective-permute-start.65 = (bf16[4,80,2560]{2,1,0:T(8,128)(2,1)}, bf16[4,80,2560]{2,1,0:T(8,128)(2,1)}, u32[]{:S(2)}, u32[]{:S(2)}) collective-permute-start(bf16[4,80,2560]{2,1,0:T(8,128)(2,1)} %shard_map.216.refs_0_), channel_id=1, source_target_pairs={{0,4},{4,0},{1,5},{5,1},{2,6},{6,2},{3,7},{7,3},{8,12},{12,8},{9,1... | collective-permute-start | bytes 4915208 | tf_op jit(solution)/shard_map/ppermute | solution.py:61
  958.1 19.0 %collective-permute-start.64 = (bf16[4,160,480]{2,1,0:T(8,128)(2,1)S(1)}, bf16[4,160,480]{2,1,0:T(8,128)(2,1)S(1)}, u32[]{:S(2)}, u32[]{:S(2)}) collective-permute-start(bf16[4,160,480]{2,1,0:T(8,128)(2,1)S(1)} %get-tuple-element.160), channel_id=1, source_target_pairs={{8,0},{16,8},{24,16},{9,1},{17,9},{25,17},{10,2},{18,10},{26,18},{... | collective-permute-start | bytes 1843208 | tf_op jit(solution)/shard_map/ppermute | solution.py:486
  991.4 19.1 %collective-permute-start.69 = (bf16[4,160,480]{2,1,0:T(8,128)(2,1)S(1)}, bf16[4,160,480]{2,1,0:T(8,128)(2,1)S(1)}, u32[]{:S(2)}, u32[]{:S(2)}) collective-permute-start(bf16[4,160,480]{2,1,0:T(8,128)(2,1)S(1)} %all-to-all-done.6.refs_0_), channel_id=1, source_target_pairs={{8,0},{16,8},{24,16},{9,1},{17,9},{25,17},{10,2},{18,10},{26,18},{... | collective-permute-start | bytes 1843208 | tf_op jit(solution)/shard_map/ppermute | solution.py:500
  992.7 19.1 %collective-permute-start.66 = (bf16[4,160,480]{2,1,0:T(8,128)(2,1)S(1)}, bf16[4,160,480]{2,1,0:T(8,128)(2,1)S(1)}, u32[]{:S(2)}, u32[]{:S(2)}) collective-permute-start(bf16[4,160,480]{2,1,0:T(8,128)(2,1)S(1)} %all-to-all-done.6.refs_0_), channel_id=1, source_target_pairs={{0,8},{8,16},{16,24},{1,9},{9,17},{17,25},{2,10},{10,18},{18,26},{... | collective-permute-start | bytes 1843208 | tf_op jit(solution)/shard_map/ppermute | solution.py:499
  1010.5 17.8 %collective-permute-start.70 = (bf16[4,160,480]{2,1,0:T(8,128)(2,1)S(1)}, bf16[4,160,480]{2,1,0:T(8,128)(2,1)S(1)}, u32[]{:S(2)}, u32[]{:S(2)}) collective-permute-start(bf16[4,160,480]{2,1,0:T(8,128)(2,1)S(1)} %collective-permute-done.69.refs_4_), channel_id=1, source_target_pairs={{8,0},{16,8},{9,1},{17,9},{10,2},{18,10},{11,3},{19,11},{12,4},{20... | collective-permute-start | bytes 1843208 | tf_op jit(solution)/shard_map/ppermute | solution.py:500
  (78 other events, 1429.7 us)
Sparse Core Ops, SparseCore 0:
  13.4 68.0 all-gather.4
  156.5 86.9 reduce-scatter.4
  247.2 41.0 all-gather.6
  290.2 41.1 all-gather.8
  361.9 56.5 reduce-scatter.6
  465.0 68.9 all-gather.10
  746.4 63.3 reduce-scatter.10
  870.3 67.6 reduce-scatter.8

commit v3 on v2

--- a/solution.py
+++ b/solution.py
@@ -3,6 +3,7 @@
 import numpy as np
 from jax import lax
 from jax.experimental import pallas as pl
+from jax.experimental.layout import Layout, with_layout_constraint
 from jax.experimental.pallas import tpu as pltpu
 from jax.sharding import Mesh
 from jax.sharding import PartitionSpec as P
@@ -482,6 +483,7 @@
             down = (down.astype(F32) + self.down.astype(F32)).astype(BF16)
         if earlier:
             up, down = after(up, *earlier), after(down, *earlier)
+        self.sent = (up, down)
         self.up = lax.ppermute(up, "z", [(i, i + 1) for i in range(step)])
         self.down = lax.ppermute(down, "z", [(i, i - 1) for i in range(n_z - step, n_z)])
 
@@ -504,8 +506,8 @@
         return [mine] + [swap(mine, "core", e) for e in range(1, lax.axis_size("core"))]
 
 
-def run_sums(sums, waits):
-    previous, slot = None, 0
+def run_sums(previous, sums, waits):
+    slot = previous.n_z
 
     def due():
         return tuple(waits[slot]()) if slot in waits else ()
@@ -513,11 +515,8 @@
     for one in sums:
         n_z = one.n_z
         for step in range(1, n_z):
-            earlier = due()
-            if previous is not None:
-                earlier += (previous.ups[step], previous.downs[step])
-            one.add(step, *earlier)
-            if previous is not None and step + 1 < n_z:
+            one.add(step, *due(), previous.ups[step], previous.downs[step])
+            if step + 1 < n_z:
                 previous.spread(step + 1)
             slot += 1
         one.close()
@@ -587,7 +586,8 @@
     payloads = lax.all_gather(first, in_plane, axis=0, tiled=True)
 
     w_qkv = do(lambda *w: pack_qkv(*w, c, n_f, n_c), w_query, w_key, w_value)
-    w_qkv = lax.all_to_all(w_qkv, "f", 0, 0)
+    w_qkv = lax.all_to_all(with_layout_constraint(w_qkv, Layout((0, 1, 2))), "f", 0, 0)
+    w_qkv = with_layout_constraint(w_qkv, Layout((0, 1, 2)))
     gate_parts, up_parts = do(
         lambda *w: [slice_columns(x, c, n_f, n_c) for x in w], w_gate, w_up
     )
@@ -662,11 +662,22 @@
         grad_g = (grad_mid * up * sigmoid * (1.0 + gate * (1.0 - sigmoid))).astype(BF16)
         return grad_g, (grad_mid * (gate * sigmoid)).astype(BF16)
 
-    grad_g, grad_u = do(work, dy_all, down_rows, gate, up)
-    h_two_parts = do(lambda g, u: (nt(g, gate_full) + nt(u, up_full)).astype(BF16), grad_g, grad_u)
+    grad_down = do(lambda mid, dy: tn(mid, dy).astype(BF16), mid, dy_all)
+    sum_down = ZSum(grad_down.reshape(n_z, hidden // n_z, width), 0)
+    sum_down.add(1)
+    grad_g, grad_u = do(work, after(dy_all, *sum_down.sent), down_rows, gate, up)
+    sum_down.add(2, grad_g, grad_u)
+    h_two_parts = do(
+        lambda g, u: (nt(g, gate_full) + nt(u, up_full)).astype(BF16),
+        after(grad_g, *sum_down.sent), grad_u,
+    )
     h_two_back = reduce_plane(h_two_parts)
-
-    grad_down = tn(mid, dy_all).astype(BF16)
+    for step in range(3, n_z):
+        sum_down.add(step, h_two_parts)
+    sum_down.close()
+    sum_down.spread(1)
+    h_two_back = after(h_two_back, sum_down.own)
+
     grad_gate = tn(h_two, grad_g).astype(BF16)
     grad_up = tn(h_two, grad_u).astype(BF16)
     grad_gain_two, grad_norm = rms_backward(
@@ -718,11 +729,10 @@
 
     gate_shards = to_shards(grad_gate.reshape(n_f, shard, hidden))
     up_shards = to_shards(after(grad_up.reshape(n_f, shard, hidden), gate_shards))
-    sum_down = ZSum(by_z(grad_down, 0), 0)
     sum_gate = ZSum(by_z(gate_shards, 1), 1)
     sum_up = ZSum(by_z(up_shards, 1), 1)
     sum_out = ZSum(by_z(grad_out, 0), 0)
-    sum_qkv = ZSum(by_z(grad_w_qkv.reshape(n_f, shard, qkv_width), 1), 1, to_shards)
+    sum_qkv = ZSum(by_z(to_shards(grad_w_qkv.reshape(n_f, shard, qkv_width)), 1), 1)
     def finish_rows(one):
         cores = one.result()
         piece_rows, columns = cores[0].shape[1:]
@@ -769,8 +779,12 @@
         return which * n_z + min(step, n_z - 1)
 
     run_sums(
-        [sum_down, sum_gate, sum_up, sum_out, sum_qkv],
+        sum_down,
+        [sum_gate, sum_up, sum_out, sum_qkv],
         {
+            slot(2, 0): lambda: [grad_kv],
+            slot(2, 2): lambda: [grad_qkv],
+            slot(2, 3): lambda: [grad_w_qkv, h_one_parts],
             slot(3, 0): down_done,
             slot(3, 2): gate_done,
             slot(4, 2): lambda: [*up_done(), gain_grads],

time: 1080 us -> 1040 us (0.963)
  waiting for transfers between devices: 528 us -> 490 us
  starting transfers between devices: 194 us -> 207 us
    ppermute x15, waiting for transfers between devices: 114 us -> 78.1 us  [spread(): lax.ppermute(down, 'z', [(i, i - 1) for i in range(1, n_z - step + 1)])]
    all_to_all x3, waiting for transfers between devices: 11.1 us -> 33 us  [to_shards(): return lax.all_to_all(grad, 'f', 0, 0)]
    ppermute x15, waiting for transfers between devices: 36.7 us -> 23.1 us  [add(): lax.ppermute(down, 'z', [(i, i - 1) for i in range(n_z - step, n_z)])]
    ppermute x15, starting transfers between devices: 67.5 us -> 81 us  [add(): self.up = lax.ppermute(up, 'z', [(i, i + 1) for i in range(step)])]
    convert_element_type x10 -> x9, other arithmetic: 25.1 us -> 20.8 us  [add(): up = (up.astype(F32) + self.up.astype(F32)).astype(BF16)]
  transfers between devices with their start and end apart: 88 -> 88, of which waited for: 42 -> 40; matrix products, arithmetic and copies ran while one was open for 14% -> 14% of each run, Pallas kernels for 11% -> 12%
where the time goes in v3:
time: 1040 us; the launch traced here: 1030 us
  waiting for transfers between devices  490 us (47%)
  starting transfers between devices  207 us (20%)
  Pallas kernels  132 us (13%)
  matrix products  106 us (10%)
  other arithmetic  46.9 us (5%)
  local copies, waits for them, and re-layouts  34.2 us (3%)
  between operations  15.9 us (2%)
    ppermute x15, waiting for transfers between devices, add(): self.up = lax.ppermute(up, 'z', [(i, i + 1) for i in range(step)])  143 us
    ppermute x15, starting transfers between devices, add(): self.up = lax.ppermute(up, 'z', [(i, i + 1) for i in range(step)])  81 us
    ppermute x15, waiting for transfers between devices, spread(): lax.ppermute(down, 'z', [(i, i - 1) for i in range(1, n_z - step + 1)])  78.1 us
    all_to_all x1, waiting for transfers between devices, per_device(): up_full = lax.all_to_all(up_parts, 'f', 0, 0).reshape(width, hidden)  64.9 us
    all_gather x1, waiting for transfers between devices, per_device(): h_two = lax.all_gather(h_two, in_plane, axis=0, tiled=True)  40.3 us
    ppermute x15, starting transfers between devices, spread(): lax.ppermute(up, 'z', [(i, i + 1) for i in range(step - 1, n_z - 1)])  37.7 us
    dot_general x4, matrix products, nn(): lax.dot_general(a, b, (((1,), (0,)), ((), ())), preferred_element_type=F32)  33.5 us
    all_to_all x3, waiting for transfers between devices, to_shards(): return lax.all_to_all(grad, 'f', 0, 0)  33 us
  transfers between devices with their start and end apart: 88, of which 40 were waited for; matrix products, arithmetic and copies ran while one was open for 14% of the time, Pallas kernels for 12%

profile of v3, /device:TPU:0, one launch (start us, length us, event | category | flops | bytes accessed | tf_op | source)
XLA Modules:
  0.0 1030.9 jit_solution(5973241073710869314)
XLA Ops:
  22.4 5.2 all-to-all-start
  37.5 26.7 %all-to-all-done = bf16[4,640,480]{1,2,0:T(8,128)(2,1)} async-done(((bf16[4,640,480]{1,2,0:T(8,128)(2,1)}), bf16[4,640,480]{1,2,0:T(8,128)(2,1)}, u32[]{:S(2)}, u32[]{:S(2)}) %all-to-all-start) | async-done | bytes 2457632 | tf_op jit(solution)/shard_map/all_to_all | solution.py:589
  68.6 12.8 %all-gather.5.cloned.1.call-done.block = bf16[1280,2560]{1,0:T(8,128)(2,1)} async-done(((bf16[160,2560]{1,0:T(8,128)(2,1)}), bf16[1280,2560]{1,0:T(8,128)(2,1)}) %all-gather.5.cloned.1.call-update) | async-done | bytes 6553616 | tf_op jit(solution)/shard_map/all_gather | solution.py:586
  88.6 11.1 %shard_map.207 = (bf16[1024,2560]{1,0:T(8,128)(2,1)}, bf16[320,1024]{1,0:T(8,128)(2,1)}, bf16[160,1024]{1,0:T(8,128)(2,1)}, f32[40,1024]{1,0:T(8,128)}, f32[40,1024]{1,0:T(8,128)}, /*index=5*/s32[8,1,128]{2,1,0:T(1,128)}) custom-call(s32[1]{0:T(128)} %bitcast.1.where, bf16[1280,2560]{1,0:T(8,128)(2,1)} %all-gather.5.cloned.1.call-done.block, ...), custom_call_target="tpu_custom_call" | custom-call | flops 2516582400 | bytes 10485760 | tf_op jit(solution)/shard_map/pallas_call | solution.py:184
  105.9 5.7 collective-permute-done.2.refs_4_
  111.5 20.4 %collective-permute-done.1.refs_3_ = bf16[160,1024]{1,0:T(8,128)(2,1)} collective-permute-done((bf16[160,1024]{1,0:T(8,128)(2,1)}, bf16[160,1024]{1,0:T(8,128)(2,1)}, u32[]{:S(2)}, u32[]{:S(2)}) %collective-permute-start.1) | collective-permute-done | bytes 327712 | tf_op jit(solution)/shard_map/ppermute | solution.py:460
  131.9 14.0 %shard_map.208 = (f32[320,1024]{1,0:T(8,128)}, bf16[320,1024]{1,0:T(8,128)(2,1)}, f32[4,4,256]{2,1,0:T(4,128)}) custom-call(bf16[320,1024]{1,0:T(8,128)(2,1)} %get-tuple-element.117.refs_0_, bf16[160,1024]{1,0:T(8,128)(2,1)} %get-tuple-element.118.refs_1_, bf16[160,1024]{1,0:T(8,128)(2,1)} %collective-permute-done.refs_2_, ...), custom_call_target="tpu_custom_call" | custom-call | flops 1342177280 | bytes 2621440 | tf_op jit(solution)/shard_map/pallas_call | solution.py:258
  152.0 5.1 all-to-all-start.2
  157.8 64.9 %all-to-all-done.2 = bf16[4,640,896]{2,1,0:T(8,128)(2,1)} async-done(((bf16[4,640,896]{2,1,0:T(8,128)(2,1)}), bf16[4,640,896]{2,1,0:T(8,128)(2,1)}, u32[]{:S(2)}, u32[]{:S(2)}) %all-to-all-start.2) | async-done | bytes 4587552 | tf_op jit(solution)/shard_map/all_to_all | solution.py:639
  222.6 16.4 %reduce-scatter.5.cloned.1.call-done = bf16[128,2560]{1,0:T(8,128)(2,1)} async-done(((bf16[1024,2560]{1,0:T(8,128)(2,1)}), bf16[128,2560]{1,0:T(8,128)(2,1)}) %reduce-scatter.5.cloned.1.call-update) | async-done | bytes 655376 | tf_op jit(solution)/shard_map/reduce_scatter | solution.py:630
  243.6 40.3 %all-gather.7.cloned.1.call-done = bf16[1024,2560]{1,0:T(8,128)(2,1)} async-done(((bf16[128,2560]{1,0:T(8,128)(2,1)}), bf16[1024,2560]{1,0:T(8,128)(2,1)}) %all-gather.7.cloned.1.call-update) | async-done | bytes 5242896 | tf_op jit(solution)/shard_map/all_gather | solution.py:650
  283.9 9.0 fusion.56
  292.9 11.2 %multiply_convert_fusion.2 = (bf16[1024,896]{1,0:T(8,128)(2,1)S(1)}, f32[1024,896]{1,0:T(8,128)}) fusion(f32[1024,896]{1,0:T(8,128)S(1)} %fusion.56, bf16[1024,2560]{1,0:T(8,128)(2,1)S(1)} %copy-done.40, bf16[2560,896]{1,0:T(8,128)(2,1)} %bitcast.14), kind=kOutput, calls=%fused_computation.12 | convolution fusion | flops 4703125504 | bytes 19005440 | tf_op jit(solution)/shard_map/dot_general | solution.py:230
  306.9 20.1 %all-gather.9.cloned.1.call-done = bf16[1024,2560]{1,0:T(8,128)(2,1)} async-done(((bf16[128,2560]{1,0:T(8,128)(2,1)}), bf16[1024,2560]{1,0:T(8,128)(2,1)}) %all-gather.9.cloned.1.call-update) | async-done | bytes 5242896 | tf_op jit(solution)/shard_map/all_gather | solution.py:611
  327.0 7.6 convolution_convert_fusion.5
  339.9 8.8 multiply_convert_fusion
  348.7 15.5 %collective-permute-done.3 = bf16[224,2560]{1,0:T(8,128)(2,1)S(1)} collective-permute-done((bf16[224,2560]{1,0:T(8,128)(2,1)S(1)}, bf16[224,2560]{1,0:T(8,128)(2,1)S(1)}, u32[]{:S(2)}, u32[]{:S(2)}) %collective-permute-start.3) | collective-permute-done | bytes 1146912 | tf_op jit(solution)/shard_map/ppermute | solution.py:487
  364.8 7.5 fusion.57
  372.3 9.7 add_convert_fusion
  382.1 5.5 collective-permute-start.5
  389.3 21.3 %collective-permute-done.5 = bf16[224,2560]{1,0:T(8,128)(2,1)} collective-permute-done((bf16[224,2560]{1,0:T(8,128)(2,1)S(1)}, bf16[224,2560]{1,0:T(8,128)(2,1)}, u32[]{:S(2)}, u32[]{:S(2)}) %collective-permute-start.5) | collective-permute-done | bytes 1146912 | tf_op jit(solution)/shard_map/ppermute | solution.py:487
  414.6 7.9 collective-permute-start.6
  423.8 9.5 convolution_convert_fusion.3
  438.3 6.3 collective-permute-done.6
  462.3 33.0 %all-to-all-done.5 = bf16[4,640,896]{2,1,0:T(8,128)(2,1)} async-done(((bf16[4,640,896]{2,1,0:T(8,128)(2,1)}), bf16[4,640,896]{2,1,0:T(8,128)(2,1)}, u32[]{:S(2)}, u32[]{:S(2)}) %all-to-all-start.5) | async-done | bytes 4587552 | tf_op jit(solution)/shard_map/all_to_all | solution.py:724
  504.6 20.8 %collective-permute-done.21 = bf16[4,160,896]{2,1,0:T(8,128)(2,1)S(1)} collective-permute-done((bf16[4,160,896]{2,1,0:T(8,128)(2,1)S(1)}, bf16[4,160,896]{2,1,0:T(8,128)(2,1)S(1)}, u32[]{:S(2)}, u32[]{:S(2)}) %collective-permute-start.21) | collective-permute-done | bytes 1146912 | tf_op jit(solution)/shard_map/ppermute | solution.py:487
  536.2 19.6 %collective-permute-done.22 = bf16[4,160,896]{2,1,0:T(8,128)(2,1)S(1)} collective-permute-done((bf16[4,160,896]{2,1,0:T(8,128)(2,1)S(1)}, bf16[4,160,896]{2,1,0:T(8,128)(2,1)S(1)}, u32[]{:S(2)}, u32[]{:S(2)}) %collective-permute-start.22) | collective-permute-done | bytes 1146912 | tf_op jit(solution)/shard_map/ppermute | solution.py:487
  561.4 7.6 collective-permute-start.23
  570.2 7.3 convolution_convert_fusion.4
  577.6 5.0 all-to-all-start.6
  582.6 6.9 collective-permute-done.23
  589.5 5.1 collective-permute-done.26
  598.3 5.7 collective-permute-start.27
  604.6 17.8 %collective-permute-done.28.refs_4_ = bf16[4,160,896]{2,1,0:T(8,128)(2,1)S(1)} collective-permute-done((bf16[4,160,896]{2,1,0:T(8,128)(2,1)S(1)}, bf16[4,160,896]{2,1,0:T(8,128)(2,1)S(1)}, u32[]{:S(2)}, u32[]{:S(2)}) %collective-permute-start.28) | collective-permute-done | bytes 1146912 | tf_op jit(solution)/shard_map/ppermute | solution.py:502
  625.3 5.7 convolution_convert_fusion.8.refs_5_
  631.0 17.2 %shard_map.209 = (f32[320,1024]{1,0:T(8,128)}, bf16[4,160,1024]{2,1,0:T(8,128)(2,1)}) custom-call(s32[4]{0:T(128)} %pad_add_fusion.1.where, bf16[320,1024]{1,0:T(8,128)(2,1)} %get-tuple-element.117.refs_0_, bf16[160,1024]{1,0:T(8,128)(2,1)} %get-tuple-element.118.refs_1_, bf16[160,1024]{1,0:T(8,128)(2,1)} %collective-permute-done.refs_2_, ...), custom_call_target="tpu_custom_call" | custom-call | flops 3355443200 | bytes 3932160 | tf_op jit(solution)/shard_map/pallas_call | solution.py:316
  648.2 5.8 all-to-all-start.3
  662.2 5.9 shard_map.210.refs_0_
  672.6 20.7 %collective-permute-done.29 = bf16[4,160,896]{2,1,0:T(8,128)(2,1)S(1)} collective-permute-done((bf16[4,160,896]{2,1,0:T(8,128)(2,1)}, bf16[4,160,896]{2,1,0:T(8,128)(2,1)S(1)}, u32[]{:S(2)}, u32[]{:S(2)}) %collective-permute-start.29) | collective-permute-done | bytes 1146912 | tf_op jit(solution)/shard_map/ppermute | solution.py:487
  696.9 5.4 collective-permute-start.32
  705.7 5.9 convolution_convert_fusion.1
  711.7 6.9 collective-permute-done.32
  722.1 8.4 collective-permute-start.35
  731.8 6.8 shard_map.212.refs_0_
  738.6 5.4 convolution_convert_fusion.6
  752.9 5.7 collective-permute-start.39
  758.5 11.6 %shard_map.211 = f32[1792,2560]{1,0:T(8,128)} custom-call(s32[1]{0:T(128)} %bitcast.2.where, bf16[4,224,2560]{2,1,0:T(8,128)(2,1)} %shard_map.210.refs_0_, bf16[4,224,2560]{2,1,0:T(8,128)(2,1)} %collective-permute-done.20.refs_1_), custom_call_target="tpu_custom_call" | custom-call | bytes 18350080 | tf_op jit(solution)/shard_map/pallas_call | solution.py:441
  779.5 8.5 collective-permute-start.41
  793.6 8.6 collective-permute-done.43.refs_5_
  802.1 6.1 collective-permute-start.44
  815.7 10.0 shard_map.213
  832.7 6.3 shard_map.214.refs_0_
  844.6 8.9 convolution_convert_fusion.2
  861.4 5.3 collective-permute-start.52
  878.0 6.5 collective-permute-start.9
  889.4 10.0 collective-permute-done.54
  902.3 5.1 collective-permute-start.57
  921.2 10.0 shard_map.215
  936.5 7.0 shard_map.217
  943.4 6.3 collective-permute-done.61
  960.4 12.0 %collective-permute-done.69.refs_4_ = bf16[4,160,480]{2,1,0:T(8,128)(2,1)S(1)} collective-permute-done((bf16[4,160,480]{2,1,0:T(8,128)(2,1)S(1)}, bf16[4,160,480]{2,1,0:T(8,128)(2,1)S(1)}, u32[]{:S(2)}, u32[]{:S(2)}) %collective-permute-start.69) | collective-permute-done | bytes 614432 | tf_op jit(solution)/shard_map/ppermute | solution.py:502
  974.4 14.9 %collective-permute-done.70.refs_5_ = bf16[4,160,480]{2,1,0:T(8,128)(2,1)S(1)} collective-permute-done((bf16[4,160,480]{2,1,0:T(8,128)(2,1)S(1)}, bf16[4,160,480]{2,1,0:T(8,128)(2,1)S(1)}, u32[]{:S(2)}, u32[]{:S(2)}) %collective-permute-start.70) | collective-permute-done | bytes 614432 | tf_op jit(solution)/shard_map/ppermute | solution.py:502
  991.5 13.8 %collective-permute-done.71.refs_6_ = bf16[4,160,480]{2,1,0:T(8,128)(2,1)S(1)} collective-permute-done((bf16[4,160,480]{2,1,0:T(8,128)(2,1)S(1)}, bf16[4,160,480]{2,1,0:T(8,128)(2,1)S(1)}, u32[]{:S(2)}, u32[]{:S(2)}) %collective-permute-start.71) | collective-permute-done | bytes 614432 | tf_op jit(solution)/shard_map/ppermute | solution.py:502
  1016.7 7.2 shard_map.219
  (342 shorter events, 265.7 us)
Async XLA Ops:
  7.2 74.3 %all-gather.5.cloned.1.call-start = ((), (), s32[]{:S(2)}) async-start(), calls=%async_computation.11 | async-start | bytes 7372800 | tf_op jit(solution)/shard_map/all_gather | solution.py:586
  22.4 41.8 %all-to-all-start = ((bf16[4,640,480]{1,2,0:T(8,128)(2,1)}), bf16[4,640,480]{1,2,0:T(8,128)(2,1)}, u32[]{:S(2)}, u32[]{:S(2)}) async-start(bf16[4,640,480]{1,2,0:T(8,128)(2,1)} %copy.65), calls=%async_computation | async-start | bytes 4915200 | tf_op jit(solution)/shard_map/all_to_all | solution.py:589
  81.4 64.5 %all-to-all-start.1 = ((bf16[4,640,896]{2,1,0:T(8,128)(2,1)}), bf16[4,640,896]{2,1,0:T(8,128)(2,1)}, u32[]{:S(2)}, u32[]{:S(2)}) async-start(bf16[4,640,896]{2,1,0:T(8,128)(2,1)} %shard_map.205), calls=%async_computation.1 | async-start | bytes 9175040 | tf_op jit(solution)/shard_map/all_to_all | solution.py:604
  86.4 152.7 %reduce-scatter.5.cloned.1.call-start = ((), (), s32[]{:S(2)}) async-start(), calls=%async_computation.12 | async-start | bytes 5898240 | tf_op jit(solution)/shard_map/reduce_scatter | solution.py:630
  103.1 28.8 %collective-permute-start.1 = (bf16[160,1024]{1,0:T(8,128)(2,1)}, bf16[160,1024]{1,0:T(8,128)(2,1)}, u32[]{:S(2)}, u32[]{:S(2)}) collective-permute-start(bf16[160,1024]{1,0:T(8,128)(2,1)} %get-tuple-element.118.refs_1_), channel_id=1, source_target_pairs={{0,16},{8,24},{16,0},{24,8},{1,17},{9,25},{17,1},{25,9},{2,18},{10... | collective-permute-start | bytes 983048 | tf_op jit(solution)/shard_map/ppermute | solution.py:460
  103.1 28.8 %collective-permute-start = (bf16[160,1024]{1,0:T(8,128)(2,1)}, bf16[160,1024]{1,0:T(8,128)(2,1)}, u32[]{:S(2)}, u32[]{:S(2)}) collective-permute-start(bf16[160,1024]{1,0:T(8,128)(2,1)} %get-tuple-element.118.refs_1_), channel_id=1, source_target_pairs={{0,8},{8,16},{16,24},{24,0},{1,9},{9,17},{17,25},{25,1},{2,10},{10... | collective-permute-start | bytes 983048 | tf_op jit(solution)/shard_map/ppermute | solution.py:460
  152.0 70.7 %all-to-all-start.2 = ((bf16[4,640,896]{2,1,0:T(8,128)(2,1)}), bf16[4,640,896]{2,1,0:T(8,128)(2,1)}, u32[]{:S(2)}, u32[]{:S(2)}) async-start(bf16[4,640,896]{2,1,0:T(8,128)(2,1)} %shard_map.206), calls=%async_computation.3 | async-start | bytes 9175040 | tf_op jit(solution)/shard_map/all_to_all | solution.py:639
  157.1 126.8 %all-gather.7.cloned.1.call-start = ((), (), s32[]{:S(2)}) async-start(), calls=%async_computation.13 | async-start | bytes 5898240 | tf_op jit(solution)/shard_map/all_gather | solution.py:650
  242.7 84.3 %all-gather.9.cloned.1.call-start = ((), (), s32[]{:S(2)}) async-start(), calls=%async_computation.14 | async-start | bytes 5898240 | tf_op jit(solution)/shard_map/all_gather | solution.py:611
  243.3 209.7 %reduce-scatter.7.cloned.1.call-start = ((), (), s32[]{:S(2)}) async-start(), calls=%async_computation.15 | async-start | bytes 5898240 | tf_op jit(solution)/shard_map/reduce_scatter | solution.py:630
  335.6 28.6 %collective-permute-start.3 = (bf16[224,2560]{1,0:T(8,128)(2,1)S(1)}, bf16[224,2560]{1,0:T(8,128)(2,1)S(1)}, u32[]{:S(2)}, u32[]{:S(2)}) collective-permute-start(bf16[224,2560]{1,0:T(8,128)(2,1)S(1)} %get-tuple-element.210), channel_id=1, source_target_pairs={{0,8},{1,9},{2,10},{3,11},{4,12},{5,13},{6,14},{7,15}} | collective-permute-start | bytes 3440648 | tf_op jit(solution)/shard_map/ppermute | solution.py:487
  382.1 28.5 %collective-permute-start.5 = (bf16[224,2560]{1,0:T(8,128)(2,1)S(1)}, bf16[224,2560]{1,0:T(8,128)(2,1)}, u32[]{:S(2)}, u32[]{:S(2)}) collective-permute-start(bf16[224,2560]{1,0:T(8,128)(2,1)S(1)} %get-tuple-element.144), channel_id=1, source_target_pairs={{0,8},{8,16},{1,9},{9,17},{2,10},{10,18},{3,11},{11,19},{4,12},{12... | collective-permute-start | bytes 3440648 | tf_op jit(solution)/shard_map/ppermute | solution.py:487
  387.6 23.0 %collective-permute-start.7 = (bf16[224,2560]{1,0:T(8,128)(2,1)S(1)}, bf16[224,2560]{1,0:T(8,128)(2,1)}, u32[]{:S(2)}, u32[]{:S(2)}) collective-permute-start(bf16[224,2560]{1,0:T(8,128)(2,1)S(1)} %get-tuple-element.145), channel_id=1, source_target_pairs={{16,8},{24,16},{17,9},{25,17},{18,10},{26,18},{19,11},{27,19},{20,... | collective-permute-start | bytes 3440648 | tf_op jit(solution)/shard_map/ppermute | solution.py:488
  414.6 30.0 %collective-permute-start.6 = (bf16[224,2560]{1,0:T(8,128)(2,1)}, bf16[224,2560]{1,0:T(8,128)(2,1)}, u32[]{:S(2)}, u32[]{:S(2)}) collective-permute-start(bf16[224,2560]{1,0:T(8,128)(2,1)} %get-tuple-element.149), channel_id=1, source_target_pairs={{0,8},{8,16},{16,24},{1,9},{9,17},{17,25},{2,10},{10,18},{18,26},{... | collective-permute-start | bytes 3440648 | tf_op jit(solution)/shard_map/ppermute | solution.py:487
  422.5 27.0 %collective-permute-start.8 = (bf16[224,2560]{1,0:T(8,128)(2,1)S(1)}, bf16[224,2560]{1,0:T(8,128)(2,1)}, u32[]{:S(2)}, u32[]{:S(2)}) collective-permute-start(bf16[224,2560]{1,0:T(8,128)(2,1)S(1)} %get-tuple-element.150), channel_id=1, source_target_pairs={{8,0},{16,8},{24,16},{9,1},{17,9},{25,17},{10,2},{18,10},{26,18},{... | collective-permute-start | bytes 3440648 | tf_op jit(solution)/shard_map/ppermute | solution.py:488
  433.3 61.9 %all-to-all-start.5 = ((bf16[4,640,896]{2,1,0:T(8,128)(2,1)}), bf16[4,640,896]{2,1,0:T(8,128)(2,1)}, u32[]{:S(2)}, u32[]{:S(2)}) async-start(bf16[4,640,896]{2,1,0:T(8,128)(2,1)} %bitcast.267), calls=%async_computation.9 | async-start | bytes 9175040 | tf_op jit(solution)/shard_map/all_to_all | solution.py:724
  438.2 187.0 %all-gather.11.cloned.1.call-start = ((), (), s32[]{:S(2)}) async-start(), calls=%async_computation.16 | async-start | bytes 5898240 | tf_op jit(solution)/shard_map/all_gather | solution.py:689
  456.2 41.0 %collective-permute-start.17 = (bf16[224,2560]{1,0:T(8,128)(2,1)}, bf16[224,2560]{1,0:T(8,128)(2,1)S(1)}, u32[]{:S(2)}, u32[]{:S(2)}) collective-permute-start(bf16[224,2560]{1,0:T(8,128)(2,1)} %fusion.15.refs_0_), channel_id=1, source_target_pairs={{8,0},{16,8},{24,16},{9,1},{17,9},{25,17},{10,2},{18,10},{26,18},{... | collective-permute-start | bytes 3440648 | tf_op jit(solution)/shard_map/ppermute | solution.py:502
  457.6 39.5 %collective-permute-start.14 = (bf16[224,2560]{1,0:T(8,128)(2,1)}, bf16[224,2560]{1,0:T(8,128)(2,1)S(1)}, u32[]{:S(2)}, u32[]{:S(2)}) collective-permute-start(bf16[224,2560]{1,0:T(8,128)(2,1)} %fusion.15.refs_0_), channel_id=1, source_target_pairs={{0,8},{8,16},{16,24},{1,9},{9,17},{17,25},{2,10},{10,18},{18,26},{... | collective-permute-start | bytes 3440648 | tf_op jit(solution)/shard_map/ppermute | solution.py:501
  497.2 28.2 %collective-permute-start.21 = (bf16[4,160,896]{2,1,0:T(8,128)(2,1)S(1)}, bf16[4,160,896]{2,1,0:T(8,128)(2,1)S(1)}, u32[]{:S(2)}, u32[]{:S(2)}) collective-permute-start(bf16[4,160,896]{2,1,0:T(8,128)(2,1)S(1)} %get-tuple-element.156), channel_id=1, source_target_pairs={{0,8},{1,9},{2,10},{3,11},{4,12},{5,13},{6,14},{7,15}} | collective-permute-start | bytes 3440648 | tf_op jit(solution)/shard_map/ppermute | solution.py:487
  501.8 23.6 %collective-permute-start.24 = (bf16[4,160,896]{2,1,0:T(8,128)(2,1)S(1)}, bf16[4,160,896]{2,1,0:T(8,128)(2,1)S(1)}, u32[]{:S(2)}, u32[]{:S(2)}) collective-permute-start(bf16[4,160,896]{2,1,0:T(8,128)(2,1)S(1)} %get-tuple-element.159), channel_id=1, source_target_pairs={{24,16},{25,17},{26,18},{27,19},{28,20},{29,21},{30,22},{31,23}} | collective-permute-start | bytes 3440648 | tf_op jit(solution)/shard_map/ppermute | solution.py:488
  502.5 27.8 %collective-permute-start.18 = (bf16[224,2560]{1,0:T(8,128)(2,1)S(1)}, bf16[224,2560]{1,0:T(8,128)(2,1)S(1)}, u32[]{:S(2)}, u32[]{:S(2)}) collective-permute-start(bf16[224,2560]{1,0:T(8,128)(2,1)S(1)} %collective-permute-done.17.refs_4_), channel_id=1, source_target_pairs={{8,0},{16,8},{9,1},{17,9},{10,2},{18,10},{11,3},{19,11},{12,4},{20... | collective-permute-start | bytes 3440648 | tf_op jit(solution)/shard_map/ppermute | solution.py:502
  503.8 26.5 %collective-permute-start.15 = (bf16[224,2560]{1,0:T(8,128)(2,1)S(1)}, bf16[224,2560]{1,0:T(8,128)(2,1)S(1)}, u32[]{:S(2)}, u32[]{:S(2)}) collective-permute-start(bf16[224,2560]{1,0:T(8,128)(2,1)S(1)} %collective-permute-done.14.refs_1_), channel_id=1, source_target_pairs={{8,16},{16,24},{9,17},{17,25},{10,18},{18,26},{11,19},{19,27},{12,... | collective-permute-start | bytes 3440648 | tf_op jit(solution)/shard_map/ppermute | solution.py:501
  530.3 25.5 %collective-permute-start.22 = (bf16[4,160,896]{2,1,0:T(8,128)(2,1)S(1)}, bf16[4,160,896]{2,1,0:T(8,128)(2,1)S(1)}, u32[]{:S(2)}, u32[]{:S(2)}) collective-permute-start(bf16[4,160,896]{2,1,0:T(8,128)(2,1)S(1)} %get-tuple-element.157), channel_id=1, source_target_pairs={{0,8},{8,16},{1,9},{9,17},{2,10},{10,18},{3,11},{11,19},{4,12},{12... | collective-permute-start | bytes 3440648 | tf_op jit(solution)/shard_map/ppermute | solution.py:487
  533.4 22.4 %collective-permute-start.25 = (bf16[4,160,896]{2,1,0:T(8,128)(2,1)S(1)}, bf16[4,160,896]{2,1,0:T(8,128)(2,1)S(1)}, u32[]{:S(2)}, u32[]{:S(2)}) collective-permute-start(bf16[4,160,896]{2,1,0:T(8,128)(2,1)S(1)} %get-tuple-element.160), channel_id=1, source_target_pairs={{16,8},{24,16},{17,9},{25,17},{18,10},{26,18},{19,11},{27,19},{20,... | collective-permute-start | bytes 3440648 | tf_op jit(solution)/shard_map/ppermute | solution.py:488
  534.2 27.2 %collective-permute-start.19 = (bf16[224,2560]{1,0:T(8,128)(2,1)S(1)}, bf16[224,2560]{1,0:T(8,128)(2,1)S(1)}, u32[]{:S(2)}, u32[]{:S(2)}) collective-permute-start(bf16[224,2560]{1,0:T(8,128)(2,1)S(1)} %collective-permute-done.18.refs_5_), channel_id=1, source_target_pairs={{8,0},{9,1},{10,2},{11,3},{12,4},{13,5},{14,6},{15,7}} | collective-permute-start | bytes 3440648 | tf_op jit(solution)/shard_map/ppermute | solution.py:502
  535.5 25.9 %collective-permute-start.16 = (bf16[224,2560]{1,0:T(8,128)(2,1)S(1)}, bf16[224,2560]{1,0:T(8,128)(2,1)S(1)}, u32[]{:S(2)}, u32[]{:S(2)}) collective-permute-start(bf16[224,2560]{1,0:T(8,128)(2,1)S(1)} %collective-permute-done.15.refs_2_), channel_id=1, source_target_pairs={{16,24},{17,25},{18,26},{19,27},{20,28},{21,29},{22,30},{23,31}} | collective-permute-start | bytes 3440648 | tf_op jit(solution)/shard_map/ppermute | solution.py:501
  561.4 28.1 %collective-permute-start.23 = (bf16[4,160,896]{2,1,0:T(8,128)(2,1)}, bf16[4,160,896]{2,1,0:T(8,128)(2,1)}, u32[]{:S(2)}, u32[]{:S(2)}) collective-permute-start(bf16[4,160,896]{2,1,0:T(8,128)(2,1)} %get-tuple-element.158), channel_id=1, source_target_pairs={{0,8},{8,16},{16,24},{1,9},{9,17},{17,25},{2,10},{10,18},{18,26},{... | collective-permute-start | bytes 3440648 | tf_op jit(solution)/shard_map/ppermute | solution.py:487
  568.9 25.7 %collective-permute-start.26 = (bf16[4,160,896]{2,1,0:T(8,128)(2,1)}, bf16[4,160,896]{2,1,0:T(8,128)(2,1)}, u32[]{:S(2)}, u32[]{:S(2)}) collective-permute-start(bf16[4,160,896]{2,1,0:T(8,128)(2,1)} %get-tuple-element.161), channel_id=1, source_target_pairs={{8,0},{16,8},{24,16},{9,1},{17,9},{25,17},{10,2},{18,10},{26,18},{... | collective-permute-start | bytes 3440648 | tf_op jit(solution)/shard_map/ppermute | solution.py:488
  577.6 70.7 %all-to-all-start.6 = ((bf16[4,640,896]{2,1,0:T(8,128)(2,1)}), bf16[4,640,896]{2,1,0:T(8,128)(2,1)}, u32[]{:S(2)}, u32[]{:S(2)}) async-start(bf16[4,640,896]{2,1,0:T(8,128)(2,1)} %bitcast.266), calls=%async_computation.10 | async-start | bytes 9175040 | tf_op jit(solution)/shard_map/all_to_all | solution.py:724
  597.0 25.3 %collective-permute-start.28 = (bf16[4,160,896]{2,1,0:T(8,128)(2,1)S(1)}, bf16[4,160,896]{2,1,0:T(8,128)(2,1)S(1)}, u32[]{:S(2)}, u32[]{:S(2)}) collective-permute-start(bf16[4,160,896]{2,1,0:T(8,128)(2,1)S(1)} %fusion.7.refs_0_), channel_id=1, source_target_pairs={{8,0},{16,8},{24,16},{9,1},{17,9},{25,17},{10,2},{18,10},{26,18},{... | collective-permute-start | bytes 3440648 | tf_op jit(solution)/shard_map/ppermute | solution.py:502
  598.3 25.3 %collective-permute-start.27 = (bf16[4,160,896]{2,1,0:T(8,128)(2,1)S(1)}, bf16[4,160,896]{2,1,0:T(8,128)(2,1)}, u32[]{:S(2)}, u32[]{:S(2)}) collective-permute-start(bf16[4,160,896]{2,1,0:T(8,128)(2,1)S(1)} %fusion.7.refs_0_), channel_id=1, source_target_pairs={{0,8},{8,16},{16,24},{1,9},{9,17},{17,25},{2,10},{10,18},{18,26},{... | collective-permute-start | bytes 3440648 | tf_op jit(solution)/shard_map/ppermute | solution.py:501
  622.3 45.8 %collective-permute-start.31 = (bf16[4,160,896]{2,1,0:T(8,128)(2,1)S(1)}, bf16[4,160,896]{2,1,0:T(8,128)(2,1)}, u32[]{:S(2)}, u32[]{:S(2)}) collective-permute-start(bf16[4,160,896]{2,1,0:T(8,128)(2,1)S(1)} %collective-permute-done.28.refs_4_), channel_id=1, source_target_pairs={{8,0},{16,8},{9,1},{17,9},{10,2},{18,10},{11,3},{19,11},{12,4},{20... | collective-permute-start | bytes 3440648 | tf_op jit(solution)/shard_map/ppermute | solution.py:502
  623.6 46.0 %collective-permute-start.30 = (bf16[4,160,896]{2,1,0:T(8,128)(2,1)}, bf16[4,160,896]{2,1,0:T(8,128)(2,1)}, u32[]{:S(2)}, u32[]{:S(2)}) collective-permute-start(bf16[4,160,896]{2,1,0:T(8,128)(2,1)} %collective-permute-done.27.refs_1_), channel_id=1, source_target_pairs={{8,16},{16,24},{9,17},{17,25},{10,18},{18,26},{11,19},{19,27},{12,... | collective-permute-start | bytes 3440648 | tf_op jit(solution)/shard_map/ppermute | solution.py:501
  648.2 55.7 %all-to-all-start.3 = ((bf16[4,160,1024]{2,1,0:T(8,128)(2,1)}), bf16[4,160,1024]{2,1,0:T(8,128)(2,1)S(1)}, u32[]{:S(2)}, u32[]{:S(2)}) async-start(bf16[4,160,1024]{2,1,0:T(8,128)(2,1)} %get-tuple-element.154), calls=%async_computation.6 | async-start | bytes 2621440 | tf_op jit(solution)/shard_map/all_to_all | solution.py:695
  654.0 222.4 %reduce-scatter.11.cloned.1.call-start = ((), (), s32[]{:S(2)}) async-start(), calls=%async_computation.18 | async-start | bytes 5898240 | tf_op jit(solution)/shard_map/reduce_scatter | solution.py:630
  656.8 36.5 %collective-permute-start.29 = (bf16[4,160,896]{2,1,0:T(8,128)(2,1)}, bf16[4,160,896]{2,1,0:T(8,128)(2,1)S(1)}, u32[]{:S(2)}, u32[]{:S(2)}) collective-permute-start(bf16[4,160,896]{2,1,0:T(8,128)(2,1)} %get-tuple-element.162), channel_id=1, source_target_pairs={{0,8},{1,9},{2,10},{3,11},{4,12},{5,13},{6,14},{7,15}} | collective-permute-start | bytes 3440648 | tf_op jit(solution)/shard_map/ppermute | solution.py:487
  661.4 31.9 %collective-permute-start.36 = (bf16[4,160,896]{2,1,0:T(8,128)(2,1)S(1)}, bf16[4,160,896]{2,1,0:T(8,128)(2,1)S(1)}, u32[]{:S(2)}, u32[]{:S(2)}) collective-permute-start(bf16[4,160,896]{2,1,0:T(8,128)(2,1)S(1)} %get-tuple-element.165), channel_id=1, source_target_pairs={{24,16},{25,17},{26,18},{27,19},{28,20},{29,21},{30,22},{31,23}} | collective-permute-start | bytes 3440648 | tf_op jit(solution)/shard_map/ppermute | solution.py:488
  668.1 90.4 %collective-permute-start.20 = (bf16[4,224,2560]{2,1,0:T(8,128)(2,1)}, bf16[4,224,2560]{2,1,0:T(8,128)(2,1)}, u32[]{:S(2)}, u32[]{:S(2)}) collective-permute-start(bf16[4,224,2560]{2,1,0:T(8,128)(2,1)} %shard_map.210.refs_0_), channel_id=1, source_target_pairs={{0,4},{4,0},{1,5},{5,1},{2,6},{6,2},{3,7},{7,3},{8,12},{12,8},{9,1... | collective-permute-start | bytes 13762568 | tf_op jit(solution)/shard_map/ppermute | solution.py:62
  668.1 53.9 %collective-permute-start.34 = (bf16[4,160,896]{2,1,0:T(8,128)(2,1)}, bf16[4,160,896]{2,1,0:T(8,128)(2,1)}, u32[]{:S(2)}, u32[]{:S(2)}) collective-permute-start(bf16[4,160,896]{2,1,0:T(8,128)(2,1)} %collective-permute-done.31.refs_5_), channel_id=1, source_target_pairs={{8,0},{9,1},{10,2},{11,3},{12,4},{13,5},{14,6},{15,7}} | collective-permute-start | bytes 3440648 | tf_op jit(solution)/shard_map/ppermute | solution.py:502
  669.6 52.5 %collective-permute-start.33 = (bf16[4,160,896]{2,1,0:T(8,128)(2,1)}, bf16[4,160,896]{2,1,0:T(8,128)(2,1)}, u32[]{:S(2)}, u32[]{:S(2)}) collective-permute-start(bf16[4,160,896]{2,1,0:T(8,128)(2,1)} %collective-permute-done.30.refs_2_), channel_id=1, source_target_pairs={{16,24},{17,25},{18,26},{19,27},{20,28},{21,29},{22,30},{23,31}} | collective-permute-start | bytes 3440648 | tf_op jit(solution)/shard_map/ppermute | solution.py:501
  696.9 21.7 %collective-permute-start.32 = (bf16[4,160,896]{2,1,0:T(8,128)(2,1)}, bf16[4,160,896]{2,1,0:T(8,128)(2,1)}, u32[]{:S(2)}, u32[]{:S(2)}) collective-permute-start(bf16[4,160,896]{2,1,0:T(8,128)(2,1)} %get-tuple-element.163), channel_id=1, source_target_pairs={{0,8},{8,16},{1,9},{9,17},{2,10},{10,18},{3,11},{11,19},{4,12},{12... | collective-permute-start | bytes 3440648 | tf_op jit(solution)/shard_map/ppermute | solution.py:487
  722.1 23.5 %collective-permute-start.35 = (bf16[4,160,896]{2,1,0:T(8,128)(2,1)S(1)}, bf16[4,160,896]{2,1,0:T(8,128)(2,1)S(1)}, u32[]{:S(2)}, u32[]{:S(2)}) collective-permute-start(bf16[4,160,896]{2,1,0:T(8,128)(2,1)S(1)} %get-tuple-element.164), channel_id=1, source_target_pairs={{0,8},{8,16},{16,24},{1,9},{9,17},{17,25},{2,10},{10,18},{18,26},{... | collective-permute-start | bytes 3440648 | tf_op jit(solution)/shard_map/ppermute | solution.py:487
  730.5 19.3 %collective-permute-start.38 = (bf16[4,160,896]{2,1,0:T(8,128)(2,1)S(1)}, bf16[4,160,896]{2,1,0:T(8,128)(2,1)S(1)}, u32[]{:S(2)}, u32[]{:S(2)}) collective-permute-start(bf16[4,160,896]{2,1,0:T(8,128)(2,1)S(1)} %get-tuple-element.167), channel_id=1, source_target_pairs={{8,0},{16,8},{24,16},{9,1},{17,9},{25,17},{10,2},{18,10},{26,18},{... | collective-permute-start | bytes 3440648 | tf_op jit(solution)/shard_map/ppermute | solution.py:488
  738.6 77.1 %collective-permute-start.45 = (bf16[4,4,160,896]{3,2,1,0:T(8,128)(2,1)}, bf16[4,4,160,896]{3,2,1,0:T(8,128)(2,1)}, u32[]{:S(2)}, u32[]{:S(2)}) collective-permute-start(bf16[4,4,160,896]{3,2,1,0:T(8,128)(2,1)} %shard_map.212.refs_0_), channel_id=1, source_target_pairs={{0,4},{4,0},{1,5},{5,1},{2,6},{6,2},{3,7},{7,3},{8,12},{12,8},{9,1... | collective-permute-start | bytes 13762568 | tf_op jit(solution)/shard_map/ppermute | solution.py:62
  751.4 25.0 %collective-permute-start.40 = (bf16[4,160,896]{2,1,0:T(8,128)(2,1)S(1)}, bf16[4,160,896]{2,1,0:T(8,128)(2,1)S(1)}, u32[]{:S(2)}, u32[]{:S(2)}) collective-permute-start(bf16[4,160,896]{2,1,0:T(8,128)(2,1)S(1)} %fusion.11.refs_0_), channel_id=1, source_target_pairs={{8,0},{16,8},{24,16},{9,1},{17,9},{25,17},{10,2},{18,10},{26,18},{... | collective-permute-start | bytes 3440648 | tf_op jit(solution)/shard_map/ppermute | solution.py:502
  752.9 24.9 %collective-permute-start.39 = (bf16[4,160,896]{2,1,0:T(8,128)(2,1)S(1)}, bf16[4,160,896]{2,1,0:T(8,128)(2,1)}, u32[]{:S(2)}, u32[]{:S(2)}) collective-permute-start(bf16[4,160,896]{2,1,0:T(8,128)(2,1)S(1)} %fusion.11.refs_0_), channel_id=1, source_target_pairs={{0,8},{8,16},{16,24},{1,9},{9,17},{17,25},{2,10},{10,18},{18,26},{... | collective-permute-start | bytes 3440648 | tf_op jit(solution)/shard_map/ppermute | solution.py:501
  776.5 25.7 %collective-permute-start.43 = (bf16[4,160,896]{2,1,0:T(8,128)(2,1)S(1)}, bf16[4,160,896]{2,1,0:T(8,128)(2,1)}, u32[]{:S(2)}, u32[]{:S(2)}) collective-permute-start(bf16[4,160,896]{2,1,0:T(8,128)(2,1)S(1)} %collective-permute-done.40.refs_4_), channel_id=1, source_target_pairs={{8,0},{16,8},{9,1},{17,9},{10,2},{18,10},{11,3},{19,11},{12,4},{20... | collective-permute-start | bytes 3440648 | tf_op jit(solution)/shard_map/ppermute | solution.py:502
  777.8 24.4 %collective-permute-start.42 = (bf16[4,160,896]{2,1,0:T(8,128)(2,1)}, bf16[4,160,896]{2,1,0:T(8,128)(2,1)}, u32[]{:S(2)}, u32[]{:S(2)}) collective-permute-start(bf16[4,160,896]{2,1,0:T(8,128)(2,1)} %collective-permute-done.39.refs_1_), channel_id=1, source_target_pairs={{8,16},{16,24},{9,17},{17,25},{10,18},{18,26},{11,19},{19,27},{12,... | collective-permute-start | bytes 3440648 | tf_op jit(solution)/shard_map/ppermute | solution.py:501
  788.0 23.2 %collective-permute-start.49 = (bf16[80,2560]{1,0:T(8,128)(2,1)S(1)}, bf16[80,2560]{1,0:T(8,128)(2,1)S(1)}, u32[]{:S(2)}, u32[]{:S(2)}) collective-permute-start(bf16[80,2560]{1,0:T(8,128)(2,1)S(1)} %get-tuple-element.172), channel_id=1, source_target_pairs={{24,16},{25,17},{26,18},{27,19},{28,20},{29,21},{30,22},{31,23}} | collective-permute-start | bytes 1228808 | tf_op jit(solution)/shard_map/ppermute | solution.py:488
  808.2 24.5 %collective-permute-start.47 = (bf16[4,160,896]{2,1,0:T(8,128)(2,1)}, bf16[4,160,896]{2,1,0:T(8,128)(2,1)}, u32[]{:S(2)}, u32[]{:S(2)}) collective-permute-start(bf16[4,160,896]{2,1,0:T(8,128)(2,1)} %collective-permute-done.43.refs_5_), channel_id=1, source_target_pairs={{8,0},{9,1},{10,2},{11,3},{12,4},{13,5},{14,6},{15,7}} | collective-permute-start | bytes 3440648 | tf_op jit(solution)/shard_map/ppermute | solution.py:502
  809.5 23.2 %collective-permute-start.46 = (bf16[4,160,896]{2,1,0:T(8,128)(2,1)}, bf16[4,160,896]{2,1,0:T(8,128)(2,1)}, u32[]{:S(2)}, u32[]{:S(2)}) collective-permute-start(bf16[4,160,896]{2,1,0:T(8,128)(2,1)} %collective-permute-done.42.refs_2_), channel_id=1, source_target_pairs={{16,24},{17,25},{18,26},{19,27},{20,28},{21,29},{22,30},{23,31}} | collective-permute-start | bytes 3440648 | tf_op jit(solution)/shard_map/ppermute | solution.py:501
  814.6 17.3 %collective-permute-start.50 = (bf16[80,2560]{1,0:T(8,128)(2,1)S(1)}, bf16[80,2560]{1,0:T(8,128)(2,1)S(1)}, u32[]{:S(2)}, u32[]{:S(2)}) collective-permute-start(bf16[80,2560]{1,0:T(8,128)(2,1)S(1)} %get-tuple-element.173), channel_id=1, source_target_pairs={{16,8},{24,16},{17,9},{25,17},{18,10},{26,18},{19,11},{27,19},{20,... | collective-permute-start | bytes 1228808 | tf_op jit(solution)/shard_map/ppermute | solution.py:488
  827.3 39.7 %all-to-all-start.4 = ((bf16[4,640,480]{1,2,0:T(8,128)(2,1)}), bf16[4,640,480]{1,2,0:T(8,128)(2,1)}, u32[]{:S(2)}, u32[]{:S(2)}) async-start(bf16[4,640,480]{1,2,0:T(8,128)(2,1)} %bitcast.247), calls=%async_computation.8 | async-start | bytes 4915200 | tf_op jit(solution)/shard_map/all_to_all | solution.py:724
  831.9 179.5 %reduce-scatter.9.cloned.1.call-start = ((), (), s32[]{:S(2)}) async-start(), calls=%async_computation.17 | async-start | bytes 5898240 | tf_op jit(solution)/shard_map/reduce_scatter | solution.py:630
  839.0 82.3 %collective-permute-start.58 = (bf16[4,4,160,896]{3,2,1,0:T(8,128)(2,1)}, bf16[4,4,160,896]{3,2,1,0:T(8,128)(2,1)}, u32[]{:S(2)}, u32[]{:S(2)}) collective-permute-start(bf16[4,4,160,896]{3,2,1,0:T(8,128)(2,1)} %shard_map.214.refs_0_), channel_id=1, source_target_pairs={{0,4},{4,0},{1,5},{5,1},{2,6},{6,2},{3,7},{7,3},{8,12},{12,8},{9,1... | collective-permute-start | bytes 13762568 | tf_op jit(solution)/shard_map/ppermute | solution.py:62
  888.6 18.8 %collective-permute-start.59 = (bf16[80,2560]{1,0:T(8,128)(2,1)}, bf16[80,2560]{1,0:T(8,128)(2,1)S(1)}, u32[]{:S(2)}, u32[]{:S(2)}) collective-permute-start(bf16[80,2560]{1,0:T(8,128)(2,1)} %collective-permute-done.55.refs_2_), channel_id=1, source_target_pairs={{16,24},{17,25},{18,26},{19,27},{20,28},{21,29},{22,30},{23,31}} | collective-permute-start | bytes 1228808 | tf_op jit(solution)/shard_map/ppermute | solution.py:501
  900.8 18.7 %collective-permute-start.63 = (bf16[4,160,480]{2,1,0:T(8,128)(2,1)}, bf16[4,160,480]{2,1,0:T(8,128)(2,1)}, u32[]{:S(2)}, u32[]{:S(2)}) collective-permute-start(bf16[4,160,480]{2,1,0:T(8,128)(2,1)} %get-tuple-element.179), channel_id=1, source_target_pairs={{16,8},{24,16},{17,9},{25,17},{18,10},{26,18},{19,11},{27,19},{20,... | collective-permute-start | bytes 1843208 | tf_op jit(solution)/shard_map/ppermute | solution.py:488
  902.3 17.2 %collective-permute-start.57 = (bf16[4,160,480]{2,1,0:T(8,128)(2,1)}, bf16[4,160,480]{2,1,0:T(8,128)(2,1)}, u32[]{:S(2)}, u32[]{:S(2)}) collective-permute-start(bf16[4,160,480]{2,1,0:T(8,128)(2,1)} %get-tuple-element.176), channel_id=1, source_target_pairs={{0,8},{8,16},{1,9},{9,17},{2,10},{10,18},{3,11},{11,19},{4,12},{12... | collective-permute-start | bytes 1843208 | tf_op jit(solution)/shard_map/ppermute | solution.py:487
  911.6 24.8 %collective-permute-start.65 = (bf16[4,80,2560]{2,1,0:T(8,128)(2,1)}, bf16[4,80,2560]{2,1,0:T(8,128)(2,1)}, u32[]{:S(2)}, u32[]{:S(2)}) collective-permute-start(bf16[4,80,2560]{2,1,0:T(8,128)(2,1)} %shard_map.216.refs_0_), channel_id=1, source_target_pairs={{0,4},{4,0},{1,5},{5,1},{2,6},{6,2},{3,7},{7,3},{8,12},{12,8},{9,1... | collective-permute-start | bytes 4915208 | tf_op jit(solution)/shard_map/ppermute | solution.py:62
  931.3 18.4 %collective-permute-start.61 = (bf16[4,160,480]{2,1,0:T(8,128)(2,1)S(1)}, bf16[4,160,480]{2,1,0:T(8,128)(2,1)S(1)}, u32[]{:S(2)}, u32[]{:S(2)}) collective-permute-start(bf16[4,160,480]{2,1,0:T(8,128)(2,1)S(1)} %get-tuple-element.177), channel_id=1, source_target_pairs={{0,8},{8,16},{16,24},{1,9},{9,17},{17,25},{2,10},{10,18},{18,26},{... | collective-permute-start | bytes 1843208 | tf_op jit(solution)/shard_map/ppermute | solution.py:487
  935.1 18.7 %collective-permute-start.64 = (bf16[4,160,480]{2,1,0:T(8,128)(2,1)S(1)}, bf16[4,160,480]{2,1,0:T(8,128)(2,1)S(1)}, u32[]{:S(2)}, u32[]{:S(2)}) collective-permute-start(bf16[4,160,480]{2,1,0:T(8,128)(2,1)S(1)} %get-tuple-element.180), channel_id=1, source_target_pairs={{8,0},{16,8},{24,16},{9,1},{17,9},{25,17},{10,2},{18,10},{26,18},{... | collective-permute-start | bytes 1843208 | tf_op jit(solution)/shard_map/ppermute | solution.py:488
  954.2 18.2 %collective-permute-start.69 = (bf16[4,160,480]{2,1,0:T(8,128)(2,1)S(1)}, bf16[4,160,480]{2,1,0:T(8,128)(2,1)S(1)}, u32[]{:S(2)}, u32[]{:S(2)}) collective-permute-start(bf16[4,160,480]{2,1,0:T(8,128)(2,1)S(1)} %fusion.36.refs_0_), channel_id=1, source_target_pairs={{8,0},{16,8},{24,16},{9,1},{17,9},{25,17},{10,2},{18,10},{26,18},{... | collective-permute-start | bytes 1843208 | tf_op jit(solution)/shard_map/ppermute | solution.py:502
  955.8 17.9 %collective-permute-start.66 = (bf16[4,160,480]{2,1,0:T(8,128)(2,1)S(1)}, bf16[4,160,480]{2,1,0:T(8,128)(2,1)S(1)}, u32[]{:S(2)}, u32[]{:S(2)}) collective-permute-start(bf16[4,160,480]{2,1,0:T(8,128)(2,1)S(1)} %fusion.36.refs_0_), channel_id=1, source_target_pairs={{0,8},{8,16},{16,24},{1,9},{9,17},{17,25},{2,10},{10,18},{18,26},{... | collective-permute-start | bytes 1843208 | tf_op jit(solution)/shard_map/ppermute | solution.py:501
  (80 other events, 1665.9 us)
Sparse Core Ops, SparseCore 0:
  13.4 68.0 all-gather.4
  152.1 86.9 reduce-scatter.4
  242.8 41.0 all-gather.6
  285.8 41.1 all-gather.8
  382.2 55.8 reduce-scatter.6
  456.3 61.2 all-gather.10
  711.8 55.7 reduce-scatter.10
  853.6 61.9 reduce-scatter.8

commit v4 on v3

--- a/solution.py
+++ b/solution.py
@@ -782,9 +782,9 @@
         sum_down,
         [sum_gate, sum_up, sum_out, sum_qkv],
         {
-            slot(2, 0): lambda: [grad_kv],
-            slot(2, 2): lambda: [grad_qkv],
-            slot(2, 3): lambda: [grad_w_qkv, h_one_parts],
+            slot(1, 3): lambda: [grad_kv],
+            slot(2, 1): lambda: [grad_qkv],
+            slot(2, 2): lambda: [grad_w_qkv, h_one_parts],
             slot(3, 0): down_done,
             slot(3, 2): gate_done,
             slot(4, 2): lambda: [*up_done(), gain_grads],

time: 1040 us -> 1080 us (1.038)
  waiting for transfers between devices: 490 us -> 524 us
    all_to_all x3, waiting for transfers between devices: 33 us -> 56.3 us  [to_shards(): return lax.all_to_all(grad, 'f', 0, 0)]
    ppermute x15, waiting for transfers between devices: 78.1 us -> 93.1 us  [spread(): lax.ppermute(down, 'z', [(i, i - 1) for i in range(1, n_z - step + 1)])]
  transfers between devices with their start and end apart: 88 -> 88, of which waited for: 40 -> 40; matrix products, arithmetic and copies ran while one was open for 14% -> 14% of each run, Pallas kernels for 12% -> 11%
where the time goes in v4:
time: 1080 us; the launch traced here: 1070 us
  waiting for transfers between devices  524 us (49%)
  starting transfers between devices  207 us (19%)
  Pallas kernels  131 us (12%)
  matrix products  108 us (10%)
  other arithmetic  48.2 us (4%)
  local copies, waits for them, and re-layouts  36.8 us (3%)
  between operations  16 us (1%)
    ppermute x15, waiting for transfers between devices, add(): self.up = lax.ppermute(up, 'z', [(i, i + 1) for i in range(step)])  141 us
    ppermute x15, waiting for transfers between devices, spread(): lax.ppermute(down, 'z', [(i, i - 1) for i in range(1, n_z - step + 1)])  93.1 us
    ppermute x15, starting transfers between devices, add(): self.up = lax.ppermute(up, 'z', [(i, i + 1) for i in range(step)])  81.3 us
    all_to_all x1, waiting for transfers between devices, per_device(): up_full = lax.all_to_all(up_parts, 'f', 0, 0).reshape(width, hidden)  64.9 us
    all_to_all x3, waiting for transfers between devices, to_shards(): return lax.all_to_all(grad, 'f', 0, 0)  56.3 us
    ppermute x15, starting transfers between devices, spread(): lax.ppermute(up, 'z', [(i, i + 1) for i in range(step - 1, n_z - 1)])  40.7 us
    all_gather x1, waiting for transfers between devices, per_device(): h_two = lax.all_gather(h_two, in_plane, axis=0, tiled=True)  40.4 us
    dot_general x4, matrix products, nn(): lax.dot_general(a, b, (((1,), (0,)), ((), ())), preferred_element_type=F32)  34.2 us
  transfers between devices with their start and end apart: 88, of which 40 were waited for; matrix products, arithmetic and copies ran while one was open for 14% of the time, Pallas kernels for 11%

profile of v4, /device:TPU:0, one launch (start us, length us, event | category | flops | bytes accessed | tf_op | source)
XLA Modules:
  0.0 1070.6 jit_solution(5147325949215874451)
XLA Ops:
  22.4 5.2 all-to-all-start
  27.6 5.0 shard_map.205
  32.6 5.0 shard_map.206
  37.5 26.7 %all-to-all-done = bf16[4,640,480]{1,2,0:T(8,128)(2,1)} async-done(((bf16[4,640,480]{1,2,0:T(8,128)(2,1)}), bf16[4,640,480]{1,2,0:T(8,128)(2,1)}, u32[]{:S(2)}, u32[]{:S(2)}) %all-to-all-start) | async-done | bytes 2457632 | tf_op jit(solution)/shard_map/all_to_all | solution.py:589
  68.7 12.8 %all-gather.5.cloned.1.call-done.block = bf16[1280,2560]{1,0:T(8,128)(2,1)} async-done(((bf16[160,2560]{1,0:T(8,128)(2,1)}), bf16[1280,2560]{1,0:T(8,128)(2,1)}) %all-gather.5.cloned.1.call-update) | async-done | bytes 6553616 | tf_op jit(solution)/shard_map/all_gather | solution.py:586
  88.6 11.1 %shard_map.207 = (bf16[1024,2560]{1,0:T(8,128)(2,1)}, bf16[320,1024]{1,0:T(8,128)(2,1)}, bf16[160,1024]{1,0:T(8,128)(2,1)}, f32[40,1024]{1,0:T(8,128)}, f32[40,1024]{1,0:T(8,128)}, /*index=5*/s32[8,1,128]{2,1,0:T(1,128)}) custom-call(s32[1]{0:T(128)} %bitcast.1.where, bf16[1280,2560]{1,0:T(8,128)(2,1)} %all-gather.5.cloned.1.call-done.block, ...), custom_call_target="tpu_custom_call" | custom-call | flops 2516582400 | bytes 10485760 | tf_op jit(solution)/shard_map/pallas_call | solution.py:184
  105.9 5.7 collective-permute-done.2.refs_4_
  111.5 20.4 %collective-permute-done.1.refs_3_ = bf16[160,1024]{1,0:T(8,128)(2,1)} collective-permute-done((bf16[160,1024]{1,0:T(8,128)(2,1)}, bf16[160,1024]{1,0:T(8,128)(2,1)}, u32[]{:S(2)}, u32[]{:S(2)}) %collective-permute-start.1) | collective-permute-done | bytes 327712 | tf_op jit(solution)/shard_map/ppermute | solution.py:460
  131.9 14.0 %shard_map.208 = (f32[320,1024]{1,0:T(8,128)}, bf16[320,1024]{1,0:T(8,128)(2,1)}, f32[4,4,256]{2,1,0:T(4,128)}) custom-call(bf16[320,1024]{1,0:T(8,128)(2,1)} %get-tuple-element.117.refs_0_, bf16[160,1024]{1,0:T(8,128)(2,1)} %get-tuple-element.118.refs_1_, bf16[160,1024]{1,0:T(8,128)(2,1)} %collective-permute-done.refs_2_, ...), custom_call_target="tpu_custom_call" | custom-call | flops 1342177280 | bytes 2621440 | tf_op jit(solution)/shard_map/pallas_call | solution.py:258
  152.0 5.1 all-to-all-start.2
  157.8 64.9 %all-to-all-done.2 = bf16[4,640,896]{2,1,0:T(8,128)(2,1)} async-done(((bf16[4,640,896]{2,1,0:T(8,128)(2,1)}), bf16[4,640,896]{2,1,0:T(8,128)(2,1)}, u32[]{:S(2)}, u32[]{:S(2)}) %all-to-all-start.2) | async-done | bytes 4587552 | tf_op jit(solution)/shard_map/all_to_all | solution.py:639
  222.6 16.4 %reduce-scatter.5.cloned.1.call-done = bf16[128,2560]{1,0:T(8,128)(2,1)} async-done(((bf16[1024,2560]{1,0:T(8,128)(2,1)}), bf16[128,2560]{1,0:T(8,128)(2,1)}) %reduce-scatter.5.cloned.1.call-update) | async-done | bytes 655376 | tf_op jit(solution)/shard_map/reduce_scatter | solution.py:630
  243.5 40.4 %all-gather.7.cloned.1.call-done = bf16[1024,2560]{1,0:T(8,128)(2,1)} async-done(((bf16[128,2560]{1,0:T(8,128)(2,1)}), bf16[1024,2560]{1,0:T(8,128)(2,1)}) %all-gather.7.cloned.1.call-update) | async-done | bytes 5242896 | tf_op jit(solution)/shard_map/all_gather | solution.py:650
  283.9 9.0 fusion.56
  292.9 11.3 %multiply_convert_fusion.2 = (bf16[1024,896]{1,0:T(8,128)(2,1)S(1)}, f32[1024,896]{1,0:T(8,128)}) fusion(f32[1024,896]{1,0:T(8,128)S(1)} %fusion.56, bf16[1024,2560]{1,0:T(8,128)(2,1)S(1)} %copy-done.41, bf16[2560,896]{1,0:T(8,128)(2,1)} %bitcast.14), kind=kOutput, calls=%fused_computation.12 | convolution fusion | flops 4703125504 | bytes 19005440 | tf_op jit(solution)/shard_map/dot_general | solution.py:230
  306.9 20.1 %all-gather.9.cloned.1.call-done = bf16[1024,2560]{1,0:T(8,128)(2,1)} async-done(((bf16[128,2560]{1,0:T(8,128)(2,1)}), bf16[1024,2560]{1,0:T(8,128)(2,1)}) %all-gather.9.cloned.1.call-update) | async-done | bytes 5242896 | tf_op jit(solution)/shard_map/all_gather | solution.py:611
  327.0 7.6 convolution_convert_fusion.5
  339.8 8.8 multiply_convert_fusion
  348.6 15.6 %collective-permute-done.3 = bf16[224,2560]{1,0:T(8,128)(2,1)S(1)} collective-permute-done((bf16[224,2560]{1,0:T(8,128)(2,1)S(1)}, bf16[224,2560]{1,0:T(8,128)(2,1)S(1)}, u32[]{:S(2)}, u32[]{:S(2)}) %collective-permute-start.3) | collective-permute-done | bytes 1146912 | tf_op jit(solution)/shard_map/ppermute | solution.py:487
  364.8 7.5 fusion.57
  372.3 9.8 add_convert_fusion
  382.2 5.4 collective-permute-start.5
  389.2 21.4 %collective-permute-done.5 = bf16[224,2560]{1,0:T(8,128)(2,1)} collective-permute-done((bf16[224,2560]{1,0:T(8,128)(2,1)S(1)}, bf16[224,2560]{1,0:T(8,128)(2,1)}, u32[]{:S(2)}, u32[]{:S(2)}) %collective-permute-start.5) | collective-permute-done | bytes 1146912 | tf_op jit(solution)/shard_map/ppermute | solution.py:487
  414.6 7.9 collective-permute-start.6
  423.8 20.8 %collective-permute-done.6 = bf16[224,2560]{1,0:T(8,128)(2,1)} collective-permute-done((bf16[224,2560]{1,0:T(8,128)(2,1)}, bf16[224,2560]{1,0:T(8,128)(2,1)}, u32[]{:S(2)}, u32[]{:S(2)}) %collective-permute-start.6) | collective-permute-done | bytes 1146912 | tf_op jit(solution)/shard_map/ppermute | solution.py:487
  456.3 9.5 convolution_convert_fusion.3
  465.8 5.0 all-to-all-start.5
  472.3 5.6 collective-permute-start.14
  477.9 56.3 %all-to-all-done.5 = bf16[4,640,896]{2,1,0:T(8,128)(2,1)} async-done(((bf16[4,640,896]{2,1,0:T(8,128)(2,1)}), bf16[4,640,896]{2,1,0:T(8,128)(2,1)}, u32[]{:S(2)}, u32[]{:S(2)}) %all-to-all-start.5) | async-done | bytes 4587552 | tf_op jit(solution)/shard_map/all_to_all | solution.py:724
  546.2 9.6 convolution_convert_fusion.4
  555.9 5.0 all-to-all-start.6
  576.3 16.8 %collective-permute-done.22 = bf16[4,160,896]{2,1,0:T(8,128)(2,1)S(1)} collective-permute-done((bf16[4,160,896]{2,1,0:T(8,128)(2,1)S(1)}, bf16[4,160,896]{2,1,0:T(8,128)(2,1)S(1)}, u32[]{:S(2)}, u32[]{:S(2)}) %collective-permute-start.22) | collective-permute-done | bytes 1146912 | tf_op jit(solution)/shard_map/ppermute | solution.py:487
  599.5 7.2 collective-permute-start.23
  608.5 5.2 convolution_convert_fusion.8.refs_5_
  613.7 17.2 %shard_map.209 = (f32[320,1024]{1,0:T(8,128)}, bf16[4,160,1024]{2,1,0:T(8,128)(2,1)}) custom-call(s32[4]{0:T(128)} %pad_add_fusion.1.where, bf16[320,1024]{1,0:T(8,128)(2,1)} %get-tuple-element.117.refs_0_, bf16[160,1024]{1,0:T(8,128)(2,1)} %get-tuple-element.118.refs_1_, bf16[160,1024]{1,0:T(8,128)(2,1)} %collective-permute-done.refs_2_, ...), custom_call_target="tpu_custom_call" | custom-call | flops 3355443200 | bytes 3932160 | tf_op jit(solution)/shard_map/pallas_call | solution.py:316
  639.3 5.6 collective-permute-start.27
  648.1 6.0 shard_map.210.refs_0_
  654.3 24.4 %collective-permute-done.28.refs_4_ = bf16[4,160,896]{2,1,0:T(8,128)(2,1)} collective-permute-done((bf16[4,160,896]{2,1,0:T(8,128)(2,1)S(1)}, bf16[4,160,896]{2,1,0:T(8,128)(2,1)}, u32[]{:S(2)}, u32[]{:S(2)}) %collective-permute-start.28) | collective-permute-done | bytes 1146912 | tf_op jit(solution)/shard_map/ppermute | solution.py:502
  678.8 11.3 %collective-permute-start.29 = (bf16[4,160,896]{2,1,0:T(8,128)(2,1)}, bf16[4,160,896]{2,1,0:T(8,128)(2,1)}, u32[]{:S(2)}, u32[]{:S(2)}) collective-permute-start(bf16[4,160,896]{2,1,0:T(8,128)(2,1)} %get-tuple-element.163), channel_id=1, source_target_pairs={{0,8},{1,9},{2,10},{3,11},{4,12},{5,13},{6,14},{7,15}} | collective-permute-start | bytes 3440648 | tf_op jit(solution)/shard_map/ppermute | solution.py:487
  696.5 14.6 %collective-permute-done.29 = bf16[4,160,896]{2,1,0:T(8,128)(2,1)} collective-permute-done((bf16[4,160,896]{2,1,0:T(8,128)(2,1)}, bf16[4,160,896]{2,1,0:T(8,128)(2,1)}, u32[]{:S(2)}, u32[]{:S(2)}) %collective-permute-start.29) | collective-permute-done | bytes 1146912 | tf_op jit(solution)/shard_map/ppermute | solution.py:487
  733.6 6.1 convolution_convert_fusion.6
  755.6 18.4 %collective-permute-done.35 = bf16[4,160,896]{2,1,0:T(8,128)(2,1)S(1)} collective-permute-done((bf16[4,160,896]{2,1,0:T(8,128)(2,1)S(1)}, bf16[4,160,896]{2,1,0:T(8,128)(2,1)S(1)}, u32[]{:S(2)}, u32[]{:S(2)}) %collective-permute-start.35) | collective-permute-done | bytes 1146912 | tf_op jit(solution)/shard_map/ppermute | solution.py:487
  781.2 5.6 collective-permute-start.39
  786.8 6.0 shard_map.212.refs_0_
  792.8 11.6 %shard_map.211 = f32[1792,2560]{1,0:T(8,128)} custom-call(s32[1]{0:T(128)} %bitcast.2.where, bf16[4,224,2560]{2,1,0:T(8,128)(2,1)} %shard_map.210.refs_0_, bf16[4,224,2560]{2,1,0:T(8,128)(2,1)} %collective-permute-done.20.refs_1_), custom_call_target="tpu_custom_call" | custom-call | bytes 18350080 | tf_op jit(solution)/shard_map/pallas_call | solution.py:441
  811.9 7.3 collective-permute-start.41
  819.9 8.0 collective-permute-done.41
  828.0 10.4 collective-permute-done.43.refs_5_
  846.2 5.2 collective-permute-done.44
  859.6 10.0 shard_map.213
  871.7 5.9 shard_map.214.refs_0_
  877.7 7.7 collective-permute-start.48
  886.7 9.6 convolution_convert_fusion.2
  902.2 5.3 collective-permute-start.52
  918.2 6.4 collective-permute-start.9
  929.5 9.7 collective-permute-done.54
  942.1 5.0 collective-permute-start.57
  962.2 10.0 shard_map.215
  977.3 7.0 shard_map.217
  984.3 6.0 collective-permute-done.61
  1000.9 11.6 %collective-permute-done.69.refs_4_ = bf16[4,160,480]{2,1,0:T(8,128)(2,1)S(1)} collective-permute-done((bf16[4,160,480]{2,1,0:T(8,128)(2,1)S(1)}, bf16[4,160,480]{2,1,0:T(8,128)(2,1)S(1)}, u32[]{:S(2)}, u32[]{:S(2)}) %collective-permute-start.69) | collective-permute-done | bytes 614432 | tf_op jit(solution)/shard_map/ppermute | solution.py:502
  1014.5 14.6 %collective-permute-done.70.refs_5_ = bf16[4,160,480]{2,1,0:T(8,128)(2,1)S(1)} collective-permute-done((bf16[4,160,480]{2,1,0:T(8,128)(2,1)S(1)}, bf16[4,160,480]{2,1,0:T(8,128)(2,1)S(1)}, u32[]{:S(2)}, u32[]{:S(2)}) %collective-permute-start.70) | collective-permute-done | bytes 614432 | tf_op jit(solution)/shard_map/ppermute | solution.py:502
  1031.4 13.4 %collective-permute-done.71.refs_6_ = bf16[4,160,480]{2,1,0:T(8,128)(2,1)S(1)} collective-permute-done((bf16[4,160,480]{2,1,0:T(8,128)(2,1)S(1)}, bf16[4,160,480]{2,1,0:T(8,128)(2,1)S(1)}, u32[]{:S(2)}, u32[]{:S(2)}) %collective-permute-start.71) | collective-permute-done | bytes 614432 | tf_op jit(solution)/shard_map/ppermute | solution.py:502
  1056.1 7.2 shard_map.219
  (336 shorter events, 269.4 us)
Async XLA Ops:
  7.2 74.3 %all-gather.5.cloned.1.call-start = ((), (), s32[]{:S(2)}) async-start(), calls=%async_computation.11 | async-start | bytes 7372800 | tf_op jit(solution)/shard_map/all_gather | solution.py:586
  22.4 41.9 %all-to-all-start = ((bf16[4,640,480]{1,2,0:T(8,128)(2,1)}), bf16[4,640,480]{1,2,0:T(8,128)(2,1)}, u32[]{:S(2)}, u32[]{:S(2)}) async-start(bf16[4,640,480]{1,2,0:T(8,128)(2,1)} %copy.65), calls=%async_computation | async-start | bytes 4915200 | tf_op jit(solution)/shard_map/all_to_all | solution.py:589
  81.4 64.5 %all-to-all-start.1 = ((bf16[4,640,896]{2,1,0:T(8,128)(2,1)}), bf16[4,640,896]{2,1,0:T(8,128)(2,1)}, u32[]{:S(2)}, u32[]{:S(2)}) async-start(bf16[4,640,896]{2,1,0:T(8,128)(2,1)} %shard_map.205), calls=%async_computation.1 | async-start | bytes 9175040 | tf_op jit(solution)/shard_map/all_to_all | solution.py:604
  86.4 152.7 %reduce-scatter.5.cloned.1.call-start = ((), (), s32[]{:S(2)}) async-start(), calls=%async_computation.12 | async-start | bytes 5898240 | tf_op jit(solution)/shard_map/reduce_scatter | solution.py:630
  103.1 28.9 %collective-permute-start.1 = (bf16[160,1024]{1,0:T(8,128)(2,1)}, bf16[160,1024]{1,0:T(8,128)(2,1)}, u32[]{:S(2)}, u32[]{:S(2)}) collective-permute-start(bf16[160,1024]{1,0:T(8,128)(2,1)} %get-tuple-element.118.refs_1_), channel_id=1, source_target_pairs={{0,16},{8,24},{16,0},{24,8},{1,17},{9,25},{17,1},{25,9},{2,18},{10... | collective-permute-start | bytes 983048 | tf_op jit(solution)/shard_map/ppermute | solution.py:460
  103.1 28.9 %collective-permute-start = (bf16[160,1024]{1,0:T(8,128)(2,1)}, bf16[160,1024]{1,0:T(8,128)(2,1)}, u32[]{:S(2)}, u32[]{:S(2)}) collective-permute-start(bf16[160,1024]{1,0:T(8,128)(2,1)} %get-tuple-element.118.refs_1_), channel_id=1, source_target_pairs={{0,8},{8,16},{16,24},{24,0},{1,9},{9,17},{17,25},{25,1},{2,10},{10... | collective-permute-start | bytes 983048 | tf_op jit(solution)/shard_map/ppermute | solution.py:460
  152.0 70.7 %all-to-all-start.2 = ((bf16[4,640,896]{2,1,0:T(8,128)(2,1)}), bf16[4,640,896]{2,1,0:T(8,128)(2,1)}, u32[]{:S(2)}, u32[]{:S(2)}) async-start(bf16[4,640,896]{2,1,0:T(8,128)(2,1)} %shard_map.206), calls=%async_computation.3 | async-start | bytes 9175040 | tf_op jit(solution)/shard_map/all_to_all | solution.py:639
  157.1 126.8 %all-gather.7.cloned.1.call-start = ((), (), s32[]{:S(2)}) async-start(), calls=%async_computation.13 | async-start | bytes 5898240 | tf_op jit(solution)/shard_map/all_gather | solution.py:650
  242.7 84.3 %all-gather.9.cloned.1.call-start = ((), (), s32[]{:S(2)}) async-start(), calls=%async_computation.14 | async-start | bytes 5898240 | tf_op jit(solution)/shard_map/all_gather | solution.py:611
  243.2 209.7 %reduce-scatter.7.cloned.1.call-start = ((), (), s32[]{:S(2)}) async-start(), calls=%async_computation.15 | async-start | bytes 5898240 | tf_op jit(solution)/shard_map/reduce_scatter | solution.py:630
  335.6 28.6 %collective-permute-start.3 = (bf16[224,2560]{1,0:T(8,128)(2,1)S(1)}, bf16[224,2560]{1,0:T(8,128)(2,1)S(1)}, u32[]{:S(2)}, u32[]{:S(2)}) collective-permute-start(bf16[224,2560]{1,0:T(8,128)(2,1)S(1)} %get-tuple-element.210), channel_id=1, source_target_pairs={{0,8},{1,9},{2,10},{3,11},{4,12},{5,13},{6,14},{7,15}} | collective-permute-start | bytes 3440648 | tf_op jit(solution)/shard_map/ppermute | solution.py:487
  382.1 226.4 %all-gather.11.cloned.1.call-start = ((), (), s32[]{:S(2)}) async-start(), calls=%async_computation.16 | async-start | bytes 5898240 | tf_op jit(solution)/shard_map/all_gather | solution.py:689
  382.2 28.5 %collective-permute-start.5 = (bf16[224,2560]{1,0:T(8,128)(2,1)S(1)}, bf16[224,2560]{1,0:T(8,128)(2,1)}, u32[]{:S(2)}, u32[]{:S(2)}) collective-permute-start(bf16[224,2560]{1,0:T(8,128)(2,1)S(1)} %get-tuple-element.144), channel_id=1, source_target_pairs={{0,8},{8,16},{1,9},{9,17},{2,10},{10,18},{3,11},{11,19},{4,12},{12... | collective-permute-start | bytes 3440648 | tf_op jit(solution)/shard_map/ppermute | solution.py:487
  387.6 23.1 %collective-permute-start.7 = (bf16[224,2560]{1,0:T(8,128)(2,1)S(1)}, bf16[224,2560]{1,0:T(8,128)(2,1)}, u32[]{:S(2)}, u32[]{:S(2)}) collective-permute-start(bf16[224,2560]{1,0:T(8,128)(2,1)S(1)} %get-tuple-element.145), channel_id=1, source_target_pairs={{16,8},{24,16},{17,9},{25,17},{18,10},{26,18},{19,11},{27,19},{20,... | collective-permute-start | bytes 3440648 | tf_op jit(solution)/shard_map/ppermute | solution.py:488
  414.6 30.0 %collective-permute-start.6 = (bf16[224,2560]{1,0:T(8,128)(2,1)}, bf16[224,2560]{1,0:T(8,128)(2,1)}, u32[]{:S(2)}, u32[]{:S(2)}) collective-permute-start(bf16[224,2560]{1,0:T(8,128)(2,1)} %get-tuple-element.149), channel_id=1, source_target_pairs={{0,8},{8,16},{16,24},{1,9},{9,17},{17,25},{2,10},{10,18},{18,26},{... | collective-permute-start | bytes 3440648 | tf_op jit(solution)/shard_map/ppermute | solution.py:487
  422.5 27.0 %collective-permute-start.8 = (bf16[224,2560]{1,0:T(8,128)(2,1)S(1)}, bf16[224,2560]{1,0:T(8,128)(2,1)}, u32[]{:S(2)}, u32[]{:S(2)}) collective-permute-start(bf16[224,2560]{1,0:T(8,128)(2,1)S(1)} %get-tuple-element.150), channel_id=1, source_target_pairs={{8,0},{16,8},{24,16},{9,1},{17,9},{25,17},{10,2},{18,10},{26,18},{... | collective-permute-start | bytes 3440648 | tf_op jit(solution)/shard_map/ppermute | solution.py:488
  465.8 68.4 %all-to-all-start.5 = ((bf16[4,640,896]{2,1,0:T(8,128)(2,1)}), bf16[4,640,896]{2,1,0:T(8,128)(2,1)}, u32[]{:S(2)}, u32[]{:S(2)}) async-start(bf16[4,640,896]{2,1,0:T(8,128)(2,1)} %bitcast.265), calls=%async_computation.9 | async-start | bytes 9175040 | tf_op jit(solution)/shard_map/all_to_all | solution.py:724
  470.9 66.7 %collective-permute-start.17 = (bf16[224,2560]{1,0:T(8,128)(2,1)S(1)}, bf16[224,2560]{1,0:T(8,128)(2,1)S(1)}, u32[]{:S(2)}, u32[]{:S(2)}) collective-permute-start(bf16[224,2560]{1,0:T(8,128)(2,1)S(1)} %copy-done.10), channel_id=1, source_target_pairs={{8,0},{16,8},{24,16},{9,1},{17,9},{25,17},{10,2},{18,10},{26,18},{... | collective-permute-start | bytes 3440648 | tf_op jit(solution)/shard_map/ppermute | solution.py:502
  472.3 65.3 %collective-permute-start.14 = (bf16[224,2560]{1,0:T(8,128)(2,1)S(1)}, bf16[224,2560]{1,0:T(8,128)(2,1)}, u32[]{:S(2)}, u32[]{:S(2)}) collective-permute-start(bf16[224,2560]{1,0:T(8,128)(2,1)S(1)} %copy-done.10), channel_id=1, source_target_pairs={{0,8},{8,16},{16,24},{1,9},{9,17},{17,25},{2,10},{10,18},{18,26},{... | collective-permute-start | bytes 3440648 | tf_op jit(solution)/shard_map/ppermute | solution.py:501
  537.6 25.1 %collective-permute-start.21 = (bf16[4,160,896]{2,1,0:T(8,128)(2,1)}, bf16[4,160,896]{2,1,0:T(8,128)(2,1)}, u32[]{:S(2)}, u32[]{:S(2)}) collective-permute-start(bf16[4,160,896]{2,1,0:T(8,128)(2,1)} %get-tuple-element.156), channel_id=1, source_target_pairs={{0,8},{1,9},{2,10},{3,11},{4,12},{5,13},{6,14},{7,15}} | collective-permute-start | bytes 3440648 | tf_op jit(solution)/shard_map/ppermute | solution.py:487
  541.6 21.2 %collective-permute-start.24 = (bf16[4,160,896]{2,1,0:T(8,128)(2,1)}, bf16[4,160,896]{2,1,0:T(8,128)(2,1)}, u32[]{:S(2)}, u32[]{:S(2)}) collective-permute-start(bf16[4,160,896]{2,1,0:T(8,128)(2,1)} %get-tuple-element.159), channel_id=1, source_target_pairs={{24,16},{25,17},{26,18},{27,19},{28,20},{29,21},{30,22},{31,23}} | collective-permute-start | bytes 3440648 | tf_op jit(solution)/shard_map/ppermute | solution.py:488
  543.3 26.0 %collective-permute-start.18 = (bf16[224,2560]{1,0:T(8,128)(2,1)S(1)}, bf16[224,2560]{1,0:T(8,128)(2,1)S(1)}, u32[]{:S(2)}, u32[]{:S(2)}) collective-permute-start(bf16[224,2560]{1,0:T(8,128)(2,1)S(1)} %collective-permute-done.17.refs_4_), channel_id=1, source_target_pairs={{8,0},{16,8},{9,1},{17,9},{10,2},{18,10},{11,3},{19,11},{12,4},{20... | collective-permute-start | bytes 3440648 | tf_op jit(solution)/shard_map/ppermute | solution.py:502
  544.6 24.7 %collective-permute-start.15 = (bf16[224,2560]{1,0:T(8,128)(2,1)}, bf16[224,2560]{1,0:T(8,128)(2,1)}, u32[]{:S(2)}, u32[]{:S(2)}) collective-permute-start(bf16[224,2560]{1,0:T(8,128)(2,1)} %collective-permute-done.14.refs_1_), channel_id=1, source_target_pairs={{8,16},{16,24},{9,17},{17,25},{10,18},{18,26},{11,19},{19,27},{12,... | collective-permute-start | bytes 3440648 | tf_op jit(solution)/shard_map/ppermute | solution.py:501
  555.9 75.1 %all-to-all-start.6 = ((bf16[4,640,896]{2,1,0:T(8,128)(2,1)}), bf16[4,640,896]{2,1,0:T(8,128)(2,1)}, u32[]{:S(2)}, u32[]{:S(2)}) async-start(bf16[4,640,896]{2,1,0:T(8,128)(2,1)} %bitcast.264), calls=%async_computation.10 | async-start | bytes 9175040 | tf_op jit(solution)/shard_map/all_to_all | solution.py:724
  570.3 22.9 %collective-permute-start.22 = (bf16[4,160,896]{2,1,0:T(8,128)(2,1)S(1)}, bf16[4,160,896]{2,1,0:T(8,128)(2,1)S(1)}, u32[]{:S(2)}, u32[]{:S(2)}) collective-permute-start(bf16[4,160,896]{2,1,0:T(8,128)(2,1)S(1)} %get-tuple-element.157), channel_id=1, source_target_pairs={{0,8},{8,16},{1,9},{9,17},{2,10},{10,18},{3,11},{11,19},{4,12},{12... | collective-permute-start | bytes 3440648 | tf_op jit(solution)/shard_map/ppermute | solution.py:487
  572.5 20.6 %collective-permute-start.25 = (bf16[4,160,896]{2,1,0:T(8,128)(2,1)S(1)}, bf16[4,160,896]{2,1,0:T(8,128)(2,1)S(1)}, u32[]{:S(2)}, u32[]{:S(2)}) collective-permute-start(bf16[4,160,896]{2,1,0:T(8,128)(2,1)S(1)} %get-tuple-element.160), channel_id=1, source_target_pairs={{16,8},{24,16},{17,9},{25,17},{18,10},{26,18},{19,11},{27,19},{20,... | collective-permute-start | bytes 3440648 | tf_op jit(solution)/shard_map/ppermute | solution.py:488
  573.3 26.2 %collective-permute-start.19 = (bf16[224,2560]{1,0:T(8,128)(2,1)}, bf16[224,2560]{1,0:T(8,128)(2,1)}, u32[]{:S(2)}, u32[]{:S(2)}) collective-permute-start(bf16[224,2560]{1,0:T(8,128)(2,1)} %copy-done.21), channel_id=1, source_target_pairs={{8,0},{9,1},{10,2},{11,3},{12,4},{13,5},{14,6},{15,7}} | collective-permute-start | bytes 3440648 | tf_op jit(solution)/shard_map/ppermute | solution.py:502
  574.6 24.9 %collective-permute-start.16 = (bf16[224,2560]{1,0:T(8,128)(2,1)}, bf16[224,2560]{1,0:T(8,128)(2,1)}, u32[]{:S(2)}, u32[]{:S(2)}) collective-permute-start(bf16[224,2560]{1,0:T(8,128)(2,1)} %collective-permute-done.15.refs_2_), channel_id=1, source_target_pairs={{16,24},{17,25},{18,26},{19,27},{20,28},{21,29},{22,30},{23,31}} | collective-permute-start | bytes 3440648 | tf_op jit(solution)/shard_map/ppermute | solution.py:501
  599.5 36.2 %collective-permute-start.23 = (bf16[4,160,896]{2,1,0:T(8,128)(2,1)}, bf16[4,160,896]{2,1,0:T(8,128)(2,1)}, u32[]{:S(2)}, u32[]{:S(2)}) collective-permute-start(bf16[4,160,896]{2,1,0:T(8,128)(2,1)} %get-tuple-element.158), channel_id=1, source_target_pairs={{0,8},{8,16},{16,24},{1,9},{9,17},{17,25},{2,10},{10,18},{18,26},{... | collective-permute-start | bytes 3440648 | tf_op jit(solution)/shard_map/ppermute | solution.py:487
  606.6 29.0 %collective-permute-start.26 = (bf16[4,160,896]{2,1,0:T(8,128)(2,1)}, bf16[4,160,896]{2,1,0:T(8,128)(2,1)}, u32[]{:S(2)}, u32[]{:S(2)}) collective-permute-start(bf16[4,160,896]{2,1,0:T(8,128)(2,1)} %get-tuple-element.161), channel_id=1, source_target_pairs={{8,0},{16,8},{24,16},{9,1},{17,9},{25,17},{10,2},{18,10},{26,18},{... | collective-permute-start | bytes 3440648 | tf_op jit(solution)/shard_map/ppermute | solution.py:488
  631.0 65.1 %all-to-all-start.3 = ((bf16[4,160,1024]{2,1,0:T(8,128)(2,1)}), bf16[4,160,1024]{2,1,0:T(8,128)(2,1)S(1)}, u32[]{:S(2)}, u32[]{:S(2)}) async-start(bf16[4,160,1024]{2,1,0:T(8,128)(2,1)} %get-tuple-element.154), calls=%async_computation.6 | async-start | bytes 2621440 | tf_op jit(solution)/shard_map/all_to_all | solution.py:695
  635.6 281.0 %reduce-scatter.11.cloned.1.call-start = ((), (), s32[]{:S(2)}) async-start(), calls=%async_computation.18 | async-start | bytes 5898240 | tf_op jit(solution)/shard_map/reduce_scatter | solution.py:630
  638.0 40.7 %collective-permute-start.28 = (bf16[4,160,896]{2,1,0:T(8,128)(2,1)S(1)}, bf16[4,160,896]{2,1,0:T(8,128)(2,1)}, u32[]{:S(2)}, u32[]{:S(2)}) collective-permute-start(bf16[4,160,896]{2,1,0:T(8,128)(2,1)S(1)} %fusion.7.refs_0_), channel_id=1, source_target_pairs={{8,0},{16,8},{24,16},{9,1},{17,9},{25,17},{10,2},{18,10},{26,18},{... | collective-permute-start | bytes 3440648 | tf_op jit(solution)/shard_map/ppermute | solution.py:502
  639.3 39.4 %collective-permute-start.27 = (bf16[4,160,896]{2,1,0:T(8,128)(2,1)S(1)}, bf16[4,160,896]{2,1,0:T(8,128)(2,1)}, u32[]{:S(2)}, u32[]{:S(2)}) collective-permute-start(bf16[4,160,896]{2,1,0:T(8,128)(2,1)S(1)} %fusion.7.refs_0_), channel_id=1, source_target_pairs={{0,8},{8,16},{16,24},{1,9},{9,17},{17,25},{2,10},{10,18},{18,26},{... | collective-permute-start | bytes 3440648 | tf_op jit(solution)/shard_map/ppermute | solution.py:501
  654.1 138.7 %collective-permute-start.20 = (bf16[4,224,2560]{2,1,0:T(8,128)(2,1)}, bf16[4,224,2560]{2,1,0:T(8,128)(2,1)}, u32[]{:S(2)}, u32[]{:S(2)}) collective-permute-start(bf16[4,224,2560]{2,1,0:T(8,128)(2,1)} %shard_map.210.refs_0_), channel_id=1, source_target_pairs={{0,4},{4,0},{1,5},{5,1},{2,6},{6,2},{3,7},{7,3},{8,12},{12,8},{9,1... | collective-permute-start | bytes 13762568 | tf_op jit(solution)/shard_map/ppermute | solution.py:62
  678.8 32.3 %collective-permute-start.29 = (bf16[4,160,896]{2,1,0:T(8,128)(2,1)}, bf16[4,160,896]{2,1,0:T(8,128)(2,1)}, u32[]{:S(2)}, u32[]{:S(2)}) collective-permute-start(bf16[4,160,896]{2,1,0:T(8,128)(2,1)} %get-tuple-element.163), channel_id=1, source_target_pairs={{0,8},{1,9},{2,10},{3,11},{4,12},{5,13},{6,14},{7,15}} | collective-permute-start | bytes 3440648 | tf_op jit(solution)/shard_map/ppermute | solution.py:487
  690.1 21.0 %collective-permute-start.36 = (bf16[4,160,896]{2,1,0:T(8,128)(2,1)}, bf16[4,160,896]{2,1,0:T(8,128)(2,1)}, u32[]{:S(2)}, u32[]{:S(2)}) collective-permute-start(bf16[4,160,896]{2,1,0:T(8,128)(2,1)} %get-tuple-element.166), channel_id=1, source_target_pairs={{24,16},{25,17},{26,18},{27,19},{28,20},{29,21},{30,22},{31,23}} | collective-permute-start | bytes 3440648 | tf_op jit(solution)/shard_map/ppermute | solution.py:488
  693.1 26.1 %collective-permute-start.31 = (bf16[4,160,896]{2,1,0:T(8,128)(2,1)}, bf16[4,160,896]{2,1,0:T(8,128)(2,1)}, u32[]{:S(2)}, u32[]{:S(2)}) collective-permute-start(bf16[4,160,896]{2,1,0:T(8,128)(2,1)} %collective-permute-done.28.refs_4_), channel_id=1, source_target_pairs={{8,0},{16,8},{9,1},{17,9},{10,2},{18,10},{11,3},{19,11},{12,4},{20... | collective-permute-start | bytes 3440648 | tf_op jit(solution)/shard_map/ppermute | solution.py:502
  694.3 24.8 %collective-permute-start.30 = (bf16[4,160,896]{2,1,0:T(8,128)(2,1)}, bf16[4,160,896]{2,1,0:T(8,128)(2,1)}, u32[]{:S(2)}, u32[]{:S(2)}) collective-permute-start(bf16[4,160,896]{2,1,0:T(8,128)(2,1)} %collective-permute-done.27.refs_1_), channel_id=1, source_target_pairs={{8,16},{16,24},{9,17},{17,25},{10,18},{18,26},{11,19},{19,27},{12,... | collective-permute-start | bytes 3440648 | tf_op jit(solution)/shard_map/ppermute | solution.py:501
  719.2 23.6 %collective-permute-start.32 = (bf16[4,160,896]{2,1,0:T(8,128)(2,1)}, bf16[4,160,896]{2,1,0:T(8,128)(2,1)}, u32[]{:S(2)}, u32[]{:S(2)}) collective-permute-start(bf16[4,160,896]{2,1,0:T(8,128)(2,1)} %get-tuple-element.164), channel_id=1, source_target_pairs={{0,8},{8,16},{1,9},{9,17},{2,10},{10,18},{3,11},{11,19},{4,12},{12... | collective-permute-start | bytes 3440648 | tf_op jit(solution)/shard_map/ppermute | solution.py:487
  723.0 19.8 %collective-permute-start.37 = (bf16[4,160,896]{2,1,0:T(8,128)(2,1)}, bf16[4,160,896]{2,1,0:T(8,128)(2,1)}, u32[]{:S(2)}, u32[]{:S(2)}) collective-permute-start(bf16[4,160,896]{2,1,0:T(8,128)(2,1)} %get-tuple-element.167), channel_id=1, source_target_pairs={{16,8},{24,16},{17,9},{25,17},{18,10},{26,18},{19,11},{27,19},{20,... | collective-permute-start | bytes 3440648 | tf_op jit(solution)/shard_map/ppermute | solution.py:488
  724.6 24.9 %collective-permute-start.34 = (bf16[4,160,896]{2,1,0:T(8,128)(2,1)}, bf16[4,160,896]{2,1,0:T(8,128)(2,1)}, u32[]{:S(2)}, u32[]{:S(2)}) collective-permute-start(bf16[4,160,896]{2,1,0:T(8,128)(2,1)} %collective-permute-done.31.refs_5_), channel_id=1, source_target_pairs={{8,0},{9,1},{10,2},{11,3},{12,4},{13,5},{14,6},{15,7}} | collective-permute-start | bytes 3440648 | tf_op jit(solution)/shard_map/ppermute | solution.py:502
  725.9 23.6 %collective-permute-start.33 = (bf16[4,160,896]{2,1,0:T(8,128)(2,1)}, bf16[4,160,896]{2,1,0:T(8,128)(2,1)}, u32[]{:S(2)}, u32[]{:S(2)}) collective-permute-start(bf16[4,160,896]{2,1,0:T(8,128)(2,1)} %collective-permute-done.30.refs_2_), channel_id=1, source_target_pairs={{16,24},{17,25},{18,26},{19,27},{20,28},{21,29},{22,30},{23,31}} | collective-permute-start | bytes 3440648 | tf_op jit(solution)/shard_map/ppermute | solution.py:501
  749.5 24.5 %collective-permute-start.35 = (bf16[4,160,896]{2,1,0:T(8,128)(2,1)S(1)}, bf16[4,160,896]{2,1,0:T(8,128)(2,1)S(1)}, u32[]{:S(2)}, u32[]{:S(2)}) collective-permute-start(bf16[4,160,896]{2,1,0:T(8,128)(2,1)S(1)} %get-tuple-element.165), channel_id=1, source_target_pairs={{0,8},{8,16},{16,24},{1,9},{9,17},{17,25},{2,10},{10,18},{18,26},{... | collective-permute-start | bytes 3440648 | tf_op jit(solution)/shard_map/ppermute | solution.py:487
  754.3 23.9 %collective-permute-start.38 = (bf16[4,160,896]{2,1,0:T(8,128)(2,1)S(1)}, bf16[4,160,896]{2,1,0:T(8,128)(2,1)S(1)}, u32[]{:S(2)}, u32[]{:S(2)}) collective-permute-start(bf16[4,160,896]{2,1,0:T(8,128)(2,1)S(1)} %get-tuple-element.168), channel_id=1, source_target_pairs={{8,0},{16,8},{24,16},{9,1},{17,9},{25,17},{10,2},{18,10},{26,18},{... | collective-permute-start | bytes 3440648 | tf_op jit(solution)/shard_map/ppermute | solution.py:488
  779.9 28.9 %collective-permute-start.40 = (bf16[4,160,896]{2,1,0:T(8,128)(2,1)S(1)}, bf16[4,160,896]{2,1,0:T(8,128)(2,1)S(1)}, u32[]{:S(2)}, u32[]{:S(2)}) collective-permute-start(bf16[4,160,896]{2,1,0:T(8,128)(2,1)S(1)} %fusion.11.refs_0_), channel_id=1, source_target_pairs={{8,0},{16,8},{24,16},{9,1},{17,9},{25,17},{10,2},{18,10},{26,18},{... | collective-permute-start | bytes 3440648 | tf_op jit(solution)/shard_map/ppermute | solution.py:502
  781.2 28.9 %collective-permute-start.39 = (bf16[4,160,896]{2,1,0:T(8,128)(2,1)S(1)}, bf16[4,160,896]{2,1,0:T(8,128)(2,1)}, u32[]{:S(2)}, u32[]{:S(2)}) collective-permute-start(bf16[4,160,896]{2,1,0:T(8,128)(2,1)S(1)} %fusion.11.refs_0_), channel_id=1, source_target_pairs={{0,8},{8,16},{16,24},{1,9},{9,17},{17,25},{2,10},{10,18},{18,26},{... | collective-permute-start | bytes 3440648 | tf_op jit(solution)/shard_map/ppermute | solution.py:501
  792.8 66.8 %collective-permute-start.45 = (bf16[4,4,160,896]{3,2,1,0:T(8,128)(2,1)}, bf16[4,4,160,896]{3,2,1,0:T(8,128)(2,1)}, u32[]{:S(2)}, u32[]{:S(2)}) collective-permute-start(bf16[4,4,160,896]{3,2,1,0:T(8,128)(2,1)} %shard_map.212.refs_0_), channel_id=1, source_target_pairs={{0,4},{4,0},{1,5},{5,1},{2,6},{6,2},{3,7},{7,3},{8,12},{12,8},{9,1... | collective-permute-start | bytes 13762568 | tf_op jit(solution)/shard_map/ppermute | solution.py:62
  808.8 29.6 %collective-permute-start.43 = (bf16[4,160,896]{2,1,0:T(8,128)(2,1)S(1)}, bf16[4,160,896]{2,1,0:T(8,128)(2,1)}, u32[]{:S(2)}, u32[]{:S(2)}) collective-permute-start(bf16[4,160,896]{2,1,0:T(8,128)(2,1)S(1)} %collective-permute-done.40.refs_4_), channel_id=1, source_target_pairs={{8,0},{16,8},{9,1},{17,9},{10,2},{18,10},{11,3},{19,11},{12,4},{20... | collective-permute-start | bytes 3440648 | tf_op jit(solution)/shard_map/ppermute | solution.py:502
  810.1 28.3 %collective-permute-start.42 = (bf16[4,160,896]{2,1,0:T(8,128)(2,1)}, bf16[4,160,896]{2,1,0:T(8,128)(2,1)}, u32[]{:S(2)}, u32[]{:S(2)}) collective-permute-start(bf16[4,160,896]{2,1,0:T(8,128)(2,1)} %collective-permute-done.39.refs_1_), channel_id=1, source_target_pairs={{8,16},{16,24},{9,17},{17,25},{10,18},{18,26},{11,19},{19,27},{12,... | collective-permute-start | bytes 3440648 | tf_op jit(solution)/shard_map/ppermute | solution.py:501
  819.2 27.0 %collective-permute-start.49 = (bf16[80,2560]{1,0:T(8,128)(2,1)S(1)}, bf16[80,2560]{1,0:T(8,128)(2,1)S(1)}, u32[]{:S(2)}, u32[]{:S(2)}) collective-permute-start(bf16[80,2560]{1,0:T(8,128)(2,1)S(1)} %get-tuple-element.172), channel_id=1, source_target_pairs={{24,16},{25,17},{26,18},{27,19},{28,20},{29,21},{30,22},{31,23}} | collective-permute-start | bytes 1228808 | tf_op jit(solution)/shard_map/ppermute | solution.py:488
  843.2 28.5 %collective-permute-start.47 = (bf16[4,160,896]{2,1,0:T(8,128)(2,1)}, bf16[4,160,896]{2,1,0:T(8,128)(2,1)}, u32[]{:S(2)}, u32[]{:S(2)}) collective-permute-start(bf16[4,160,896]{2,1,0:T(8,128)(2,1)} %collective-permute-done.43.refs_5_), channel_id=1, source_target_pairs={{8,0},{9,1},{10,2},{11,3},{12,4},{13,5},{14,6},{15,7}} | collective-permute-start | bytes 3440648 | tf_op jit(solution)/shard_map/ppermute | solution.py:502
  844.5 27.2 %collective-permute-start.46 = (bf16[4,160,896]{2,1,0:T(8,128)(2,1)}, bf16[4,160,896]{2,1,0:T(8,128)(2,1)}, u32[]{:S(2)}, u32[]{:S(2)}) collective-permute-start(bf16[4,160,896]{2,1,0:T(8,128)(2,1)} %collective-permute-done.42.refs_2_), channel_id=1, source_target_pairs={{16,24},{17,25},{18,26},{19,27},{20,28},{21,29},{22,30},{23,31}} | collective-permute-start | bytes 3440648 | tf_op jit(solution)/shard_map/ppermute | solution.py:501
  854.6 53.2 %all-to-all-start.4 = ((bf16[4,640,480]{1,2,0:T(8,128)(2,1)}), bf16[4,640,480]{1,2,0:T(8,128)(2,1)}, u32[]{:S(2)}, u32[]{:S(2)}) async-start(bf16[4,640,480]{1,2,0:T(8,128)(2,1)} %bitcast.247), calls=%async_computation.8 | async-start | bytes 4915200 | tf_op jit(solution)/shard_map/all_to_all | solution.py:724
  859.2 191.7 %reduce-scatter.9.cloned.1.call-start = ((), (), s32[]{:S(2)}) async-start(), calls=%async_computation.17 | async-start | bytes 5898240 | tf_op jit(solution)/shard_map/reduce_scatter | solution.py:630
  877.7 84.5 %collective-permute-start.58 = (bf16[4,4,160,896]{3,2,1,0:T(8,128)(2,1)}, bf16[4,4,160,896]{3,2,1,0:T(8,128)(2,1)}, u32[]{:S(2)}, u32[]{:S(2)}) collective-permute-start(bf16[4,4,160,896]{3,2,1,0:T(8,128)(2,1)} %shard_map.214.refs_0_), channel_id=1, source_target_pairs={{0,4},{4,0},{1,5},{5,1},{2,6},{6,2},{3,7},{7,3},{8,12},{12,8},{9,1... | collective-permute-start | bytes 13762568 | tf_op jit(solution)/shard_map/ppermute | solution.py:62
  877.7 18.6 %collective-permute-start.48 = (bf16[80,2560]{1,0:T(8,128)(2,1)}, bf16[80,2560]{1,0:T(8,128)(2,1)S(1)}, u32[]{:S(2)}, u32[]{:S(2)}) collective-permute-start(bf16[80,2560]{1,0:T(8,128)(2,1)} %get-tuple-element.171), channel_id=1, source_target_pairs={{0,8},{8,16},{16,24},{1,9},{9,17},{17,25},{2,10},{10,18},{18,26},{... | collective-permute-start | bytes 1228808 | tf_op jit(solution)/shard_map/ppermute | solution.py:487
  928.8 18.4 %collective-permute-start.59 = (bf16[80,2560]{1,0:T(8,128)(2,1)}, bf16[80,2560]{1,0:T(8,128)(2,1)S(1)}, u32[]{:S(2)}, u32[]{:S(2)}) collective-permute-start(bf16[80,2560]{1,0:T(8,128)(2,1)} %collective-permute-done.55.refs_2_), channel_id=1, source_target_pairs={{16,24},{17,25},{18,26},{19,27},{20,28},{21,29},{22,30},{23,31}} | collective-permute-start | bytes 1228808 | tf_op jit(solution)/shard_map/ppermute | solution.py:501
  940.6 19.9 %collective-permute-start.63 = (bf16[4,160,480]{2,1,0:T(8,128)(2,1)}, bf16[4,160,480]{2,1,0:T(8,128)(2,1)}, u32[]{:S(2)}, u32[]{:S(2)}) collective-permute-start(bf16[4,160,480]{2,1,0:T(8,128)(2,1)} %get-tuple-element.179), channel_id=1, source_target_pairs={{16,8},{24,16},{17,9},{25,17},{18,10},{26,18},{19,11},{27,19},{20,... | collective-permute-start | bytes 1843208 | tf_op jit(solution)/shard_map/ppermute | solution.py:488
  942.1 18.4 %collective-permute-start.57 = (bf16[4,160,480]{2,1,0:T(8,128)(2,1)}, bf16[4,160,480]{2,1,0:T(8,128)(2,1)}, u32[]{:S(2)}, u32[]{:S(2)}) collective-permute-start(bf16[4,160,480]{2,1,0:T(8,128)(2,1)} %get-tuple-element.176), channel_id=1, source_target_pairs={{0,8},{8,16},{1,9},{9,17},{2,10},{10,18},{3,11},{11,19},{4,12},{12... | collective-permute-start | bytes 1843208 | tf_op jit(solution)/shard_map/ppermute | solution.py:487
  951.5 25.8 %collective-permute-start.65 = (bf16[4,80,2560]{2,1,0:T(8,128)(2,1)}, bf16[4,80,2560]{2,1,0:T(8,128)(2,1)}, u32[]{:S(2)}, u32[]{:S(2)}) collective-permute-start(bf16[4,80,2560]{2,1,0:T(8,128)(2,1)} %shard_map.216.refs_0_), channel_id=1, source_target_pairs={{0,4},{4,0},{1,5},{5,1},{2,6},{6,2},{3,7},{7,3},{8,12},{12,8},{9,1... | collective-permute-start | bytes 4915208 | tf_op jit(solution)/shard_map/ppermute | solution.py:62
  972.2 18.0 %collective-permute-start.61 = (bf16[4,160,480]{2,1,0:T(8,128)(2,1)S(1)}, bf16[4,160,480]{2,1,0:T(8,128)(2,1)S(1)}, u32[]{:S(2)}, u32[]{:S(2)}) collective-permute-start(bf16[4,160,480]{2,1,0:T(8,128)(2,1)S(1)} %get-tuple-element.177), channel_id=1, source_target_pairs={{0,8},{8,16},{16,24},{1,9},{9,17},{17,25},{2,10},{10,18},{18,26},{... | collective-permute-start | bytes 1843208 | tf_op jit(solution)/shard_map/ppermute | solution.py:487
  976.0 18.4 %collective-permute-start.64 = (bf16[4,160,480]{2,1,0:T(8,128)(2,1)S(1)}, bf16[4,160,480]{2,1,0:T(8,128)(2,1)S(1)}, u32[]{:S(2)}, u32[]{:S(2)}) collective-permute-start(bf16[4,160,480]{2,1,0:T(8,128)(2,1)S(1)} %get-tuple-element.180), channel_id=1, source_target_pairs={{8,0},{16,8},{24,16},{9,1},{17,9},{25,17},{10,2},{18,10},{26,18},{... | collective-permute-start | bytes 1843208 | tf_op jit(solution)/shard_map/ppermute | solution.py:488
  994.7 17.8 %collective-permute-start.69 = (bf16[4,160,480]{2,1,0:T(8,128)(2,1)S(1)}, bf16[4,160,480]{2,1,0:T(8,128)(2,1)S(1)}, u32[]{:S(2)}, u32[]{:S(2)}) collective-permute-start(bf16[4,160,480]{2,1,0:T(8,128)(2,1)S(1)} %fusion.36.refs_0_), channel_id=1, source_target_pairs={{8,0},{16,8},{24,16},{9,1},{17,9},{25,17},{10,2},{18,10},{26,18},{... | collective-permute-start | bytes 1843208 | tf_op jit(solution)/shard_map/ppermute | solution.py:502
  (78 other events, 1509.6 us)
Sparse Core Ops, SparseCore 0:
  13.4 68.0 all-gather.4
  152.1 86.9 reduce-scatter.4
  242.8 41.0 all-gather.6
  285.8 41.1 all-gather.8
  382.2 55.8 reduce-scatter.6
  456.4 79.8 all-gather.10
  732.6 57.6 reduce-scatter.10
  896.4 57.3 reduce-scatter.8
